TPU v7x, 32 devices: a whole 2x2x4 slice. The times are simulated.
32 devices in a mesh: crop: 2 (over y), space: 16 (over z, x, core).
Axes of the slice: x: 2, y: 2, z: 4, core: 2. Of those that a mesh axis runs over, the one named last changes fastest.
Arguments:
- features: bfloat16 [128, 8, 8, 192], P(('crop', 'space')), parts along dimension 0, may hold values from -6 to 6
- cotangent: bfloat16 [128, 8, 8, 192], P(('crop', 'space')), parts along dimension 0, may hold values from -6 to 6
- kernel: float32 [7, 7, 7, 192], replicated, may hold values from -0.3125 to 0.3125
- b_dw: float32 [192], replicated, may hold values from -3 to 3
- ln_gain: float32 [192], replicated, may hold values from 0.5 to 1.5
- ln_bias: float32 [192], replicated, may hold values from -3 to 3
- w_in_t: bfloat16 [768, 192], P('space'), may hold values from -0.4375 to 0.4375
- b_in: bfloat16 [768], P('space'), may hold values from -3 to 3
- w_out: bfloat16 [768, 192], P('space'), may hold values from -0.21875 to 0.21875
- b_out: float32 [192], replicated, may hold values from -3 to 3
- gamma: float32 [192], replicated, may hold values from 0.5 to 1.5
Outputs:
- block_out: bfloat16 [128, 8, 8, 192], P(('crop', 'space')), parts along dimension 0
- d_x: bfloat16 [128, 8, 8, 192], P(('crop', 'space')), parts along dimension 0
- d_kernel: float32 [14, 7, 7, 192], P('crop'), parts along dimension 0
- d_b_dw: float32 [384], P('crop'), parts along dimension 0
- d_ln_gain: float32 [384], P('crop'), parts along dimension 0
- d_ln_bias: float32 [384], P('crop'), parts along dimension 0
- d_w_in: float32 [1536, 192], P(('crop', 'space')), parts along dimension 0
- d_b_in: float32 [1536], P(('crop', 'space')), parts along dimension 0
- d_w_out: float32 [1536, 192], P(('crop', 'space')), parts along dimension 0
- d_b_out: float32 [384], P('crop'), parts along dimension 0
- d_gamma: float32 [384], P('crop'), parts along dimension 0
There are 2 independent parts, one for each index of `crop`. A program takes and returns all parts, laid end to end along the dimension named above; an argument that names none is the same for every part. Nothing has to cross between parts.
All inputs are finite; a program needn't handle non-finite values.
Results may differ from a plain program's by a relative error of at most 0.0065.
Values may be sent and summed in bfloat16 or wider, within the bound.
No kernel may reach another device: no remote copies, remote signals or barrier semaphores. Data moves between devices by JAX's collectives and lax.ppermute only.
A program may use at most 64 MiB of HBM per device.

v0:
```python
import jax
import jax.numpy as jnp
from jax import lax
from jax.sharding import PartitionSpec as P

root_half = 0.7071067811865476
inv_root_tau = 0.3989422804014327


def padded_2(x, sides, width):
    for axis, dim in sides:
        size, length = (lax.axis_size(axis), x.shape[dim])
        up = [(i, (i + 1) % size) for i in range(size - 1)]
        down = [(j, i) for i, j in up]
        last = lax.slice_in_dim(x, length - width, length, axis=dim)
        initial = lax.slice_in_dim(x, 0, width, axis=dim)
        before = lax.ppermute(last, axis, up)
        after = lax.ppermute(initial, axis, down)
        x = jnp.concatenate([before, x, after], axis=dim)
    return x


def gelu_value(pre):
    return 0.5 * pre * (1.0 + lax.erf(pre * root_half))


def gelu_slope(pre):
    return 0.5 * (1.0 + lax.erf(pre * root_half)) + pre * jnp.exp(-0.5 * pre * pre) * inv_root_tau


def stencil(padded, kernel, size_x, size_y, size_z):
    width = kernel.shape[0]
    chans = padded.shape[3]

    def stencil_over_x(along_x, total):
        plane = lax.dynamic_slice_in_dim(padded, along_x, size_x, 0)
        taps_x = lax.dynamic_index_in_dim(kernel, along_x, 0, keepdims=False)

        def stencil_over_y(along_y, inner):
            strip = lax.dynamic_slice_in_dim(plane, along_y, size_y, 1)
            taps_y = lax.dynamic_index_in_dim(taps_x, along_y, 0, keepdims=False)
            for along_z in range(width):
                window = strip[:, :, along_z : along_z + size_z]
                inner = inner + window.astype(jnp.float32) * taps_y[along_z]
            return inner

        return lax.fori_loop(0, width, stencil_over_y, total)

    start = jnp.zeros((size_x, size_y, size_z, chans), jnp.float32)
    return lax.fori_loop(0, width, stencil_over_x, start)


def kernel_terms(padded, grad, width):
    size_x, size_y, size_z, chans = grad.shape
    grad_f = grad.astype(jnp.float32)

    def kernel_over_x(along_x):
        plane = lax.dynamic_slice_in_dim(padded, along_x, size_x, 0)

        def kernel_over_y(along_y):
            strip = lax.dynamic_slice_in_dim(plane, along_y, size_y, 1)
            terms = []
            for along_z in range(width):
                window = strip[:, :, along_z : along_z + size_z]
                terms.append(jnp.sum(window.astype(jnp.float32) * grad_f, axis=(0, 1, 2)))
            return jnp.stack(terms)

        return lax.map(kernel_over_y, jnp.arange(width, dtype=jnp.int32))

    return lax.map(kernel_over_x, jnp.arange(width, dtype=jnp.int32))


def side_pad(field, half):
    return jnp.pad(field, ((0, 0), (half, half), (half, half), (0, 0)))


def on_device(
    features, cotangent, kernel, b_dw, ln_gain, ln_bias, w_in_t, b_in, w_out, b_out, gamma
):
    size_x, size_y, size_z, chans = features.shape
    width = kernel.shape[0]
    half = width // 2
    scale = float(size_x * lax.axis_size("space") * size_y * size_z) ** (-0.5)
    rows = size_x * size_y * size_z
    with_rim = padded_2(features, (("space", 0),), half)
    padded = side_pad(with_rim, half)
    mixed = stencil(padded, kernel, size_x, size_y, size_z) + b_dw
    centred = mixed - jnp.mean(mixed, axis=-1, keepdims=True)
    inverse = lax.rsqrt(jnp.mean(centred * centred, axis=-1, keepdims=True) + 1e-06)
    unit_value = centred * inverse
    normed = (unit_value * ln_gain + ln_bias).astype(jnp.bfloat16)
    normed_rows = normed.reshape(rows, chans)
    w_in_all, b_in_all, w_out_all = (
        lax.all_gather(w_in_t, "space", axis=0, tiled=True),
        lax.all_gather(b_in, "space", axis=0, tiled=True),
        lax.all_gather(w_out, "space", axis=0, tiled=True),
    )
    pre = lax.dot_general(
        normed_rows, w_in_all, (((1,), (1,)), ((), ())), preferred_element_type=jnp.float32
    )
    pre = pre + b_in_all.astype(jnp.float32)
    hidden = gelu_value(pre).astype(jnp.bfloat16)
    branch = jnp.dot(hidden, w_out_all, preferred_element_type=jnp.float32) + b_out
    output = (features.reshape(rows, chans).astype(jnp.float32) + gamma * branch).astype(
        jnp.bfloat16
    )
    cot_f = cotangent.reshape(rows, chans).astype(jnp.float32)
    d_branch = gamma * cot_f
    d_branch_b = d_branch.astype(jnp.bfloat16)
    d_hidden = lax.dot_general(
        d_branch_b, w_out_all, (((1,), (1,)), ((), ())), preferred_element_type=jnp.float32
    )
    d_pre = d_hidden * gelu_slope(pre)
    d_pre_b = d_pre.astype(jnp.bfloat16)
    d_normed = jnp.dot(d_pre_b, w_in_all, preferred_element_type=jnp.float32)
    term_bi = jnp.sum(d_pre, axis=0) * scale
    term_wo = (
        lax.dot_general(
            hidden, d_branch_b, (((0,), (0,)), ((), ())), preferred_element_type=jnp.float32
        )
        * scale
    )
    term_wi = (
        lax.dot_general(
            d_pre_b, normed_rows, (((0,), (0,)), ((), ())), preferred_element_type=jnp.float32
        )
        * scale
    )
    d_w_in, d_b_in, d_w_out = (
        lax.psum_scatter(term_wi, "space", scatter_dimension=0, tiled=True),
        lax.psum_scatter(term_bi, "space", scatter_dimension=0, tiled=True),
        lax.psum_scatter(term_wo, "space", scatter_dimension=0, tiled=True),
    )
    d_normed = d_normed.reshape(size_x, size_y, size_z, chans)
    term_gain = jnp.sum(d_normed * unit_value, axis=(0, 1, 2)) * scale
    term_bias = jnp.sum(d_normed, axis=(0, 1, 2)) * scale
    scaled = d_normed * ln_gain
    d_mixed = inverse * (
        scaled
        - jnp.mean(scaled, axis=-1, keepdims=True)
        - unit_value * jnp.mean(scaled * unit_value, axis=-1, keepdims=True)
    )
    term_bdw = jnp.sum(d_mixed, axis=(0, 1, 2)) * scale
    d_mixed_b = d_mixed.astype(jnp.bfloat16)
    term_kernel = kernel_terms(padded, d_mixed_b, width) * scale
    term_bout = jnp.sum(d_branch, axis=0) * scale
    term_gamma = jnp.sum(cot_f * branch, axis=0) * scale
    grad_rim = padded_2(d_mixed_b, (("space", 0),), half)
    grad_pad = side_pad(grad_rim, half)
    back = stencil(grad_pad, kernel[::-1, ::-1, ::-1], size_x, size_y, size_z)
    d_x = (cotangent.astype(jnp.float32) + back).astype(jnp.bfloat16)
    bias_units = jnp.zeros((1,), jnp.float32)
    d_kernel, d_b_dw, d_ln_gain, d_ln_bias, d_b_out, d_gamma, bias_sum = lax.psum(
        (term_kernel, term_bdw, term_gain, term_bias, term_bout, term_gamma, bias_units), "space"
    )
    return (
        output.reshape(size_x, size_y, size_z, chans),
        d_x,
        d_kernel,
        d_b_dw,
        d_ln_gain,
        d_ln_bias,
        d_w_in,
        d_b_in,
        d_w_out,
        d_b_out,
        d_gamma,
    )


def solution(mesh):
    in_specs = (
        P(("crop", "space"), None, None, None),
        P(("crop", "space"), None, None, None),
        P(),
        P(),
        P(),
        P(),
        P("space", None),
        P("space"),
        P("space", None),
        P(),
        P(),
    )
    out_specs = (
        P(("crop", "space"), None, None, None),
        P(("crop", "space"), None, None, None),
        P("crop", None, None, None),
        P("crop"),
        P("crop"),
        P("crop"),
        P(("crop", "space"), None),
        P(("crop", "space")),
        P(("crop", "space"), None),
        P("crop"),
        P("crop"),
    )
    return jax.shard_map(
        on_device, mesh=mesh, in_specs=in_specs, out_specs=out_specs, check_vma=False
    )
```

profile of v0, /device:TPU:0, one launch (start us, length us, event | category | flops | bytes accessed | tf_op | source)
XLA Modules:
  0.0 516.6 jit_solution(11511662149112973641)
XLA Ops:
  7.3 1.0 fusion.17
  8.2 1.3 collective-permute-start.1
  9.6 3.0 collective-permute-start
  12.6 0.9 bitcast_convert_fusion
  13.6 1.0 copy.34
  14.6 0.8 copy.32
  16.9 34.5 %all-reduce.2 = bf16[768]{0:T(1024)(128)(2,1)S(1)} all-reduce(bf16[768]{0:T(1024)(128)(2,1)S(1)} %dynamic-update-slice), channel_id=1, replica_groups=mesh['crop'=2,'space'=16] {'space'}, use_global_device_ids=true, to_apply=%add.2 | all-reduce | flops 768 | bytes 3072
  51.3 18.2 %all_gather.9 = bf16[768,192]{1,0:T(8,128)(2,1)S(1)} all-gather(bf16[48,192]{1,0:T(8,128)(2,1)S(1)} %copy-done.5), channel_id=1, replica_groups=mesh['crop'=2,'space'=16] {'space'}, dimensions={0}, use_global_device_ids=true | all-gather | bytes 313344 | tf_op jit(solution)/shard_map/all_gather | solution.py:94
  69.6 1.7 rev.3
  72.0 20.4 %all_gather.11 = bf16[768,192]{1,0:T(8,128)(2,1)S(1)} all-gather(bf16[48,192]{1,0:T(8,128)(2,1)S(1)} %copy-done.6), channel_id=1, replica_groups=mesh['crop'=2,'space'=16] {'space'}, dimensions={0}, use_global_device_ids=true | all-gather | bytes 313344 | tf_op jit(solution)/shard_map/all_gather | solution.py:96
  92.8 28.8 %while.93 = (s32[]{:T(128)}, f32[4,8,8,192]{3,2,1,0:T(8,128)S(1)}, bf16[10,14,14,192]{3,2,1,0:T(8,128)(2,1)S(1)}, f32[7,7,7,192]{3,2,1,0:T(8,128)}, s32[]{:T(128...) while((s32[]{:T(128)}, f32[4,8,8,192]{3,2,1,0:T(8,128)S(1)}, ...), condition=%wide.region_3.4_spmd, body=%wide.region_0.3_spmd.sunk | while | flops 1032202 | bytes 1775354 | solution.py:50
  92.8 0.8 dynamic-slice_bitcast_fusion.4
  93.7 3.2 while.98
  97.0 0.8 dynamic-slice_bitcast_fusion.4
  97.8 3.2 while.98
  101.1 0.8 dynamic-slice_bitcast_fusion.4
  101.9 3.2 while.98
  105.2 0.8 dynamic-slice_bitcast_fusion.4
  106.0 3.2 while.98
  109.3 0.8 dynamic-slice_bitcast_fusion.4
  110.1 3.2 while.98
  113.4 0.8 dynamic-slice_bitcast_fusion.4
  114.3 3.2 while.98
  117.6 0.8 dynamic-slice_bitcast_fusion.4
  118.4 3.2 while.98
  123.6 1.2 convolution_multiply_fusion.1
  125.6 0.7 fusion.16
  126.3 1.3 collective-permute-start.3
  127.5 3.7 collective-permute-start.2
  131.2 166.9 %while.97 = (s32[]{:T(128)}, f32[7,7,7,192]{3,2,1,0:T(8,128)S(1)}, s32[7]{0:T(128)S(1)}, bf16[10,14,14,192]{3,2,1,0:T(8,128)(2,1)S(1)}, f32[4,8,8,192]{3,2,1,0:T...) while((s32[]{:T(128)}, f32[7,7,7,192]{3,2,1,0:T(8,128)S(1)}, ...), condition=%wide.region_22.23_spmd, body=%wide.region_12.22_spmd.sunk | while | flops 1030864 | bytes 1634706 | solution.py:70
  133.8 21.2 %while.100 = (s32[]{:T(128)}, f32[7,7,192]{2,1,0:T(8,128)S(1)}, s32[7]{0:T(128)S(1)}, bf16[4,14,14,192]{3,2,1,0:T(8,128)(2,1)S(1)}, f32[4,8,8,192]{3,2,1,0:T(8,1...) while((s32[]{:T(128)}, f32[7,7,192]{2,1,0:T(8,128)S(1)}, ...), condition=%wide.region_21.21_spmd, body=%wide.region_13.20_spmd.sunk | while | flops 1030859 | bytes 917539 | solution.py:68
  155.1 0.6 dynamic_slice.88
  157.6 21.2 %while.100 = (s32[]{:T(128)}, f32[7,7,192]{2,1,0:T(8,128)S(1)}, s32[7]{0:T(128)S(1)}, bf16[4,14,14,192]{3,2,1,0:T(8,128)(2,1)S(1)}, f32[4,8,8,192]{3,2,1,0:T(8,1...) while((s32[]{:T(128)}, f32[7,7,192]{2,1,0:T(8,128)S(1)}, ...), condition=%wide.region_21.21_spmd, body=%wide.region_13.20_spmd.sunk | while | flops 1030859 | bytes 917539 | solution.py:68
  181.5 21.2 %while.100 = (s32[]{:T(128)}, f32[7,7,192]{2,1,0:T(8,128)S(1)}, s32[7]{0:T(128)S(1)}, bf16[4,14,14,192]{3,2,1,0:T(8,128)(2,1)S(1)}, f32[4,8,8,192]{3,2,1,0:T(8,1...) while((s32[]{:T(128)}, f32[7,7,192]{2,1,0:T(8,128)S(1)}, ...), condition=%wide.region_21.21_spmd, body=%wide.region_13.20_spmd.sunk | while | flops 1030859 | bytes 917539 | solution.py:68
  205.3 21.2 %while.100 = (s32[]{:T(128)}, f32[7,7,192]{2,1,0:T(8,128)S(1)}, s32[7]{0:T(128)S(1)}, bf16[4,14,14,192]{3,2,1,0:T(8,128)(2,1)S(1)}, f32[4,8,8,192]{3,2,1,0:T(8,1...) while((s32[]{:T(128)}, f32[7,7,192]{2,1,0:T(8,128)S(1)}, ...), condition=%wide.region_21.21_spmd, body=%wide.region_13.20_spmd.sunk | while | flops 1030859 | bytes 917539 | solution.py:68
  229.2 21.2 %while.100 = (s32[]{:T(128)}, f32[7,7,192]{2,1,0:T(8,128)S(1)}, s32[7]{0:T(128)S(1)}, bf16[4,14,14,192]{3,2,1,0:T(8,128)(2,1)S(1)}, f32[4,8,8,192]{3,2,1,0:T(8,1...) while((s32[]{:T(128)}, f32[7,7,192]{2,1,0:T(8,128)S(1)}, ...), condition=%wide.region_21.21_spmd, body=%wide.region_13.20_spmd.sunk | while | flops 1030859 | bytes 917539 | solution.py:68
  253.0 21.2 %while.100 = (s32[]{:T(128)}, f32[7,7,192]{2,1,0:T(8,128)S(1)}, s32[7]{0:T(128)S(1)}, bf16[4,14,14,192]{3,2,1,0:T(8,128)(2,1)S(1)}, f32[4,8,8,192]{3,2,1,0:T(8,1...) while((s32[]{:T(128)}, f32[7,7,192]{2,1,0:T(8,128)S(1)}, ...), condition=%wide.region_21.21_spmd, body=%wide.region_13.20_spmd.sunk | while | flops 1030859 | bytes 917539 | solution.py:68
  276.9 21.2 %while.100 = (s32[]{:T(128)}, f32[7,7,192]{2,1,0:T(8,128)S(1)}, s32[7]{0:T(128)S(1)}, bf16[4,14,14,192]{3,2,1,0:T(8,128)(2,1)S(1)}, f32[4,8,8,192]{3,2,1,0:T(8,1...) while((s32[]{:T(128)}, f32[7,7,192]{2,1,0:T(8,128)S(1)}, ...), condition=%wide.region_21.21_spmd, body=%wide.region_13.20_spmd.sunk | while | flops 1030859 | bytes 917539 | solution.py:68
  298.1 0.8 broadcast_multiply_fusion
  299.0 0.7 reduce-scatter.3.cloned.1.call-update
  300.2 1.3 convolution_multiply_fusion
  301.5 0.8 copy.33
  302.3 1.3 select_maximum_fusion
  303.7 28.8 %while.95 = (s32[]{:T(128)}, f32[4,8,8,192]{3,2,1,0:T(8,128)S(1)}, bf16[10,14,14,192]{3,2,1,0:T(8,128)(2,1)S(1)}, f32[7,7,7,192]{3,2,1,0:T(8,128)}, s32[]{:T(128...) while((s32[]{:T(128)}, f32[4,8,8,192]{3,2,1,0:T(8,128)S(1)}, ...), condition=%wide.region_11.12_spmd, body=%wide.region_8.11_spmd.sunk | while | flops 1032202 | bytes 1775354 | solution.py:50
  303.7 0.8 dynamic-slice_bitcast_fusion.5
  304.5 3.2 while.99
  307.8 0.8 dynamic-slice_bitcast_fusion.5
  308.7 3.2 while.99
  311.9 0.8 dynamic-slice_bitcast_fusion.5
  312.8 3.2 while.99
  316.1 0.8 dynamic-slice_bitcast_fusion.5
  316.9 3.2 while.99
  320.2 0.8 dynamic-slice_bitcast_fusion.5
  321.0 3.2 while.99
  324.3 0.8 dynamic-slice_bitcast_fusion.5
  325.1 3.2 while.99
  328.4 0.8 dynamic-slice_bitcast_fusion.5
  329.3 3.2 while.99
  332.5 0.7 multiply_reduce_fusion.7
  333.2 32.1 %all-reduce.4 = (f32[192]{0:T(256)}, f32[192]{0:T(256)}, f32[192]{0:T(256)}, f32[768]{0:T(1024)S(1)}, f32[192]{0:T(256)}, /*index=5*/f32[192]{0:T(256)}) all-reduce(f32[192]{0:T(256)S(1)} %get-tuple-element.526, f32[192]{0:T(256)S(1)} %get-tuple-element.525, ...), channel_id=1, replica_groups=mesh['crop'=2,'space'=16] {'space'}, use_global_device_ids=true, to_apply=%region_25.26 | all-reduce | flops 1728 | bytes 13824 | tf_op jit(solution)/shard_map/psum | solution.py:153
  365.9 20.5 %all-reduce.7.cloned.1.call-done = f32[7,7,7,192]{3,2,1,0:T(8,128)} async-done(((f32[7,7,7,192]{3,2,1,0:T(8,128)}), f32[7,7,7,192]{3,2,1,0:T(8,128)}) %all-reduce.7.cloned.1.call-update) | async-done | bytes 263440 | tf_op jit(solution)/shard_map/psum | solution.py:153
  386.4 61.7 %reduce-scatter.3.cloned.1.call-done = f32[48,192]{1,0:T(8,128)} async-done(((f32[768,192]{1,0:T(8,128)}), f32[48,192]{1,0:T(8,128)}) %reduce-scatter.3.cloned.1.call-update) | async-done | bytes 36880 | tf_op jit(solution)/shard_map/reduce_scatter | solution.py:130
  448.1 60.2 %reduce-scatter.5.cloned.1.call-done = f32[48,192]{1,0:T(8,128)} async-done(((f32[768,192]{1,0:T(8,128)}), f32[48,192]{1,0:T(8,128)}) %reduce-scatter.5.cloned.1.call-update) | async-done | bytes 36880 | tf_op jit(solution)/shard_map/reduce_scatter | solution.py:132
  508.3 1.8 copy.83
  (504 shorter events, 104.9 us)
Async XLA Ops:
  7.2 8.2 %copy-start.9 = (u32[32]{0:T(128)S(1)}, u32[32]{0:T(128)}, u32[]{:S(2)}) copy-start(u32[32]{0:T(128)} %constant.179) | copy-start | bytes 388
  7.2 9.4 %copy-start.12 = (bf16[48]{0:T(256)(128)(2,1)S(1)}, bf16[48]{0:T(256)(128)(2,1)}, u32[]{:S(2)}) copy-start(bf16[48]{0:T(256)(128)(2,1)} %param.30) | copy-start | bytes 292
  7.2 44.1 %copy-start.5 = (bf16[48,192]{1,0:T(8,128)(2,1)S(1)}, bf16[48,192]{1,0:T(8,128)(2,1)}, u32[]{:S(2)}) copy-start(bf16[48,192]{1,0:T(8,128)(2,1)} %param.29) | copy-start | bytes 55300
  7.2 379.2 %all-reduce.7.cloned.1.call-start = ((), (), s32[]{:S(2)}) async-start(), calls=%async_computation.2 | async-start | bytes 802816 | tf_op jit(solution)/shard_map/psum | solution.py:153
  8.2 84.1 %collective-permute-start.1 = (bf16[3,8,8,192]{3,2,1,0:T(8,128)(2,1)S(1)}, bf16[3,8,8,192]{3,2,1,0:T(8,128)(2,1)S(1)}, u32[]{:S(2)}, u32[]{:S(2)}) collective-permute-start(bf16[3,8,8,192]{3,2,1,0:T(8,128)(2,1)S(1)} %get-tuple-element.517), channel_id=1, source_target_pairs={{1,0},{2,1},{3,2},{4,3},{5,4},{6,5},{7,6},{8,7},{9,8},{10,9},{11,1... | collective-permute-start | bytes 221192 | tf_op jit(solution)/shard_map/ppermute | solution.py:18
  9.5 62.4 %copy-start.6 = (bf16[48,192]{1,0:T(8,128)(2,1)S(1)}, bf16[48,192]{1,0:T(8,128)(2,1)}, u32[]{:S(2)}) copy-start(bf16[48,192]{1,0:T(8,128)(2,1)} %param.31) | copy-start | bytes 55300
  9.6 82.8 %collective-permute-start = (bf16[3,8,8,192]{3,2,1,0:T(8,128)(2,1)S(1)}, bf16[3,8,8,192]{3,2,1,0:T(8,128)(2,1)S(1)}, u32[]{:S(2)}, u32[]{:S(2)}) collective-permute-start(bf16[3,8,8,192]{3,2,1,0:T(8,128)(2,1)S(1)} %get-tuple-element.516), channel_id=1, source_target_pairs={{0,1},{1,2},{2,3},{3,4},{4,5},{5,6},{6,7},{7,8},{8,9},{9,10},{10,1... | collective-permute-start | bytes 221192 | tf_op jit(solution)/shard_map/ppermute | solution.py:17
  14.6 77.8 %copy-start = (bf16[4,8,8,192]{3,2,1,0:T(8,128)(2,1)S(1)}, bf16[4,8,8,192]{3,2,1,0:T(8,128)(2,1)}, u32[]{:S(2)}) copy-start(bf16[4,8,8,192]{3,2,1,0:T(8,128)(2,1)} %param.23) | copy-start | bytes 294916
  92.7 28.9 %copy-start.4 = (f32[192]{0:T(256)S(1)}, f32[192]{0:T(256)}, u32[]{:S(2)}) copy-start(f32[192]{0:T(256)} %param.26) | copy-start | bytes 2308
  92.8 29.3 %copy-start.7 = (f32[192]{0:T(256)S(1)}, f32[192]{0:T(256)}, u32[]{:S(2)}) copy-start(f32[192]{0:T(256)} %param.27) | copy-start | bytes 2308
  92.8 29.3 %copy-start.10 = (f32[192]{0:T(256)S(1)}, f32[192]{0:T(256)}, u32[]{:S(2)}) copy-start(f32[192]{0:T(256)} %param.28) | copy-start | bytes 2308
  122.0 0.7 copy-start.8
  125.0 6.2 %copy-start.3 = (f32[7,7,7,192]{3,2,1,0:T(8,128)S(1)}, f32[7,7,7,192]{3,2,1,0:T(8,128)}, u32[]{:S(2)}) copy-start(f32[7,7,7,192]{3,2,1,0:T(8,128)} %custom-call.1) | copy-start | bytes 790276
  126.3 176.1 %collective-permute-start.3 = (bf16[3,8,8,192]{3,2,1,0:T(8,128)(2,1)}, bf16[3,8,8,192]{3,2,1,0:T(8,128)(2,1)}, u32[]{:S(2)}, u32[]{:S(2)}) collective-permute-start(bf16[3,8,8,192]{3,2,1,0:T(8,128)(2,1)} %get-tuple-element.515), channel_id=1, source_target_pairs={{1,0},{2,1},{3,2},{4,3},{5,4},{6,5},{7,6},{8,7},{9,8},{10,9},{11,1... | collective-permute-start | bytes 221192 | tf_op jit(solution)/shard_map/ppermute | solution.py:18
  127.5 174.8 %collective-permute-start.2 = (bf16[3,8,8,192]{3,2,1,0:T(8,128)(2,1)}, bf16[3,8,8,192]{3,2,1,0:T(8,128)(2,1)}, u32[]{:S(2)}, u32[]{:S(2)}) collective-permute-start(bf16[3,8,8,192]{3,2,1,0:T(8,128)(2,1)} %get-tuple-element.514), channel_id=1, source_target_pairs={{0,1},{1,2},{2,3},{3,4},{4,5},{5,6},{6,7},{7,8},{8,9},{9,10},{10,1... | collective-permute-start | bytes 221192 | tf_op jit(solution)/shard_map/ppermute | solution.py:17
  298.1 1.7 copy-start.1
  298.1 1.7 copy-start.11
  299.0 149.2 %reduce-scatter.3.cloned.1.call-start = ((), (), s32[]{:S(2)}) async-start(), calls=%async_computation.3 | async-start | bytes 835584 | tf_op jit(solution)/shard_map/reduce_scatter | solution.py:130
  299.7 208.6 %reduce-scatter.5.cloned.1.call-start = ((), (), s32[]{:S(2)}) async-start(), calls=%async_computation.4 | async-start | bytes 835584 | tf_op jit(solution)/shard_map/reduce_scatter | solution.py:132
  303.6 28.9 %copy-start.2 = (bf16[4,8,8,192]{3,2,1,0:T(8,128)(2,1)S(1)}, bf16[4,8,8,192]{3,2,1,0:T(8,128)(2,1)}, u32[]{:S(2)}) copy-start(bf16[4,8,8,192]{3,2,1,0:T(8,128)(2,1)} %param.24) | copy-start | bytes 294916
Sparse Core Ops, SparseCore 0:
  299.1 87.2 all-reduce.6
  390.5 57.5 reduce-scatter.2
  452.7 55.5 reduce-scatter.4
where the time goes:
time: 519 us; the launch traced here: 517 us
  waiting for transfers between devices  143 us (28%)
  loops' own time  113 us (22%)
  blocking collectives  105 us (20%)
  other arithmetic  67.9 us (13%)
  local copies, waits for them, and re-layouts  58.7 us (11%)
  between operations  15.5 us (3%)
  starting transfers between devices  9.39 us (2%)
    another operation x7, loops' own time, kernel_over_x(): return lax.map(kernel_over_y, jnp.arange(width, dtype=jnp.int32))  96.4 us
    reduce_scatter x1, waiting for transfers between devices, on_device(): lax.psum_scatter(term_wi, 'space', scatter_dimension=0, tiled=True)  61.7 us
    reduce_scatter x1, waiting for transfers between devices, on_device(): lax.psum_scatter(term_wo, 'space', scatter_dimension=0, tiled=True)  60.2 us
    add x98, other arithmetic, stencil_over_y(): inner = inner + window.astype(jnp.float32) * taps_y[along_z]  41.2 us
    unnamed x1, blocking collectives  34.5 us
    dynamic_slice x56, local copies, waits for them, and re-layouts, kernel_terms(): return lax.map(kernel_over_x, jnp.arange(width, dtype=jnp.int32))  32.8 us
    psum x1, blocking collectives, on_device(): lax.psum((term_kernel, term_bdw, term_gain, term_bias, term_bout, term_ga...  32.1 us
    reduce_sum x49, other arithmetic, kernel_over_y(): terms.append(jnp.sum(window.astype(jnp.float32) * grad_f, axis=(0, 1, 2)))  21.6 us
  transfers between devices with their start and end apart: 7, of which 3 were waited for; matrix products, arithmetic and copies ran while one was open for 18% of the time, Pallas kernels for 0%

commit v1 on v0

v1 whole, which is shorter than its diff:
```python
import jax
import jax.numpy as jnp
from jax import lax
from jax.experimental import pallas as pl
from jax.experimental.pallas import tpu as pltpu
from jax.sharding import PartitionSpec as P

root_half = 0.7071067811865476
inv_root_tau = 0.3989422804014327
F32 = jnp.float32
BF16 = jnp.bfloat16
LANE = 128
VMEM = pl.BlockSpec(memory_space=pltpu.VMEM)
SMEM = pl.BlockSpec(memory_space=pltpu.SMEM)


def swap(x, bit):
    size = lax.axis_size("space")
    return lax.ppermute(x, "space", [(i, i ^ bit) for i in range(size)])


def swap_odd(x):
    size = lax.axis_size("space")
    pairs = [(i, i + 1) for i in range(1, size - 1, 2)]
    return lax.ppermute(x, "space", pairs + [(j, i) for i, j in pairs])


def shifted(v, by):
    if by == 0:
        return v
    row = lax.broadcasted_iota(jnp.int32, v.shape, 0)
    keep = (row < 8 - by) if by > 0 else (row >= -by)
    return jnp.where(keep, pltpu.roll(v, (-by) % 8, axis=0), 0.0)


def fill_planes(odd, x_ref, p_ref, q_ref, z_ref):
    for plane in range(10):
        if plane < 3:
            v = jnp.where(odd, p_ref[plane + 1].astype(F32), q_ref[plane + 1].astype(F32))
        elif plane < 7:
            v = x_ref[plane - 3].astype(F32)
        else:
            v = jnp.where(odd, q_ref[plane - 7].astype(F32), p_ref[plane - 7].astype(F32))
        z_ref[plane] = v[:, :, :LANE]
        rest = v[:, :, LANE:]
        if plane < 8:
            z_ref[10 + plane, :, :, 0:64] = rest
        if plane >= 2:
            z_ref[8 + plane, :, :, 64:128] = rest


def fill_taps(k_ref, t_ref):
    for a in range(7):
        for b in range(7):
            v = k_ref[a, b]
            t_ref[0, a, b, 0:7] = v[:, :LANE]
            t_ref[1, a, b, 0:7, 0:64] = v[:, LANE:]
            t_ref[1, a, b, 0:7, 64:128] = v[:, LANE:]


def stencil(z_ref, t_ref, u_ref, flip):
    def unit(u, carry):
        base = jnp.where(u < 4, u, u + 6)
        group = jnp.where(u < 4, 0, 1)
        total = [None] * 8
        for e in range(7):
            acc = [None] * 8
            for a in range(7):
                taps = []
                for b in range(7):
                    fa, fb, fe = (6 - a, 6 - b, 6 - e) if flip else (a, b, e)
                    taps.append(jnp.broadcast_to(t_ref[group, fa, fb, fe : fe + 1], (8, LANE)))
                for source in range(8):
                    x = z_ref[base + a, source]
                    for b in range(7):
                        j = source - b + 3
                        if 0 <= j < 8:
                            term = x * taps[b]
                            acc[j] = term if acc[j] is None else acc[j] + term
            for j in range(8):
                part = shifted(acc[j], e - 3)
                total[j] = part if total[j] is None else total[j] + part
        for j in range(8):
            u_ref[u, j] = total[j]
        return carry

    lax.fori_loop(0, 6, unit, 0)


def forward_kernel(odd_ref, x_ref, p_ref, q_ref, k_ref, vec_ref, na_ref, unit_ref, z_ref, t_ref, u_ref, m_ref):
    fill_planes(odd_ref[0] == 1, x_ref, p_ref, q_ref, z_ref)
    fill_taps(k_ref, t_ref)
    stencil(z_ref, t_ref, u_ref, False)
    for i in range(4):
        m_ref[64 * i : 64 * i + 64, 0:LANE] = u_ref[i].reshape(64, LANE)
    for i in range(2):
        v = u_ref[4 + i].reshape(64, LANE)
        m_ref[64 * i : 64 * i + 64, LANE : LANE + 64] = v[:, 0:64]
        m_ref[64 * i + 128 : 64 * i + 192, LANE : LANE + 64] = v[:, 64:128]
    chans = k_ref.shape[3]
    mixed = m_ref[...] + vec_ref[0:1]
    centred = mixed - jnp.mean(mixed, axis=-1, keepdims=True)
    inverse = lax.rsqrt(jnp.mean(centred * centred, axis=-1, keepdims=True) + 1e-06)
    unit = centred * inverse
    normed = unit * vec_ref[1:2] + vec_ref[2:3]
    rows = unit.shape[0]
    na_ref[:, 0:chans] = normed.astype(BF16)
    one = (lax.broadcasted_iota(jnp.int32, (rows, 256 - chans), 1) == 0).astype(F32)
    na_ref[:, chans:256] = one.astype(BF16)
    unit_ref[:, 0:chans] = unit
    unit_ref[:, chans:256] = jnp.broadcast_to(inverse, (rows, 256 - chans))


def pointwise_kernel(g0_ref, g1_ref, na_ref, unit_ref, x_ref, c_ref, vec_ref, out_ref, dm_ref, w0_ref, w1_ref, small_ref):
    rows, chans = na_ref.shape[0], x_ref.shape[3]
    normed = na_ref[...]
    cot = c_ref[...].astype(F32).reshape(rows, chans)
    gamma = vec_ref[4:5]
    d_branch = cot * gamma
    d_b = jnp.concatenate([d_branch, jnp.zeros((rows, 256 - chans), F32)], axis=1).astype(BF16)
    branch = jnp.zeros((rows, 256), F32)
    d_normed = jnp.zeros((rows, 256), F32)
    over_c = (((1,), (1,)), ((), ()))
    over_rows = (((0,), (0,)), ((), ()))
    for g_ref, w_ref in ((g0_ref, w0_ref), (g1_ref, w1_ref)):
        step = 128
        for first in range(0, g_ref.shape[0], step):
            here = slice(first, first + step)
            w_in = g_ref[here, 0:256]
            w_out = g_ref[here, 256:512]
            pre = lax.dot_general(normed, w_in, over_c, preferred_element_type=F32)
            d_hidden = lax.dot_general(d_b, w_out, over_c, preferred_element_type=F32)
            cdf = 0.5 * (1.0 + lax.erf(pre * root_half))
            hidden = (pre * cdf).astype(BF16)
            slope = cdf + pre * jnp.exp(-0.5 * pre * pre) * inv_root_tau
            d_pre = (d_hidden * slope).astype(BF16)
            branch = branch + jnp.dot(hidden, w_out, preferred_element_type=F32)
            d_normed = d_normed + jnp.dot(d_pre, w_in, preferred_element_type=F32)
            w_ref[here, 0:256] = lax.dot_general(d_pre, normed, over_rows, preferred_element_type=F32).astype(BF16)
            w_ref[here, 256:512] = lax.dot_general(hidden, d_b, over_rows, preferred_element_type=F32).astype(BF16)
    branch = branch[:, 0:chans] + vec_ref[3:4]
    x = x_ref[...].astype(F32).reshape(rows, chans)
    out_ref[...] = (x + gamma * branch).reshape(out_ref.shape).astype(BF16)
    d_normed = d_normed[:, 0:chans]
    unit = unit_ref[:, 0:chans]
    inverse = unit_ref[:, chans : chans + 1]
    scaled = d_normed * vec_ref[1:2]
    d_mixed = inverse * (
        scaled
        - jnp.mean(scaled, axis=-1, keepdims=True)
        - unit * jnp.mean(scaled * unit, axis=-1, keepdims=True)
    )
    dm_ref[...] = d_mixed.reshape(dm_ref.shape).astype(BF16)
    small_ref[...] = jnp.zeros(small_ref.shape, F32)
    sums = (d_mixed, d_normed * unit, d_normed, d_branch, cot * branch)
    for i, term in enumerate(sums):
        small_ref[i : i + 1, 0:chans] = jnp.sum(term, axis=0, keepdims=True)


def rows_to_one(v):
    row = lax.broadcasted_iota(jnp.int32, (8, LANE), 0)
    v = list(v) + [jnp.zeros((8, LANE), F32)]
    for half in (4, 2, 1):
        low = (row & half) == 0
        v = [
            jnp.where(low, v[i], v[i + half])
            + jnp.where(
                low,
                pltpu.roll(v[i], 8 - half, axis=0),
                pltpu.roll(v[i + half], half, axis=0),
            )
            for i in range(half)
        ]
    return v[0]


HALF = 320


def grad_kernel(odd_ref, x_ref, p_ref, q_ref, g_ref, small_ref, keep_ref, send_ref, z_ref, s_ref, wa_ref, wb_ref, w_ref):
    odd = odd_ref[0]
    fill_planes(odd == 1, x_ref, p_ref, q_ref, z_ref)
    for i in range(4):
        v = g_ref[i].astype(F32)
        s_ref[3, i] = v[:, :, :LANE]
        s_ref[3, 4 + i % 2, :, :, 64 * (i // 2) : 64 * (i // 2) + 64] = v[:, :, LANE:]

    def shift_unit(u, carry):
        for j in range(8):
            v = s_ref[3, u, j]
            for e in range(7):
                if e != 3:
                    s_ref[e, u, j] = shifted(v, 3 - e)
        return carry

    lax.fori_loop(0, 6, shift_unit, 0)

    def over_a(a, carry):
        for e in range(7):
            for units, into in (((0, 1, 2, 3), wa_ref), ((4, 5), wb_ref)):
                acc = [None] * 7
                for u in units:
                    base = u if u < 4 else u + 6
                    grads = [s_ref[e, u, j] for j in range(8)]
                    for source in range(8):
                        x = z_ref[base + a, source]
                        for b in range(7):
                            j = source - b + 3
                            if 0 <= j < 8:
                                term = x * grads[j]
                                acc[b] = term if acc[b] is None else acc[b] + term
                one = rows_to_one(acc)
                if len(units) == 2:
                    one = one + pltpu.roll(one, 64, axis=1)
                into[pl.ds(a * 64 + e, 8, stride=8), :] = one
        return carry

    for b in range(49):
        at = 64 * (b // 7) + 8 * (b % 7)
        wa_ref[at : at + 8] = jnp.zeros((8, LANE), F32)
        wb_ref[at : at + 8] = jnp.zeros((8, LANE), F32)
    lax.fori_loop(0, 7, over_a, 0)

    low = lax.broadcasted_iota(jnp.int32, (56, LANE), 1) < 64
    for a in range(5):
        w_ref[0, 56 * a : 56 * a + 56] = wa_ref[64 * a : 64 * a + 56]
    w_ref[0, 280:288] = small_ref[:, 0:LANE]
    w_ref[0, 288:HALF] = jnp.zeros((HALF - 288, LANE), F32)
    for a in range(5, 7):
        w_ref[1, 56 * (a - 5) : 56 * (a - 5) + 56] = wa_ref[64 * a : 64 * a + 56]
    for a in range(3):
        w_ref[1, 112 + 56 * a : 168 + 56 * a] = jnp.where(
            low, wb_ref[64 * a : 64 * a + 56], wb_ref[64 * (a + 4) : 64 * (a + 4) + 56]
        )
    w_ref[1, 280:312] = jnp.where(low[0:32], wb_ref[192:224], wb_ref[224:256])
    w_ref[1, 312:320] = small_ref[:, LANE:256]
    keep_ref[...] = w_ref[odd].astype(BF16)
    send_ref[...] = w_ref[1 - odd].astype(BF16)


def unpack_kernel(scale, odd_ref, mine_ref, other_ref, dk_ref, small_ref, w_ref):
    odd = odd_ref[0]
    w_ref[odd] = mine_ref[...].astype(F32) * scale
    w_ref[1 - odd] = other_ref[...].astype(F32) * scale
    for a in range(7):
        for b in range(7):
            row = 56 * a + 8 * b if a < 5 else 56 * (a - 5) + 8 * b
            main = w_ref[0 if a < 5 else 1, row : row + 7]
            if a == 3:
                at, lane = 280 + 8 * (b % 4), 64 * (b // 4)
            else:
                at, lane = 112 + 56 * (a % 4) + 8 * b, 64 * (a // 4)
            rest = w_ref[1, at : at + 7]
            dk_ref[a, b, :, 0:LANE] = main
            dk_ref[a, b, :, LANE : LANE + 64] = rest[:, lane : lane + 64]
    small_ref[:, 0:LANE] = w_ref[0, 280:288]
    small_ref[:, LANE:256] = w_ref[1, 312:320]


def back_kernel(odd_ref, g_ref, p_ref, q_ref, k_ref, c_ref, dx_ref, z_ref, t_ref, u_ref):
    fill_planes(odd_ref[0] == 1, g_ref, p_ref, q_ref, z_ref)
    fill_taps(k_ref, t_ref)
    stencil(z_ref, t_ref, u_ref, True)
    for i in range(4):
        cot = c_ref[i].astype(F32)
        dx_ref[i, :, :, 0:LANE] = (cot[:, :, 0:LANE] + u_ref[i]).astype(BF16)
        v = u_ref[4 + i % 2]
        rest = v[:, :, 64 * (i // 2) : 64 * (i // 2) + 64]
        dx_ref[i, :, :, LANE : LANE + 64] = (cot[:, :, LANE:] + rest).astype(BF16)


def params(mib):
    return pltpu.CompilerParams(vmem_limit_bytes=mib * 1024 * 1024)


def struct(shape, dtype):
    return jax.ShapeDtypeStruct(shape, dtype)


def on_device(
    features, cotangent, kernel, b_dw, ln_gain, ln_bias, w_in_t, b_in, w_out, b_out, gamma
):
    size_x, size_y, size_z, chans = features.shape
    devices = lax.axis_size("space")
    scale = float(size_x * devices * size_y * size_z) ** (-0.5)
    rows = size_x * size_y * size_z
    units = w_in_t.shape[0]
    bits = [1 << i for i in range(devices.bit_length() - 1)]
    odd = lax.rem(lax.axis_index("space"), 2).astype(jnp.int32).reshape(1)
    vecs = jnp.stack([b_dw, ln_gain, ln_bias, b_out, gamma, gamma, gamma, gamma])

    weights = jnp.concatenate(
        [
            w_in_t,
            b_in[:, None],
            jnp.zeros((units, 255 - chans), BF16),
            w_out,
            jnp.zeros((units, 256 - chans), BF16),
        ],
        axis=1,
    )
    for bit in bits[:0:-1]:
        weights = jnp.concatenate([weights, swap(weights, bit)], axis=0)
    weights_other = swap(weights, 1)
    x_core, x_far = swap(features, 1), swap_odd(features)

    z_scratch = pltpu.VMEM((18, size_y, size_z, LANE), F32)
    t_scratch = pltpu.VMEM((2, 7, 7, 8, LANE), F32)
    u_scratch = pltpu.VMEM((6, size_y, size_z, LANE), F32)
    normed, unit = pl.pallas_call(
        forward_kernel,
        out_shape=(struct((rows, 256), BF16), struct((rows, 256), F32)),
        in_specs=[SMEM] + [VMEM] * 5,
        out_specs=(VMEM, VMEM),
        scratch_shapes=[z_scratch, t_scratch, u_scratch, pltpu.VMEM((rows, chans), F32)],
        compiler_params=params(12),
        name="forward_stencil",
    )(odd, features, x_core, x_far, kernel, vecs)

    half = weights.shape[0]
    output, d_mixed, grad_keep, grad_send, small = pl.pallas_call(
        pointwise_kernel,
        out_shape=(
            struct(features.shape, BF16),
            struct(features.shape, BF16),
            struct((half, 512), BF16),
            struct((half, 512), BF16),
            struct((8, 256), F32),
        ),
        in_specs=[VMEM] * 7,
        out_specs=(VMEM,) * 5,
        compiler_params=params(16),
        name="pointwise",
    )(weights, weights_other, normed, unit, features, cotangent, vecs)

    g_core, g_far = swap(d_mixed, 1), swap_odd(d_mixed)

    total = grad_keep.astype(F32) + swap(grad_send, 1).astype(F32)
    for bit in bits[1:]:
        n = total.shape[0] // 2
        sent = total[n:].astype(BF16)
        total = total[:n] + swap(sent, bit).astype(F32)
    total = total * scale
    d_w_in, d_b_in, d_w_out = (
        total[:, 0:chans],
        total[:, chans],
        total[:, 256 : 256 + chans],
    )

    keep, send = pl.pallas_call(
        grad_kernel,
        out_shape=(struct((HALF, LANE), BF16), struct((HALF, LANE), BF16)),
        in_specs=[SMEM] + [VMEM] * 5,
        out_specs=(VMEM, VMEM),
        scratch_shapes=[
            z_scratch,
            pltpu.VMEM((7, 6, size_y, size_z, LANE), F32),
            pltpu.VMEM((448, LANE), F32),
            pltpu.VMEM((448, LANE), F32),
            pltpu.VMEM((2, HALF, LANE), F32),
        ],
        compiler_params=params(12),
        name="kernel_gradient",
    )(odd, features, x_core, x_far, d_mixed, small)
    mine = keep.astype(F32) + swap(send, 1).astype(F32)
    for bit in bits[1:]:
        sent = mine.astype(BF16)
        mine = sent.astype(F32) + swap(sent, bit).astype(F32)
    mine = mine.astype(BF16)
    other = swap(mine, 1)

    d_x = pl.pallas_call(
        back_kernel,
        out_shape=struct(features.shape, BF16),
        in_specs=[SMEM] + [VMEM] * 5,
        out_specs=VMEM,
        scratch_shapes=[z_scratch, t_scratch, u_scratch],
        compiler_params=params(12),
        name="backward_stencil",
    )(odd, d_mixed, g_core, g_far, kernel, cotangent)

    d_kernel, sums = pl.pallas_call(
        lambda *refs: unpack_kernel(scale, *refs),
        out_shape=(struct(kernel.shape, F32), struct((8, 256), F32)),
        in_specs=[SMEM] + [VMEM] * 2,
        out_specs=(VMEM, VMEM),
        scratch_shapes=[pltpu.VMEM((2, HALF, LANE), F32)],
        compiler_params=params(4),
        name="unpack",
    )(odd, mine, other)
    return (
        output,
        d_x,
        d_kernel,
        sums[0, :chans],
        sums[1, :chans],
        sums[2, :chans],
        d_w_in,
        d_b_in,
        d_w_out,
        sums[3, :chans],
        sums[4, :chans],
    )


def solution(mesh):
    in_specs = (
        P(("crop", "space"), None, None, None),
        P(("crop", "space"), None, None, None),
        P(),
        P(),
        P(),
        P(),
        P("space", None),
        P("space"),
        P("space", None),
        P(),
        P(),
    )
    out_specs = (
        P(("crop", "space"), None, None, None),
        P(("crop", "space"), None, None, None),
        P("crop", None, None, None),
        P("crop"),
        P("crop"),
        P("crop"),
        P(("crop", "space"), None),
        P(("crop", "space")),
        P(("crop", "space"), None),
        P("crop"),
        P("crop"),
    )
    return jax.shard_map(
        on_device, mesh=mesh, in_specs=in_specs, out_specs=out_specs, check_vma=False
    )
```

time: 519 us -> 67.7 us (0.13)
  waiting for transfers between devices: 143 us -> 15.3 us
  loops' own time: 113 us -> 0 us
  blocking collectives: 105 us -> 0 us
  other arithmetic: 67.9 us -> 0.34 us
  local copies, waits for them, and re-layouts: 58.7 us -> 4.32 us
  starting transfers between devices: 9.39 us -> 29.7 us
  Pallas kernels: 0 us -> 16.9 us
  between operations: 15.5 us -> 0.88 us
    reduce_scatter x2 -> x0, waiting for transfers between devices: 122 us -> none  [the longest x1 61.7 us: on_device(): lax.psum_scatter(term_wi, 'space', scatter_dimension=0, tiled=True)]
    another operation x24 -> x0, loops' own time: 113 us -> none  [the longest x7 96.4 us: kernel_over_x(): return lax.map(kernel_over_y, jnp.arange(width, dtype=jnp.int32))]
    add x98 -> x3, other arithmetic: 41.2 us -> 0.18 us  [the longest x1 0.11 us: on_device(): total = grad_keep.astype(F32) + swap(grad_send, 1).astype(F32)]
    all_gather x2 -> x0, blocking collectives: 38.6 us -> none  [the longest x1 20.4 us: on_device(): lax.all_gather(w_out, 'space', axis=0, tiled=True)]
    unnamed x1 -> x0, blocking collectives: 34.5 us -> none
    dynamic_slice x77 -> x0, local copies, waits for them, and re-layouts: 33.6 us -> none  [the longest x56 32.8 us: kernel_terms(): return lax.map(kernel_over_x, jnp.arange(width, dtype=jnp.int32))]
    psum x1 -> x0, blocking collectives: 32.1 us -> none  [on_device(): lax.psum((term_kernel, term_bdw, term_gain, term_bias, term_bout, term_ga...]
    reduce_sum x54 -> x0, other arithmetic: 23.1 us -> none  [the longest x49 21.6 us: kernel_over_y(): terms.append(jnp.sum(window.astype(jnp.float32) * grad_f, axis=(0, 1, 2)))]
  transfers between devices with their start and end apart: 7 -> 17, of which waited for: 3 -> 9; matrix products, arithmetic and copies ran while one was open for 18% -> 1% of each run, Pallas kernels for 0% -> 15%
where the time goes in v1:
time: 67.7 us; the launch traced here: 67.5 us
  starting transfers between devices  29.7 us (44%)
  Pallas kernels  16.9 us (25%)
  waiting for transfers between devices  15.3 us (23%)
  local copies, waits for them, and re-layouts  4.32 us (6%)
  between operations  0.88 us (1%)
    ppermute x15, starting transfers between devices, swap(): return lax.ppermute(x, 'space', [(i, i ^ bit) for i in range(size)])  28.3 us
    ppermute x15, waiting for transfers between devices, swap(): return lax.ppermute(x, 'space', [(i, i ^ bit) for i in range(size)])  15.3 us
    pallas_call x1, Pallas kernels, on_device(): pl.pallas_call(back_kernel, out_shape=struct(features.shape, BF16), in_sp...  4.87 us
    pallas_call x1, Pallas kernels, on_device(): pl.pallas_call(forward_kernel, out_shape=(struct((rows, 256), BF16), stru...  4.37 us
    pallas_call x1, Pallas kernels, on_device(): pl.pallas_call(grad_kernel, out_shape=(struct((HALF, LANE), BF16), struct...  4.12 us
    pallas_call x1, Pallas kernels, on_device(): pl.pallas_call(pointwise_kernel, out_shape=(struct(features.shape, BF16),...  2.66 us
    unnamed x20, local copies, waits for them, and re-layouts  1.39 us
  transfers between devices with their start and end apart: 17, of which 9 were waited for; matrix products, arithmetic and copies ran while one was open for 1% of the time, Pallas kernels for 15%

profile of v1, /device:TPU:0, one launch (start us, length us, event | category | flops | bytes accessed | tf_op | source)
XLA Modules:
  0.0 67.5 jit_solution(13620263742714796968)
XLA Ops:
  0.6 0.0 copy-start.9
  0.7 0.0 copy-start.3
  0.7 0.6 copy-done.9
  1.3 0.1 copy.23
  1.4 0.0 copy-done.3
  1.4 0.8 %concatenate.14 = bf16[48,512]{1,0:T(8,128)(2,1)S(1)} concatenate(bf16[48,192]{1,0:T(8,128)(2,1)S(1)} %copy-done.3, bf16[48,1]{1,0:T(8,128)(2,1)S(1)} %copy.23, bf16[48,63]{1,0:T(8,128)(2,1)S(1)} %broadcast_in_dim.10, bf16[48,192]{1,0:T(8,128)(2,1)} %param.19, bf16[48,64]{1,0:T(8,128)(2,1)S(1)} %broadcast_in_dim.11), dimensions={1} | concatenate | bytes 98304 | tf_op jit(solution)/shard_map/concatenate | solution.py:292
  2.3 4.1 %collective-permute-start = (bf16[48,512]{1,0:T(8,128)(2,1)S(1)}, bf16[48,512]{1,0:T(8,128)(2,1)S(1)}, u32[]{:S(2)}, u32[]{:S(2)}) collective-permute-start(bf16[48,512]{1,0:T(8,128)(2,1)S(1)} %concatenate.14), channel_id=1, source_target_pairs={{0,8},{1,9},{2,10},{3,11},{4,12},{5,13},{6,14},{7,15},{8,0},{9,1},... | collective-permute-start | bytes 147464 | tf_op jit(solution)/shard_map/ppermute | solution.py:19
  6.4 2.6 %collective-permute-done = bf16[48,512]{1,0:T(8,128)(2,1)S(1)} collective-permute-done((bf16[48,512]{1,0:T(8,128)(2,1)S(1)}, bf16[48,512]{1,0:T(8,128)(2,1)S(1)}, u32[]{:S(2)}, u32[]{:S(2)}) %collective-permute-start) | collective-permute-done | bytes 49184 | tf_op jit(solution)/shard_map/ppermute | solution.py:19
  9.0 1.4 %collective-permute-start.1 = (bf16[96,512]{1,0:T(8,128)(2,1)S(1)}, bf16[96,512]{1,0:T(8,128)(2,1)S(1)}, u32[]{:S(2)}, u32[]{:S(2)}) collective-permute-start(bf16[96,512]{1,0:T(8,128)(2,1)S(1)} %pad_maximum_fusion.2), channel_id=1, source_target_pairs={{0,4},{1,5},{2,6},{3,7},{4,0},{5,1},{6,2},{7,3},{8,12},{9,13},{10,... | collective-permute-start | bytes 294920 | tf_op jit(solution)/shard_map/ppermute | solution.py:19
  10.4 3.2 %collective-permute-done.1 = bf16[96,512]{1,0:T(8,128)(2,1)S(1)} collective-permute-done((bf16[96,512]{1,0:T(8,128)(2,1)S(1)}, bf16[96,512]{1,0:T(8,128)(2,1)S(1)}, u32[]{:S(2)}, u32[]{:S(2)}) %collective-permute-start.1) | collective-permute-done | bytes 98336 | tf_op jit(solution)/shard_map/ppermute | solution.py:19
  13.7 0.0 copy-start.1
  13.7 0.0 copy-start
  13.7 1.8 %collective-permute-start.2 = (bf16[192,512]{1,0:T(8,128)(2,1)S(1)}, bf16[192,512]{1,0:T(8,128)(2,1)S(1)}, u32[]{:S(2)}, u32[]{:S(2)}) collective-permute-start(bf16[192,512]{1,0:T(8,128)(2,1)S(1)} %pad_maximum_fusion.1), channel_id=1, source_target_pairs={{0,2},{1,3},{2,0},{3,1},{4,6},{5,7},{6,4},{7,5},{8,10},{9,11},{10,... | collective-permute-start | bytes 589832 | tf_op jit(solution)/shard_map/ppermute | solution.py:19
  15.5 4.0 %collective-permute-done.2 = bf16[192,512]{1,0:T(8,128)(2,1)S(1)} collective-permute-done((bf16[192,512]{1,0:T(8,128)(2,1)S(1)}, bf16[192,512]{1,0:T(8,128)(2,1)S(1)}, u32[]{:S(2)}, u32[]{:S(2)}) %collective-permute-start.2) | collective-permute-done | bytes 196640 | tf_op jit(solution)/shard_map/ppermute | solution.py:19
  19.5 0.1 collective-permute-start.3
  19.5 0.0 copy-done.1
  19.5 0.7 collective-permute-start.5
  20.2 3.1 %collective-permute-start.4 = (bf16[4,8,8,192]{3,2,1,0:T(8,128)(2,1)S(1)}, bf16[4,8,8,192]{3,2,1,0:T(8,128)(2,1)S(1)}, u32[]{:S(2)}, u32[]{:S(2)}) collective-permute-start(bf16[4,8,8,192]{3,2,1,0:T(8,128)(2,1)S(1)} %copy-done.1), channel_id=1, source_target_pairs={{0,1},{1,0},{2,3},{3,2},{4,5},{5,4},{6,7},{7,6},{8,9},{9,8},{10,11... | collective-permute-start | bytes 294920 | tf_op jit(solution)/shard_map/ppermute | solution.py:19
  23.3 0.0 copy-start.5
  23.3 0.0 copy-start.6
  23.3 0.0 copy-start.7
  23.4 0.0 copy-start.8
  23.4 0.0 copy-start.4
  23.4 0.7 copy-done.5
  24.0 0.0 copy-done.6
  24.0 0.0 copy-done.7
  24.1 0.0 copy-done.8
  24.1 0.0 copy-done.4
  24.1 0.0 collective-permute-done.5.q_ref
  24.1 0.2 collective-permute-done.4.p_ref
  24.3 0.0 copy-done
  24.3 4.4 %forward_stencil.1 = (bf16[256,256]{1,0:T(8,128)(2,1)S(1)}, f32[256,256]{1,0:T(8,128)S(1)}) custom-call(s32[1]{0:T(128)} %bitcast.1.odd_ref.refs_0_, bf16[4,8,8,192]{3,2,1,0:T(8,128)(2,1)S(1)} %copy-done.1, bf16[4,8,8,192]{3,2,1,0:T(8,128)(2,1)S(1)} %collective-permute-done.4.p_ref, bf16[4,8,8,192]{3,2,1,0:T(8,128)(2,1)S(1)} %collective-permute-done.5.q_ref, ...), custom_call_target="tpu_custom_call" | custom-call | tf_op jit(solution)/shard_map/forward_stencil/pallas_call | solution.py:310
  28.7 0.0 collective-permute-done.3.g1_ref
  28.7 0.0 copy-done.2
  28.7 2.7 %pointwise.1 = (bf16[4,8,8,192]{3,2,1,0:T(8,128)(2,1)}, bf16[4,8,8,192]{3,2,1,0:T(8,128)(2,1)S(1)}, bf16[384,512]{1,0:T(8,128)(2,1)S(1)}, bf16[384,512]{1,0:T(8,128)(2,1)S(1)}, f32[8,256]{1,0:T(8,128)S(1)}) custom-call(bf16[384,512]{1,0:T(8,128)(2,1)S(1)} %pad_maximum_fusion.g0_ref, bf16[384,512]{1,0:T(8,128)(2,1)S(1)} %collective-permute-done.3.g1_ref, ...), custom_call_target="tpu_custom_call" | custom-call | tf_op jit(solution)/shard_map/pointwise/pallas_call | solution.py:321
  31.4 4.1 %kernel_gradient.1 = (bf16[320,128]{1,0:T(8,128)(2,1)S(1)}, bf16[320,128]{1,0:T(8,128)(2,1)S(1)}) custom-call(s32[1]{0:T(128)} %bitcast.1.odd_ref.refs_0_, bf16[4,8,8,192]{3,2,1,0:T(8,128)(2,1)S(1)} %copy-done.1, bf16[4,8,8,192]{3,2,1,0:T(8,128)(2,1)S(1)} %collective-permute-done.4.p_ref, bf16[4,8,8,192]{3,2,1,0:T(8,128)(2,1)S(1)} %collective-permute-done.5.q_ref, ...), custom_call_target="tpu_custom_call" | custom-call | tf_op jit(solution)/shard_map/kernel_gradient/pallas_call | solution.py:350
  35.5 2.1 %collective-permute-start.8 = (bf16[320,128]{1,0:T(8,128)(2,1)S(1)}, bf16[320,128]{1,0:T(8,128)(2,1)S(1)}, u32[]{:S(2)}, u32[]{:S(2)}) collective-permute-start(bf16[320,128]{1,0:T(8,128)(2,1)S(1)} %get-tuple-element.28), channel_id=1, source_target_pairs={{0,1},{1,0},{2,3},{3,2},{4,5},{5,4},{6,7},{7,6},{8,9},{9,8},{10,11... | collective-permute-start | bytes 245768 | tf_op jit(solution)/shard_map/ppermute | solution.py:19
  37.6 0.1 collective-permute-start.13
  37.7 0.8 %collective-permute-done.8 = bf16[320,128]{1,0:T(8,128)(2,1)S(1)} collective-permute-done((bf16[320,128]{1,0:T(8,128)(2,1)S(1)}, bf16[320,128]{1,0:T(8,128)(2,1)S(1)}, u32[]{:S(2)}, u32[]{:S(2)}) %collective-permute-start.8) | collective-permute-done | bytes 81952 | tf_op jit(solution)/shard_map/ppermute | solution.py:19
  38.5 2.7 %collective-permute-start.9 = (bf16[320,128]{1,0:T(8,128)(2,1)S(1)}, bf16[320,128]{1,0:T(8,128)(2,1)S(1)}, u32[]{:S(2)}, u32[]{:S(2)}) collective-permute-start(bf16[320,128]{1,0:T(8,128)(2,1)S(1)} %add_convert_fusion.3), channel_id=1, source_target_pairs={{0,2},{1,3},{2,0},{3,1},{4,6},{5,7},{6,4},{7,5},{8,10},{9,11},{10,... | collective-permute-start | bytes 245768 | tf_op jit(solution)/shard_map/ppermute | solution.py:19
  41.2 0.7 collective-permute-start.7
  41.9 1.4 %collective-permute-start.6 = (bf16[4,8,8,192]{3,2,1,0:T(8,128)(2,1)S(1)}, bf16[4,8,8,192]{3,2,1,0:T(8,128)(2,1)S(1)}, u32[]{:S(2)}, u32[]{:S(2)}) collective-permute-start(bf16[4,8,8,192]{3,2,1,0:T(8,128)(2,1)S(1)} %get-tuple-element.25.g_ref), channel_id=1, source_target_pairs={{0,1},{1,0},{2,3},{3,2},{4,5},{5,4},{6,7},{7,6},{8,9},{9,8},{10,11... | collective-permute-start | bytes 294920 | tf_op jit(solution)/shard_map/ppermute | solution.py:19
  43.3 0.9 %collective-permute-done.9 = bf16[320,128]{1,0:T(8,128)(2,1)S(1)} collective-permute-done((bf16[320,128]{1,0:T(8,128)(2,1)S(1)}, bf16[320,128]{1,0:T(8,128)(2,1)S(1)}, u32[]{:S(2)}, u32[]{:S(2)}) %collective-permute-start.9) | collective-permute-done | bytes 81952 | tf_op jit(solution)/shard_map/ppermute | solution.py:19
  44.2 2.0 %collective-permute-start.10 = (bf16[320,128]{1,0:T(8,128)(2,1)S(1)}, bf16[320,128]{1,0:T(8,128)(2,1)S(1)}, u32[]{:S(2)}, u32[]{:S(2)}) collective-permute-start(bf16[320,128]{1,0:T(8,128)(2,1)S(1)} %add_convert_fusion.2), channel_id=1, source_target_pairs={{0,4},{1,5},{2,6},{3,7},{4,0},{5,1},{6,2},{7,3},{8,12},{9,13},{10,... | collective-permute-start | bytes 245768 | tf_op jit(solution)/shard_map/ppermute | solution.py:19
  46.2 0.0 collective-permute-done.13
  46.2 0.1 convert_add_fusion
  46.3 1.5 %collective-permute-start.14 = (bf16[192,512]{1,0:T(8,128)(2,1)S(1)}, bf16[192,512]{1,0:T(8,128)(2,1)S(1)}, u32[]{:S(2)}, u32[]{:S(2)}) collective-permute-start(bf16[192,512]{1,0:T(8,128)(2,1)S(1)} %slice.77), channel_id=1, source_target_pairs={{0,2},{1,3},{2,0},{3,1},{4,6},{5,7},{6,4},{7,5},{8,10},{9,11},{10,... | collective-permute-start | bytes 589832 | tf_op jit(solution)/shard_map/ppermute | solution.py:19
  47.9 1.4 %collective-permute-done.10 = bf16[320,128]{1,0:T(8,128)(2,1)S(1)} collective-permute-done((bf16[320,128]{1,0:T(8,128)(2,1)S(1)}, bf16[320,128]{1,0:T(8,128)(2,1)S(1)}, u32[]{:S(2)}, u32[]{:S(2)}) %collective-permute-start.10) | collective-permute-done | bytes 81952 | tf_op jit(solution)/shard_map/ppermute | solution.py:19
  49.3 3.0 %collective-permute-start.11 = (bf16[320,128]{1,0:T(8,128)(2,1)S(1)}, bf16[320,128]{1,0:T(8,128)(2,1)S(1)}, u32[]{:S(2)}, u32[]{:S(2)}) collective-permute-start(bf16[320,128]{1,0:T(8,128)(2,1)S(1)} %add_convert_fusion.1), channel_id=1, source_target_pairs={{0,8},{1,9},{2,10},{3,11},{4,12},{5,13},{6,14},{7,15},{8,0},{9,1},... | collective-permute-start | bytes 245768 | tf_op jit(solution)/shard_map/ppermute | solution.py:19
  52.3 0.4 collective-permute-done.14
  52.7 1.9 %collective-permute-start.15 = (bf16[96,512]{1,0:T(8,128)(2,1)S(1)}, bf16[96,512]{1,0:T(8,128)(2,1)S(1)}, u32[]{:S(2)}, u32[]{:S(2)}) collective-permute-start(bf16[96,512]{1,0:T(8,128)(2,1)S(1)} %slice.78), channel_id=1, source_target_pairs={{0,4},{1,5},{2,6},{3,7},{4,0},{5,1},{6,2},{7,3},{8,12},{9,13},{10,... | collective-permute-start | bytes 294920 | tf_op jit(solution)/shard_map/ppermute | solution.py:19
  54.7 0.0 collective-permute-done.11
  54.7 0.1 collective-permute-start.12
  54.8 0.0 collective-permute-done.7.q_ref
  54.8 0.0 collective-permute-done.6.p_ref
  54.8 4.9 %backward_stencil.1 = bf16[4,8,8,192]{3,2,1,0:T(8,128)(2,1)} custom-call(s32[1]{0:T(128)} %bitcast.1.odd_ref.refs_0_, bf16[4,8,8,192]{3,2,1,0:T(8,128)(2,1)S(1)} %get-tuple-element.25.g_ref, bf16[4,8,8,192]{3,2,1,0:T(8,128)(2,1)S(1)} %collective-permute-done.6.p_ref, bf16[4,8,8,192]{3,2,1,0:T(8,128)(2,1)S(1)} %collective-permute-done.7.q_ref, ...), custom_call_target="tpu_custom_call" | custom-call | tf_op jit(solution)/shard_map/backward_stencil/pallas_call | solution.py:372
  59.7 0.0 collective-permute-done.12.refs_2_
  59.7 0.9 %unpack.1 = (f32[7,7,7,192]{3,2,1,0:T(8,128)}, f32[8,256]{1,0:T(8,128)S(1)}) custom-call(s32[1]{0:T(128)} %bitcast.1.odd_ref.refs_0_, bf16[320,128]{1,0:T(8,128)(2,1)S(1)} %add_convert_fusion.refs_1_, bf16[320,128]{1,0:T(8,128)(2,1)S(1)} %collective-permute-done.12.refs_2_), custom_call_target="tpu_custom_call" | custom-call | tf_op jit(solution)/shard_map/unpack/pallas_call | solution.py:382
  60.6 0.0 collective-permute-done.15
  60.6 3.1 %collective-permute-start.16 = (bf16[48,512]{1,0:T(8,128)(2,1)S(1)}, bf16[48,512]{1,0:T(8,128)(2,1)S(1)}, u32[]{:S(2)}, u32[]{:S(2)}) collective-permute-start(bf16[48,512]{1,0:T(8,128)(2,1)S(1)} %slice.79), channel_id=1, source_target_pairs={{0,8},{1,9},{2,10},{3,11},{4,12},{5,13},{6,14},{7,15},{8,0},{9,1},... | collective-permute-start | bytes 147464 | tf_op jit(solution)/shard_map/ppermute | solution.py:19
  63.7 0.6 fusion.2
  64.3 1.8 %collective-permute-done.16 = bf16[48,512]{1,0:T(8,128)(2,1)S(1)} collective-permute-done((bf16[48,512]{1,0:T(8,128)(2,1)S(1)}, bf16[48,512]{1,0:T(8,128)(2,1)S(1)}, u32[]{:S(2)}, u32[]{:S(2)}) %collective-permute-start.16) | collective-permute-done | bytes 49184 | tf_op jit(solution)/shard_map/ppermute | solution.py:19
  66.1 0.7 %slice_reduce_fusion = f32[48]{0:T(128)} fusion(f32[48,512]{1,0:T(8,128)S(1)} %fusion), kind=kLoop, calls=%fused_computation.15 | loop fusion | bytes 384 | tf_op jit(solution)/shard_map/slice | solution.py:346
  66.8 0.6 fusion.1
  (17 shorter events, 0.3 us)
Async XLA Ops:
  0.6 0.7 copy-start.9
  0.7 0.8 %copy-start.3 = (bf16[48,192]{1,0:T(8,128)(2,1)S(1)}, bf16[48,192]{1,0:T(8,128)(2,1)}, u32[]{:S(2)}) copy-start(bf16[48,192]{1,0:T(8,128)(2,1)} %param.17) | copy-start | bytes 55300
  2.3 6.7 %collective-permute-start = (bf16[48,512]{1,0:T(8,128)(2,1)S(1)}, bf16[48,512]{1,0:T(8,128)(2,1)S(1)}, u32[]{:S(2)}, u32[]{:S(2)}) collective-permute-start(bf16[48,512]{1,0:T(8,128)(2,1)S(1)} %concatenate.14), channel_id=1, source_target_pairs={{0,8},{1,9},{2,10},{3,11},{4,12},{5,13},{6,14},{7,15},{8,0},{9,1},... | collective-permute-start | bytes 147464 | tf_op jit(solution)/shard_map/ppermute | solution.py:19
  9.0 4.7 %collective-permute-start.1 = (bf16[96,512]{1,0:T(8,128)(2,1)S(1)}, bf16[96,512]{1,0:T(8,128)(2,1)S(1)}, u32[]{:S(2)}, u32[]{:S(2)}) collective-permute-start(bf16[96,512]{1,0:T(8,128)(2,1)S(1)} %pad_maximum_fusion.2), channel_id=1, source_target_pairs={{0,4},{1,5},{2,6},{3,7},{4,0},{5,1},{6,2},{7,3},{8,12},{9,13},{10,... | collective-permute-start | bytes 294920 | tf_op jit(solution)/shard_map/ppermute | solution.py:19
  13.7 5.9 %copy-start.1 = (bf16[4,8,8,192]{3,2,1,0:T(8,128)(2,1)S(1)}, bf16[4,8,8,192]{3,2,1,0:T(8,128)(2,1)}, u32[]{:S(2)}) copy-start(bf16[4,8,8,192]{3,2,1,0:T(8,128)(2,1)} %x_ref.5) | copy-start | bytes 294916
  13.7 10.7 %copy-start = (f32[7,7,7,192]{3,2,1,0:T(8,128)S(1)}, f32[7,7,7,192]{3,2,1,0:T(8,128)}, u32[]{:S(2)}) copy-start(f32[7,7,7,192]{3,2,1,0:T(8,128)} %k_ref.3) | copy-start | bytes 790276
  13.7 5.7 %collective-permute-start.2 = (bf16[192,512]{1,0:T(8,128)(2,1)S(1)}, bf16[192,512]{1,0:T(8,128)(2,1)S(1)}, u32[]{:S(2)}, u32[]{:S(2)}) collective-permute-start(bf16[192,512]{1,0:T(8,128)(2,1)S(1)} %pad_maximum_fusion.1), channel_id=1, source_target_pairs={{0,2},{1,3},{2,0},{3,1},{4,6},{5,7},{6,4},{7,5},{8,10},{9,11},{10,... | collective-permute-start | bytes 589832 | tf_op jit(solution)/shard_map/ppermute | solution.py:19
  19.5 9.3 %collective-permute-start.3 = (bf16[384,512]{1,0:T(8,128)(2,1)S(1)}, bf16[384,512]{1,0:T(8,128)(2,1)S(1)}, u32[]{:S(2)}, u32[]{:S(2)}) collective-permute-start(bf16[384,512]{1,0:T(8,128)(2,1)S(1)} %pad_maximum_fusion.g0_ref), channel_id=1, source_target_pairs={{0,1},{1,0},{2,3},{3,2},{4,5},{5,4},{6,7},{7,6},{8,9},{9,8},{10,11... | collective-permute-start | bytes 1179656 | tf_op jit(solution)/shard_map/ppermute | solution.py:19
  19.5 4.6 %collective-permute-start.5 = (bf16[4,8,8,192]{3,2,1,0:T(8,128)(2,1)S(1)}, bf16[4,8,8,192]{3,2,1,0:T(8,128)(2,1)S(1)}, u32[]{:S(2)}, u32[]{:S(2)}) collective-permute-start(bf16[4,8,8,192]{3,2,1,0:T(8,128)(2,1)S(1)} %copy-done.1), channel_id=1, source_target_pairs={{1,2},{3,4},{5,6},{7,8},{9,10},{11,12},{13,14},{2,1},{4,3},{6,5},{... | collective-permute-start | bytes 294920 | tf_op jit(solution)/shard_map/ppermute | solution.py:25
  20.2 4.1 %collective-permute-start.4 = (bf16[4,8,8,192]{3,2,1,0:T(8,128)(2,1)S(1)}, bf16[4,8,8,192]{3,2,1,0:T(8,128)(2,1)S(1)}, u32[]{:S(2)}, u32[]{:S(2)}) collective-permute-start(bf16[4,8,8,192]{3,2,1,0:T(8,128)(2,1)S(1)} %copy-done.1), channel_id=1, source_target_pairs={{0,1},{1,0},{2,3},{3,2},{4,5},{5,4},{6,7},{7,6},{8,9},{9,8},{10,11... | collective-permute-start | bytes 294920 | tf_op jit(solution)/shard_map/ppermute | solution.py:19
  23.3 0.7 %copy-start.5 = (f32[192]{0:T(256)S(1)}, f32[192]{0:T(256)}, u32[]{:S(2)}) copy-start(f32[192]{0:T(256)} %param.14) | copy-start | bytes 2308
  23.3 0.7 %copy-start.6 = (f32[192]{0:T(256)S(1)}, f32[192]{0:T(256)}, u32[]{:S(2)}) copy-start(f32[192]{0:T(256)} %param.15) | copy-start | bytes 2308
  23.3 0.7 %copy-start.7 = (f32[192]{0:T(256)S(1)}, f32[192]{0:T(256)}, u32[]{:S(2)}) copy-start(f32[192]{0:T(256)} %param.16) | copy-start | bytes 2308
  23.4 0.7 %copy-start.8 = (f32[192]{0:T(256)S(1)}, f32[192]{0:T(256)}, u32[]{:S(2)}) copy-start(f32[192]{0:T(256)} %param.20) | copy-start | bytes 2308
  23.4 0.7 %copy-start.4 = (f32[192]{0:T(256)S(1)}, f32[192]{0:T(256)}, u32[]{:S(2)}) copy-start(f32[192]{0:T(256)} %param.21) | copy-start | bytes 2308
  24.3 4.4 %copy-start.2 = (bf16[4,8,8,192]{3,2,1,0:T(8,128)(2,1)S(1)}, bf16[4,8,8,192]{3,2,1,0:T(8,128)(2,1)}, u32[]{:S(2)}) copy-start(bf16[4,8,8,192]{3,2,1,0:T(8,128)(2,1)} %c_ref.3) | copy-start | bytes 294916
  35.5 3.0 %collective-permute-start.8 = (bf16[320,128]{1,0:T(8,128)(2,1)S(1)}, bf16[320,128]{1,0:T(8,128)(2,1)S(1)}, u32[]{:S(2)}, u32[]{:S(2)}) collective-permute-start(bf16[320,128]{1,0:T(8,128)(2,1)S(1)} %get-tuple-element.28), channel_id=1, source_target_pairs={{0,1},{1,0},{2,3},{3,2},{4,5},{5,4},{6,7},{7,6},{8,9},{9,8},{10,11... | collective-permute-start | bytes 245768 | tf_op jit(solution)/shard_map/ppermute | solution.py:19
  37.6 8.6 %collective-permute-start.13 = (bf16[384,512]{1,0:T(8,128)(2,1)S(1)}, bf16[384,512]{1,0:T(8,128)(2,1)S(1)}, u32[]{:S(2)}, u32[]{:S(2)}) collective-permute-start(bf16[384,512]{1,0:T(8,128)(2,1)S(1)} %get-tuple-element.32), channel_id=1, source_target_pairs={{0,1},{1,0},{2,3},{3,2},{4,5},{5,4},{6,7},{7,6},{8,9},{9,8},{10,11... | collective-permute-start | bytes 1179656 | tf_op jit(solution)/shard_map/ppermute | solution.py:19
  38.5 5.6 %collective-permute-start.9 = (bf16[320,128]{1,0:T(8,128)(2,1)S(1)}, bf16[320,128]{1,0:T(8,128)(2,1)S(1)}, u32[]{:S(2)}, u32[]{:S(2)}) collective-permute-start(bf16[320,128]{1,0:T(8,128)(2,1)S(1)} %add_convert_fusion.3), channel_id=1, source_target_pairs={{0,2},{1,3},{2,0},{3,1},{4,6},{5,7},{6,4},{7,5},{8,10},{9,11},{10,... | collective-permute-start | bytes 245768 | tf_op jit(solution)/shard_map/ppermute | solution.py:19
  41.2 13.6 %collective-permute-start.7 = (bf16[4,8,8,192]{3,2,1,0:T(8,128)(2,1)S(1)}, bf16[4,8,8,192]{3,2,1,0:T(8,128)(2,1)S(1)}, u32[]{:S(2)}, u32[]{:S(2)}) collective-permute-start(bf16[4,8,8,192]{3,2,1,0:T(8,128)(2,1)S(1)} %get-tuple-element.25.g_ref), channel_id=1, source_target_pairs={{1,2},{3,4},{5,6},{7,8},{9,10},{11,12},{13,14},{2,1},{4,3},{6,5},{... | collective-permute-start | bytes 294920 | tf_op jit(solution)/shard_map/ppermute | solution.py:25
  41.9 13.0 %collective-permute-start.6 = (bf16[4,8,8,192]{3,2,1,0:T(8,128)(2,1)S(1)}, bf16[4,8,8,192]{3,2,1,0:T(8,128)(2,1)S(1)}, u32[]{:S(2)}, u32[]{:S(2)}) collective-permute-start(bf16[4,8,8,192]{3,2,1,0:T(8,128)(2,1)S(1)} %get-tuple-element.25.g_ref), channel_id=1, source_target_pairs={{0,1},{1,0},{2,3},{3,2},{4,5},{5,4},{6,7},{7,6},{8,9},{9,8},{10,11... | collective-permute-start | bytes 294920 | tf_op jit(solution)/shard_map/ppermute | solution.py:19
  44.2 5.0 %collective-permute-start.10 = (bf16[320,128]{1,0:T(8,128)(2,1)S(1)}, bf16[320,128]{1,0:T(8,128)(2,1)S(1)}, u32[]{:S(2)}, u32[]{:S(2)}) collective-permute-start(bf16[320,128]{1,0:T(8,128)(2,1)S(1)} %add_convert_fusion.2), channel_id=1, source_target_pairs={{0,4},{1,5},{2,6},{3,7},{4,0},{5,1},{6,2},{7,3},{8,12},{9,13},{10,... | collective-permute-start | bytes 245768 | tf_op jit(solution)/shard_map/ppermute | solution.py:19
  46.3 6.3 %collective-permute-start.14 = (bf16[192,512]{1,0:T(8,128)(2,1)S(1)}, bf16[192,512]{1,0:T(8,128)(2,1)S(1)}, u32[]{:S(2)}, u32[]{:S(2)}) collective-permute-start(bf16[192,512]{1,0:T(8,128)(2,1)S(1)} %slice.77), channel_id=1, source_target_pairs={{0,2},{1,3},{2,0},{3,1},{4,6},{5,7},{6,4},{7,5},{8,10},{9,11},{10,... | collective-permute-start | bytes 589832 | tf_op jit(solution)/shard_map/ppermute | solution.py:19
  49.3 5.4 %collective-permute-start.11 = (bf16[320,128]{1,0:T(8,128)(2,1)S(1)}, bf16[320,128]{1,0:T(8,128)(2,1)S(1)}, u32[]{:S(2)}, u32[]{:S(2)}) collective-permute-start(bf16[320,128]{1,0:T(8,128)(2,1)S(1)} %add_convert_fusion.1), channel_id=1, source_target_pairs={{0,8},{1,9},{2,10},{3,11},{4,12},{5,13},{6,14},{7,15},{8,0},{9,1},... | collective-permute-start | bytes 245768 | tf_op jit(solution)/shard_map/ppermute | solution.py:19
  52.7 7.8 %collective-permute-start.15 = (bf16[96,512]{1,0:T(8,128)(2,1)S(1)}, bf16[96,512]{1,0:T(8,128)(2,1)S(1)}, u32[]{:S(2)}, u32[]{:S(2)}) collective-permute-start(bf16[96,512]{1,0:T(8,128)(2,1)S(1)} %slice.78), channel_id=1, source_target_pairs={{0,4},{1,5},{2,6},{3,7},{4,0},{5,1},{6,2},{7,3},{8,12},{9,13},{10,... | collective-permute-start | bytes 294920 | tf_op jit(solution)/shard_map/ppermute | solution.py:19
  54.7 5.0 %collective-permute-start.12 = (bf16[320,128]{1,0:T(8,128)(2,1)S(1)}, bf16[320,128]{1,0:T(8,128)(2,1)S(1)}, u32[]{:S(2)}, u32[]{:S(2)}) collective-permute-start(bf16[320,128]{1,0:T(8,128)(2,1)S(1)} %add_convert_fusion.refs_1_), channel_id=1, source_target_pairs={{0,1},{1,0},{2,3},{3,2},{4,5},{5,4},{6,7},{7,6},{8,9},{9,8},{10,11... | collective-permute-start | bytes 245768 | tf_op jit(solution)/shard_map/ppermute | solution.py:19
  60.6 5.5 %collective-permute-start.16 = (bf16[48,512]{1,0:T(8,128)(2,1)S(1)}, bf16[48,512]{1,0:T(8,128)(2,1)S(1)}, u32[]{:S(2)}, u32[]{:S(2)}) collective-permute-start(bf16[48,512]{1,0:T(8,128)(2,1)S(1)} %slice.79), channel_id=1, source_target_pairs={{0,8},{1,9},{2,10},{3,11},{4,12},{5,13},{6,14},{7,15},{8,0},{9,1},... | collective-permute-start | bytes 147464 | tf_op jit(solution)/shard_map/ppermute | solution.py:19

commit v2 on v1

v2 whole, which is shorter than its diff:
```python
import functools

import jax
import jax.numpy as jnp
import numpy as np
from jax import lax
from jax.experimental import pallas as pl
from jax.experimental.pallas import tpu as pltpu
from jax.sharding import PartitionSpec as P

root_half = 0.7071067811865476
inv_root_tau = 0.3989422804014327
F32 = jnp.float32
BF16 = jnp.bfloat16
LANE = 128
VMEM = pl.BlockSpec(memory_space=pltpu.VMEM)
HBM = pl.BlockSpec(memory_space=pltpu.HBM)
SMEM = pl.BlockSpec(memory_space=pltpu.SMEM)

POINTS = (0.4, 0.8, 1.25, 2.5)
PAIRS = len(POINTS)


def analysis():
    finite = [0.0] + [sign * p for p in POINTS for sign in (1.0, -1.0)]
    vander = np.array([[x**k for k in range(10)] for x in finite] + [[0.0] * 9 + [1.0]])
    inverse = np.linalg.inv(vander).T
    even = [{k: float(inverse[1 + 2 * q, k]) for k in (2, 4, 6, 8)} for q in range(PAIRS)]
    odd = [{k: float(inverse[1 + 2 * q, k]) for k in (1, 3, 5, 7)} for q in range(PAIRS)]
    zero = {k: float(inverse[0, k]) for k in (0, 2, 4, 6, 8)}
    infinity = {k: float(inverse[9, k]) for k in (1, 3, 5, 7, 9)}
    return even, odd, zero, infinity


def evaluation(size):
    even = [{k: p**k for k in range(0, size, 2)} for p in POINTS]
    odd = [{k: p**k for k in range(1, size, 2)} for p in POINTS]
    return even, odd, {0: 1.0}, {size - 1: 1.0}


def weighted(load, weights):
    total = None
    for k, w in weights.items():
        term = load(k) if w == 1.0 else load(k) * w
        total = term if total is None else total + term
    return total


def low_lanes(shape):
    return lax.broadcasted_iota(jnp.int32, shape, len(shape) - 1) < 64


def to_points(tables, main, rest, store):
    even, odd, zero, infinity = tables
    for q in range(PAIRS):
        e, o = weighted(main, even[q]), weighted(main, odd[q])
        store(1 + 2 * q, e + o)
        store(2 + 2 * q, e - o)
        e, o = weighted(rest, even[q]), weighted(rest, odd[q])
        store(10 + q, jnp.where(low_lanes(e.shape), e + o, e - o))
    store(0, weighted(main, zero))
    store(9, weighted(main, infinity))
    z, i = weighted(rest, zero), weighted(rest, infinity)
    store(14, jnp.where(low_lanes(z.shape), z, i))


def from_points(size, load, power=0):
    main, rest = [None] * size, [None] * size

    def add(into, k, v, w):
        term = v if w == 1.0 else v * w
        into[k] = term if into[k] is None else into[k] + term

    for q in range(PAIRS):
        plus, minus, both = load(1 + 2 * q), load(2 + 2 * q), load(10 + q)
        swapped = pltpu.roll(both, 64, axis=both.ndim - 1)
        sums = (plus + minus, both + swapped), (plus - minus, both - swapped)
        for k in range(size):
            m, r = sums[k % 2]
            add(main, k, m, POINTS[q] ** (k + power))
            add(rest, k, r, POINTS[q] ** (k + power))
    ends = load(14)
    add(main, 0, load(0), 1.0)
    add(rest, 0, ends, 1.0)
    add(main, size - 1, load(9), 1.0)
    add(rest, size - 1, pltpu.roll(ends, 64, axis=ends.ndim - 1), 1.0)
    return main, rest


def swap(x, bit):
    size = lax.axis_size("space")
    return lax.ppermute(x, "space", [(i, i ^ bit) for i in range(size)])


def swap_odd(x):
    size = lax.axis_size("space")
    return lax.ppermute(x, "space", [(i, (i + 1 if i % 2 else i - 1) % size) for i in range(size)])


def shifted(v, by):
    if by == 0:
        return v
    row = lax.broadcasted_iota(jnp.int32, v.shape, 0)
    keep = (row < 8 - by) if by > 0 else (row >= -by)
    return jnp.where(keep, pltpu.roll(v, (-by) % 8, axis=0), 0.0)


def split(v, z_ref, plane):
    z_ref[0, plane] = v[..., :LANE]
    z_ref[1, plane, ..., 0:64] = v[..., LANE:]
    z_ref[1, plane, ..., 64:128] = v[..., LANE:]


def pack_planes(first, load, out_ref):
    for k in range(3):
        v = load(first + k)
        cells = v.shape[0]
        at = k * cells * 3 // 2
        out_ref[at : at + cells] = v[:, :LANE].astype(BF16)
        pair = jnp.concatenate([v[: cells // 2, LANE:], v[cells // 2 :, LANE:]], axis=1)
        out_ref[at + cells : at + cells * 3 // 2] = pair.astype(BF16)


def fill_rim(last, me_ref, p_ref, q_ref, z_ref):
    me = me_ref[0]
    odd = lax.rem(me, 2) == 1
    p, q = p_ref[...].astype(F32), q_ref[...].astype(F32)
    before = jnp.where(me == 0, 0.0, jnp.where(odd, p, q))
    after = jnp.where(me == last, 0.0, jnp.where(odd, q, p))
    rows, cols = z_ref.shape[2], z_ref.shape[3]
    cells = rows * cols
    for k in range(3):
        at = k * cells * 3 // 2
        for v, plane in ((before, k), (after, k + 7)):
            z_ref[0, plane] = v[at : at + cells].reshape(rows, cols, LANE)
            pair = v[at + cells : at + cells * 3 // 2]
            swapped = pltpu.roll(pair, 64, axis=1)
            low = low_lanes(pair.shape)
            z_ref[1, plane, : rows // 2] = jnp.where(low, pair, swapped).reshape(rows // 2, cols, LANE)
            z_ref[1, plane, rows // 2 :] = jnp.where(low, swapped, pair).reshape(rows // 2, cols, LANE)


def fill_taps(k_ref, r_ref, t_ref):
    for a in range(7):
        for b in range(7):
            v = k_ref[a, b]
            r_ref[0, a, b, 0:7] = v[:, :LANE]
            r_ref[1, a, b, 0:7, 0:64] = v[:, LANE:]
            r_ref[1, a, b, 0:7, 64:128] = v[:, LANE:]
    for b in range(7):

        def store(u, v):
            t_ref[u, b] = v
            if u == 14:
                t_ref[15, b] = pltpu.roll(v, 64, axis=1)

        to_points(evaluation(7), lambda k: r_ref[0, k, b], lambda k: r_ref[1, k, b], store)


def reversed_unit(u):
    same_sign = 2 * PAIRS - 1 - 2 * ((u - 1) // 2) + (u - 1) % 2
    paired = 19 + PAIRS - u
    return jnp.where(
        u == 0, 9, jnp.where(u < 9, same_sign, jnp.where(u == 9, 0, jnp.where(u < 14, paired, 15)))
    )


def stencil(z_ref, t_ref, s_ref, u_ref, flip):
    def row(j, carry):
        def store(u, v):
            s_ref[3, u, j] = v

        to_points(analysis(), lambda k: z_ref[0, k, j], lambda k: z_ref[1, k, j], store)
        return carry

    lax.fori_loop(0, 8, row, 0)

    def unit(u, carry):
        taps_at = reversed_unit(u) if flip else u
        rows = [s_ref[3, u, j] for j in range(8)]
        for e in range(7):
            if e != 3:
                for j in range(8):
                    s_ref[e, u, j] = shifted(rows[j], e - 3)
        acc = [None] * 8
        for e in range(7):
            taps = []
            for b in range(7):
                fb, fe = (6 - b, 6 - e) if flip else (b, e)
                taps.append(jnp.broadcast_to(t_ref[taps_at, fb, fe : fe + 1], (8, LANE)))
            for source in range(8):
                x = rows[source] if e == 3 else s_ref[e, u, source]
                for b in range(7):
                    j = source - b + 3
                    if 0 <= j < 8:
                        term = x * taps[b]
                        acc[j] = term if acc[j] is None else acc[j] + term
        for j in range(8):
            u_ref[u, j] = acc[j]
        return carry

    lax.fori_loop(0, 3 * (PAIRS + 1), unit, 0)


def fetch(sources, targets, sem):
    copies = [pltpu.make_async_copy(x, y, sem.at[i]) for i, (x, y) in enumerate(zip(sources, targets))]
    for copy in copies:
        copy.start()
    return copies


def pack_kernel(me_ref, wi_hbm, b_hbm, wo_hbm, x_hbm, out_ref, core_ref, far_ref, wi_ref, b_ref, wo_ref, x_ref, sem):
    copies = fetch((x_hbm, wi_hbm, b_hbm, wo_hbm), (x_ref, wi_ref, b_ref, wo_ref), sem)
    units = wi_ref.shape[0]
    high = (out_ref.shape[0] - 16) // 3
    out_ref[...] = jnp.zeros(out_ref.shape, BF16)
    for copy in copies:
        copy.wait()
    w_in, w_out = wi_ref[...].astype(F32), wo_ref[...].astype(F32)
    out_ref[0:units] = w_in[:, :LANE].astype(BF16)
    out_ref[high : high + units] = jnp.concatenate([w_in[:, LANE:], w_out[:, LANE:]], axis=1).astype(BF16)
    out_ref[2 * high : 2 * high + units] = w_out[:, :LANE].astype(BF16)
    line = b_ref[...].astype(F32).reshape(1, units)
    line = jnp.concatenate([line, jnp.zeros((1, LANE - units), F32)], axis=1)
    first = lax.broadcasted_iota(jnp.int32, (16, LANE), 0) == 0
    out_ref[3 * high : 3 * high + 16] = jnp.where(first, jnp.broadcast_to(line, (16, LANE)), 0.0).astype(BF16)
    odd = lax.rem(me_ref[0], 2)

    def plane(i):
        v = x_ref[i].astype(F32)
        return v.reshape(v.shape[0] * v.shape[1], v.shape[2])

    pack_planes(1 - odd, plane, core_ref)
    pack_planes(odd, plane, far_ref)


def gather_lines(lines, high):
    count = -(-len(lines) * high // LANE)
    out = [jnp.zeros((8, LANE), F32)] * count
    lane = lax.broadcasted_iota(jnp.int32, (8, LANE), 1)
    for i, line in enumerate(lines):
        at, shift = divmod(i * high, LANE)
        moved = pltpu.roll(line, shift, axis=1) if shift else line
        out[at] = out[at] + jnp.where(lane >= shift, moved, 0.0)
        if shift + high > LANE:
            out[at + 1] = out[at + 1] + jnp.where(lane < shift, moved, 0.0)
    return out


def scatter_lines(full, count, high):
    lane = lax.broadcasted_iota(jnp.int32, (8, LANE), 1)
    lines = []
    for i in range(count):
        at, shift = divmod(i * high, LANE)
        v = pltpu.roll(full[at], LANE - shift, axis=1) if shift else full[at]
        if shift + high > LANE:
            v = jnp.where(lane < LANE - shift, v, pltpu.roll(full[at + 1], LANE - shift, axis=1))
        lines.append(jnp.where(lane < high, v, 0.0))
    return lines


def prepare_kernel(*refs):
    sources, refs = refs[:9], refs[9:]
    (w_ref, z_ref, t_ref, vec_ref, xf_ref, cf_ref, db_ref), refs = refs[:7], refs[7:]
    r_ref, x_ref, c_ref, k_ref, *vec_refs, sem = refs
    copies = fetch(sources, (x_ref, c_ref, k_ref, *vec_refs, w_ref), sem)
    copies[2].wait()
    fill_taps(k_ref, r_ref, t_ref)
    for copy in copies[:2] + copies[3:]:
        copy.wait()
    rows, chans = xf_ref.shape
    for i, ref in enumerate(vec_refs):
        vec_ref[i : i + 1] = ref[...].reshape(1, chans)
    for i in range(4):
        split(x_ref[i].astype(F32), z_ref, i)
    xf_ref[...] = x_ref[...].astype(F32).reshape(rows, chans)
    cot = c_ref[...].astype(F32).reshape(rows, chans)
    cf_ref[...] = cot
    d_branch = cot * vec_ref[4:5]
    vec_ref[5:6] = jnp.sum(d_branch, axis=0, keepdims=True)
    vec_ref[6:8] = jnp.zeros((2, chans), F32)
    db_ref[...] = jnp.concatenate([d_branch, jnp.zeros((rows, 256 - chans), F32)], axis=1).astype(BF16)


def forward_kernel(last, me_ref, own_ref, p_ref, q_ref, t_ref, vec_ref, na_ref, unit_ref, s_ref, z_ref, u_ref, m_ref):
    fill_rim(last, me_ref, p_ref, q_ref, z_ref)
    z_ref[:, 3:7] = own_ref[...]
    stencil(z_ref, t_ref, s_ref, u_ref, False)

    def row(j, carry):
        main, rest = from_points(4, lambda u: u_ref[u, j])
        for i in range(4):
            at = pl.ds(pl.multiple_of(64 * i + 8 * j, 8), 8)
            m_ref[at, 0:LANE] = main[i]
            m_ref[at, LANE : LANE + 64] = rest[i][:, 0:64]
        return carry

    lax.fori_loop(0, 8, row, 0)
    chans = m_ref.shape[1]
    mixed = m_ref[...] + vec_ref[0:1]
    centred = mixed - jnp.mean(mixed, axis=-1, keepdims=True)
    inverse = lax.rsqrt(jnp.mean(centred * centred, axis=-1, keepdims=True) + 1e-06)
    unit = centred * inverse
    normed = unit * vec_ref[1:2] + vec_ref[2:3]
    rows = unit.shape[0]
    na_ref[:, 0:chans] = normed.astype(BF16)
    na_ref[:, chans:256] = jnp.zeros((rows, 256 - chans), BF16)
    unit_ref[:, 0:chans] = unit
    unit_ref[:, chans:256] = jnp.broadcast_to(inverse, (rows, 256 - chans))


def pointwise_kernel(me_ref, g0_ref, g1_ref, na_ref, unit_ref, xf_ref, cf_ref, db_ref, vec_ref, out_ref, dm_ref, core_ref, far_ref, w0_ref, w1_ref, small_ref, wi_ref, wo_ref, di_ref, do_ref, m_ref):
    rows, chans = xf_ref.shape
    normed = na_ref[...]
    d_b = db_ref[...]
    gamma = vec_ref[4:5]
    branch = jnp.zeros((rows, 256), F32)
    d_normed = jnp.zeros((rows, 256), F32)
    over_c = (((1,), (1,)), ((), ()))
    over_rows = (((0,), (0,)), ((), ()))
    pieces, high = g0_ref.shape[0], (g0_ref.shape[1] - 16) // 3
    low = low_lanes((high, LANE))
    first_row = lax.broadcasted_iota(jnp.int32, (16, LANE), 0) == 0
    for g_ref, w_ref in ((g0_ref, w0_ref), (g1_ref, w1_ref)):
        lines = []
        for i in range(pieces):
            here = slice(i * high, i * high + high)
            rest = g_ref[i, high : 2 * high].astype(F32)
            wi_ref[here, 0:LANE] = g_ref[i, 0:high]
            wi_ref[here, LANE:256] = jnp.where(low, rest, 0.0).astype(BF16)
            wo_ref[here, 0:LANE] = g_ref[i, 2 * high : 3 * high]
            wo_ref[here, LANE:256] = jnp.where(low, pltpu.roll(rest, 64, axis=1), 0.0).astype(BF16)
            line = g_ref[i, 3 * high : 3 * high + 16].astype(F32)[0:1]
            lines.append(jnp.broadcast_to(line, (8, LANE)))
        bias = gather_lines(lines, high)
        d_bias = []
        for c in range(pieces * high // LANE):
            here = slice(c * LANE, c * LANE + LANE)
            w_in, w_out = wi_ref[here], wo_ref[here]
            pre = lax.dot_general(normed, w_in, over_c, preferred_element_type=F32) + bias[c][0:1]
            d_hidden = lax.dot_general(d_b, w_out, over_c, preferred_element_type=F32)
            cdf = 0.5 * (1.0 + lax.erf(pre * root_half))
            hidden = (pre * cdf).astype(BF16)
            slope = cdf + pre * jnp.exp(-0.5 * pre * pre) * inv_root_tau
            d_pre = d_hidden * slope
            d_bias.append(jnp.broadcast_to(jnp.sum(d_pre, axis=0, keepdims=True), (8, LANE)))
            d_pre = d_pre.astype(BF16)
            branch = branch + jnp.dot(hidden, w_out, preferred_element_type=F32)
            d_normed = d_normed + jnp.dot(d_pre, w_in, preferred_element_type=F32)
            di_ref[here] = lax.dot_general(d_pre, normed, over_rows, preferred_element_type=F32)
            do_ref[here] = lax.dot_general(hidden, d_b, over_rows, preferred_element_type=F32)
        for i, line in enumerate(scatter_lines(d_bias, pieces, high)):
            here = slice(i * high, i * high + high)
            rest = jnp.where(low, di_ref[here, LANE:256], pltpu.roll(do_ref[here, LANE:256], 64, axis=1))
            w_ref[i, 0:high] = di_ref[here, 0:LANE].astype(w_ref.dtype)
            w_ref[i, high : 2 * high] = rest.astype(w_ref.dtype)
            w_ref[i, 2 * high : 3 * high] = do_ref[here, 0:LANE].astype(w_ref.dtype)
            line = jnp.where(first_row, jnp.broadcast_to(line[0:1], (16, LANE)), 0.0)
            w_ref[i, 3 * high : 3 * high + 16] = line.astype(w_ref.dtype)
    branch = branch[:, 0:chans] + vec_ref[3:4]
    out_ref[...] = (xf_ref[...] + gamma * branch).reshape(out_ref.shape).astype(BF16)
    d_normed = d_normed[:, 0:chans]
    unit = unit_ref[:, 0:chans]
    inverse = unit_ref[:, chans : chans + 1]
    scaled = d_normed * vec_ref[1:2]
    d_mixed = inverse * (
        scaled
        - jnp.mean(scaled, axis=-1, keepdims=True)
        - unit * jnp.mean(scaled * unit, axis=-1, keepdims=True)
    )
    dm_ref[...] = d_mixed.reshape(dm_ref.shape).astype(BF16)
    m_ref[...] = d_mixed.reshape(m_ref.shape)
    odd = lax.rem(me_ref[0], 2)
    pack_planes(1 - odd, lambda i: m_ref[i], core_ref)
    pack_planes(odd, lambda i: m_ref[i], far_ref)
    small_ref[...] = jnp.zeros(small_ref.shape, F32)
    sums = (d_mixed, d_normed * unit, d_normed, None, cf_ref[...] * branch)
    for i, term in enumerate(sums):
        total = vec_ref[5:6] if term is None else jnp.sum(term, axis=0, keepdims=True)
        small_ref[i : i + 1, 0:chans] = total


def rows_to_one(v):
    row = lax.broadcasted_iota(jnp.int32, (8, LANE), 0)
    v = list(v) + [jnp.zeros((8, LANE), F32)]
    for half in (4, 2, 1):
        low = (row & half) == 0
        v = [
            jnp.where(low, v[i], v[i + half])
            + jnp.where(
                low,
                pltpu.roll(v[i], 8 - half, axis=0),
                pltpu.roll(v[i + half], half, axis=0),
            )
            for i in range(half)
        ]
    return v[0]


HALF = 320


def grad_kernel(me_ref, s_ref, g_ref, small_ref, keep_ref, send_ref, z_ref, t_ref, o_ref, wa_ref, wb_ref, w_ref):
    odd = lax.rem(me_ref[0], 2)
    for i in range(4):
        split(g_ref[i].astype(F32), z_ref, i)

    def row(j, carry):
        def store(u, v):
            t_ref[u, j] = v

        to_points(evaluation(4), lambda k: z_ref[0, k, j], lambda k: z_ref[1, k, j], store)
        return carry

    lax.fori_loop(0, 8, row, 0)

    def unit(u, carry):
        grads = [t_ref[u, j] for j in range(8)]
        for e in range(7):
            acc = [None] * 7
            for source in range(8):
                x = s_ref[e, u, source]
                for b in range(7):
                    j = source - b + 3
                    if 0 <= j < 8:
                        term = x * grads[j]
                        acc[b] = term if acc[b] is None else acc[b] + term
            o_ref[u, e] = rows_to_one(acc)
        return carry

    lax.fori_loop(0, 3 * (PAIRS + 1), unit, 0)

    for b in range(49):
        at = 64 * (b // 7) + 8 * (b % 7)
        wa_ref[at : at + 8] = jnp.zeros((8, LANE), F32)
        wb_ref[at : at + 8] = jnp.zeros((8, LANE), F32)
    for e in range(7):
        main, rest = from_points(7, lambda u: o_ref[u, e])
        for a in range(7):
            wa_ref[pl.ds(a * 64 + e, 8, stride=8), :] = main[a]
            one = jnp.where(low_lanes((8, LANE)), rest[a], pltpu.roll(rest[a], 64, axis=1))
            wb_ref[pl.ds(a * 64 + e, 8, stride=8), :] = one

    low = lax.broadcasted_iota(jnp.int32, (56, LANE), 1) < 64
    for a in range(5):
        w_ref[0, 56 * a : 56 * a + 56] = wa_ref[64 * a : 64 * a + 56]
    w_ref[0, 280:288] = small_ref[:, 0:LANE]
    w_ref[0, 288:HALF] = jnp.zeros((HALF - 288, LANE), F32)
    for a in range(5, 7):
        w_ref[1, 56 * (a - 5) : 56 * (a - 5) + 56] = wa_ref[64 * a : 64 * a + 56]
    for a in range(3):
        w_ref[1, 112 + 56 * a : 168 + 56 * a] = jnp.where(
            low, wb_ref[64 * a : 64 * a + 56], wb_ref[64 * (a + 4) : 64 * (a + 4) + 56]
        )
    w_ref[1, 280:312] = jnp.where(low[0:32], wb_ref[192:224], wb_ref[224:256])
    w_ref[1, 312:320] = small_ref[:, LANE:256]
    keep_ref[...] = w_ref[odd]
    send_ref[...] = w_ref[1 - odd].astype(BF16)


def unpack_kernel(scale, me_ref, mine_ref, other_ref, dk_ref, *refs):
    odd, small_refs, w_ref = lax.rem(me_ref[0], 2), refs[:5], refs[5]
    w_ref[odd] = mine_ref[...].astype(F32) * scale
    w_ref[1 - odd] = other_ref[...].astype(F32) * scale
    for a in range(7):
        for b in range(7):
            row = 56 * a + 8 * b if a < 5 else 56 * (a - 5) + 8 * b
            main = w_ref[0 if a < 5 else 1, row : row + 7]
            if a == 3:
                at, lane = 280 + 8 * (b % 4), 64 * (b // 4)
            else:
                at, lane = 112 + 56 * (a % 4) + 8 * b, 64 * (a // 4)
            rest = w_ref[1, at : at + 7]
            dk_ref[a, b, :, 0:LANE] = main
            dk_ref[a, b, :, LANE : LANE + 64] = rest[:, lane : lane + 64]
    for i, ref in enumerate(small_refs):
        ref[:, 0:LANE] = w_ref[0, 280 + i : 281 + i]
        ref[:, LANE : LANE + 64] = w_ref[1, 312 + i : 313 + i, 0:64]


def finish_kernel(scale, a_ref, b_ref, wi_ref, bi_ref, wo_ref):
    total = (a_ref[...] + b_ref[...].astype(F32)) * scale
    units = wi_ref.shape[0]
    high = (total.shape[0] - 16) // 3
    rest = total[high : high + units]
    wi_ref[:, 0:LANE] = total[0:units]
    wi_ref[:, LANE : LANE + 64] = rest[:, 0:64]
    wo_ref[:, 0:LANE] = total[2 * high : 2 * high + units]
    wo_ref[:, LANE : LANE + 64] = rest[:, 64:LANE]
    bi_ref[...] = total[3 * high : 3 * high + 1, 0:units]


def back_kernel(last, me_ref, g_ref, p_ref, q_ref, t_ref, c_ref, dx_ref, z_ref, s_ref, u_ref):
    fill_rim(last, me_ref, p_ref, q_ref, z_ref)
    for i in range(4):
        split(g_ref[i].astype(F32), z_ref, 3 + i)
    stencil(z_ref, t_ref, s_ref, u_ref, True)
    main, rest = from_points(4, lambda u: u_ref[u], 6)
    for i in range(4):
        cot = c_ref[64 * i : 64 * i + 64].reshape(8, 8, c_ref.shape[1])
        dx_ref[i, :, :, 0:LANE] = (cot[:, :, 0:LANE] + main[i]).astype(BF16)
        dx_ref[i, :, :, LANE : LANE + 64] = (cot[:, :, LANE:] + rest[i][:, :, 0:64]).astype(BF16)


def params(mib):
    return pltpu.CompilerParams(vmem_limit_bytes=mib * 1024 * 1024)


def cost(us):
    return pl.CostEstimate(flops=int(us * 1.0e9), bytes_accessed=0, transcendentals=0)


def struct(shape, dtype):
    return jax.ShapeDtypeStruct(shape, dtype)


def on_device(
    features, cotangent, kernel, b_dw, ln_gain, ln_bias, w_in_t, b_in, w_out, b_out, gamma
):
    size_x, size_y, size_z, chans = features.shape
    devices = lax.axis_size("space")
    scale = float(size_x * devices * size_y * size_z) ** (-0.5)
    rows = size_x * size_y * size_z
    units = w_in_t.shape[0]
    bits = [1 << i for i in range(devices.bit_length() - 1)]
    order = bits
    me = lax.axis_index("space").astype(jnp.int32).reshape(1)
    def call(body, name, us, mib, out_shape, operands, scratch=(), spec=VMEM):
        specs = [SMEM if x is me else spec for x in operands]
        return pl.pallas_call(
            body,
            out_shape=out_shape,
            in_specs=specs,
            out_specs=jax.tree.map(lambda _: VMEM, out_shape),
            scratch_shapes=list(scratch),
            compiler_params=params(mib),
            name=name,
            cost_estimate=cost(us),
        )(*operands)

    z_scratch = pltpu.VMEM((2, 10, size_y, size_z, LANE), F32)
    u_scratch = pltpu.VMEM((15, size_y, size_z, LANE), F32)
    shifts = (7, 15, size_y, size_z, LANE)
    cells = struct((rows, chans), F32)

    high = -(-units // 16) * 16
    lines = 3 * high + 16
    rim = struct((3 * size_y * size_z * 3 // 2, LANE), BF16)
    raw = (w_in_t, b_in, w_out, features)
    piece, to_core, to_far = call(
        pack_kernel,
        "pack",
        1.0,
        56,
        (struct((lines, LANE), BF16), rim, rim),
        (me,) + raw,
        [pltpu.VMEM(x.shape, x.dtype) for x in raw] + [pltpu.SemaphoreType.DMA((4,))],
        HBM,
    )
    x_core, x_far = swap(to_core, 1), swap_odd(to_far)
    weights = swap(piece, order[-1])
    given = (features, cotangent, kernel, b_dw, ln_gain, ln_bias, b_out, gamma, piece)
    prepared = call(
        prepare_kernel,
        "prepare",
        1.0,
        6,
        (
            struct((lines, LANE), BF16),
            struct((2, 4, size_y, size_z, LANE), F32),
            struct((16, 7, 8, LANE), F32),
            struct((8, chans), F32),
            cells,
            cells,
            struct((rows, 256), BF16),
        ),
        given,
        [pltpu.VMEM((2, 7, 7, 8, LANE), F32)]
        + [pltpu.VMEM(x.shape, x.dtype) for x in given[:-1]]
        + [pltpu.SemaphoreType.DMA((len(given),))],
        HBM,
    )
    weights, x_core, prepared = lax.optimization_barrier((weights, x_core, prepared))
    piece, own, taps, vecs, x_f32, cot_f32, d_branch = prepared
    weights = jnp.stack([piece, weights])
    for bit in order[-2:1:-1]:
        weights = jnp.concatenate([weights, swap(weights, bit)], axis=0)
    weights, x_far = lax.optimization_barrier((weights, x_far))
    weights = jnp.concatenate([weights, swap(weights, order[1])], axis=0)
    forward = call(
        functools.partial(forward_kernel, devices - 1),
        "forward_stencil",
        2.5,
        10,
        (struct((rows, 256), BF16), struct((rows, 256), F32), struct(shifts, F32)),
        (me, own, x_core, x_far, taps, vecs),
        [z_scratch, u_scratch, pltpu.VMEM((rows, chans), F32)],
    )
    weights, forward = lax.optimization_barrier((weights, forward))
    normed, unit, shifted_x = forward
    weights_other = swap(weights, 1)

    pieces = weights.shape[0]
    output, d_mixed, to_core, to_far, grad_keep, grad_send, small = call(
        pointwise_kernel,
        "pointwise",
        2.5,
        16,
        (
            struct(features.shape, BF16),
            struct(features.shape, BF16),
            rim,
            rim,
            struct((pieces, lines, LANE), F32),
            struct((pieces, lines, LANE), BF16),
            struct((8, 256), F32),
        ),
        (me, weights, weights_other, normed, unit, x_f32, cot_f32, d_branch, vecs),
        [pltpu.VMEM((pieces * high, 256), BF16)] * 2
        + [pltpu.VMEM((pieces * high, 256), F32)] * 2
        + [pltpu.VMEM((size_x, size_y * size_z, chans), F32)],
    )
    keep, send = call(
        grad_kernel,
        "kernel_gradient",
        2.0,
        10,
        (struct((HALF, LANE), F32), struct((HALF, LANE), BF16)),
        (me, shifted_x, d_mixed, small),
        [
            pltpu.VMEM((2, 4, size_y, size_z, LANE), F32),
            u_scratch,
            pltpu.VMEM((15, 7, 8, LANE), F32),
            pltpu.VMEM((448, LANE), F32),
            pltpu.VMEM((448, LANE), F32),
            pltpu.VMEM((2, HALF, LANE), F32),
        ],
    )

    total = (grad_keep + swap(grad_send, 1).astype(F32)).reshape(pieces * lines, LANE)
    sums = keep + swap(send, 1).astype(F32)
    sums, to_core, to_far = lax.optimization_barrier((sums, to_core, to_far))
    g_core, g_far = swap(to_core, 1), swap_odd(to_far)
    for step, bit in enumerate(order[1:]):
        n = total.shape[0] // 2
        mine, kept = sums.astype(BF16), total[:n]
        got = swap(jnp.concatenate([mine, total[n:].astype(BF16)], axis=0), bit)
        if step == len(order) - 3:
            got, g_core, g_far = lax.optimization_barrier((got, g_core, g_far))
            d_x = call(
                functools.partial(back_kernel, devices - 1),
                "backward_stencil",
                2.5,
                10,
                struct(features.shape, BF16),
                (me, d_mixed, g_core, g_far, taps, cot_f32),
                [z_scratch, pltpu.VMEM(shifts, F32), u_scratch],
            )
        if step == len(order) - 2:
            got, d_x = lax.optimization_barrier((got, d_x))
        sums = mine.astype(F32) + got[:HALF].astype(F32)
        got = got[HALF:]
        total = kept + got.astype(F32)
    mine = sums.astype(BF16)
    other = swap(mine, 1)
    d_w_in, d_b_in, d_w_out = call(
        functools.partial(finish_kernel, scale),
        "finish",
        0.7,
        4,
        (struct((units, chans), F32), struct((1, units), F32), struct((units, chans), F32)),
        (kept, got),
    )
    d_kernel, *vectors = call(
        functools.partial(unpack_kernel, scale),
        "unpack",
        0.9,
        4,
        (struct(kernel.shape, F32),) + (struct((1, chans), F32),) * 5,
        (me, mine, other),
        [pltpu.VMEM((2, HALF, LANE), F32)],
    )
    d_b_dw, d_ln_gain, d_ln_bias, d_b_out, d_gamma = [v.reshape(chans) for v in vectors]
    return (
        output,
        d_x,
        d_kernel,
        d_b_dw,
        d_ln_gain,
        d_ln_bias,
        d_w_in,
        d_b_in.reshape(units),
        d_w_out,
        d_b_out,
        d_gamma,
    )


def solution(mesh):
    in_specs = (
        P(("crop", "space"), None, None, None),
        P(("crop", "space"), None, None, None),
        P(),
        P(),
        P(),
        P(),
        P("space", None),
        P("space"),
        P("space", None),
        P(),
        P(),
    )
    out_specs = (
        P(("crop", "space"), None, None, None),
        P(("crop", "space"), None, None, None),
        P("crop", None, None, None),
        P("crop"),
        P("crop"),
        P("crop"),
        P(("crop", "space"), None),
        P(("crop", "space")),
        P(("crop", "space"), None),
        P("crop"),
        P("crop"),
    )
    return jax.shard_map(
        on_device, mesh=mesh, in_specs=in_specs, out_specs=out_specs, check_vma=False
    )
```

time: 67.7 us -> 56.4 us (0.83)
  starting transfers between devices: 29.7 us -> 11.1 us
  waiting for transfers between devices: 15.3 us -> 28.1 us
  local copies, waits for them, and re-layouts: 4.32 us -> 0.89 us
  Pallas kernels: 16.9 us -> 14.8 us
    ppermute x15 -> x12, starting transfers between devices: 28.3 us -> 6.65 us  [swap(): return lax.ppermute(x, 'space', [(i, i ^ bit) for i in range(size)])]
    ppermute x2, waiting for transfers between devices: 0.01 us -> 8.11 us  [swap_odd(): lax.ppermute(x, 'space', [(i, (i + 1 if i % 2 else i - 1) % size) for i i...]
    ppermute x15 -> x12, waiting for transfers between devices: 15.3 us -> 20 us  [swap(): return lax.ppermute(x, 'space', [(i, i ^ bit) for i in range(size)])]
    ppermute x2, starting transfers between devices: 1.33 us -> 4.46 us  [swap_odd(): lax.ppermute(x, 'space', [(i, (i + 1 if i % 2 else i - 1) % size) for i i...]
    pallas_call x5 -> x8, Pallas kernels: 16.9 us -> 14.8 us  [call(): pl.pallas_call(body, out_shape=out_shape, in_specs=specs, out_specs=jax.t...]
    slice x6, local copies, waits for them, and re-layouts: 1.97 us -> 0.08 us  [the longest x3 0.04 us: on_device(): got = swap(jnp.concatenate([mine, total[n:].astype(BF16)], axis=0), bit)]
    concatenate x1 -> x0, local copies, waits for them, and re-layouts: 0.83 us -> none  [on_device(): jnp.concatenate([w_in_t, b_in[:, None], jnp.zeros((units, 255 - chans), B...]
  transfers between devices with their start and end apart: 17 -> 14, of which waited for: 9 -> 10; matrix products, arithmetic and copies ran while one was open for 1% -> 0% of each run, Pallas kernels for 15% -> 17%
where the time goes in v2:
time: 56.4 us; the launch traced here: 56.2 us
  waiting for transfers between devices  28.1 us (50%)
  Pallas kernels  14.8 us (26%)
  starting transfers between devices  11.1 us (20%)
  between operations  0.99 us (2%)
  local copies, waits for them, and re-layouts  0.89 us (2%)
    ppermute x12, waiting for transfers between devices, swap(): return lax.ppermute(x, 'space', [(i, i ^ bit) for i in range(size)])  20 us
    pallas_call x8, Pallas kernels, call(): pl.pallas_call(body, out_shape=out_shape, in_specs=specs, out_specs=jax.t...  14.8 us
    ppermute x2, waiting for transfers between devices, swap_odd(): lax.ppermute(x, 'space', [(i, (i + 1 if i % 2 else i - 1) % size) for i i...  8.11 us
    ppermute x12, starting transfers between devices, swap(): return lax.ppermute(x, 'space', [(i, i ^ bit) for i in range(size)])  6.65 us
    ppermute x2, starting transfers between devices, swap_odd(): lax.ppermute(x, 'space', [(i, (i + 1 if i % 2 else i - 1) % size) for i i...  4.46 us
  transfers between devices with their start and end apart: 14, of which 10 were waited for; matrix products, arithmetic and copies ran while one was open for 0% of the time, Pallas kernels for 17%

profile of v2, /device:TPU:0, one launch (start us, length us, event | category | flops | bytes accessed | tf_op | source)
XLA Modules:
  0.0 56.2 jit_solution(657562680093623438)
XLA Ops:
  0.6 0.0 copy-start.1
  0.7 0.0 copy-start.8
  0.7 0.0 copy-start.7
  0.7 0.0 copy-start.6
  0.7 0.0 copy-start.5
  0.7 0.0 copy-start.4
  0.7 0.0 copy-start
  0.7 0.0 copy-start.2
  0.7 1.8 %pack.1 = (bf16[160,128]{1,0:T(8,128)(2,1)}, bf16[288,128]{1,0:T(8,128)(2,1)}, bf16[288,128]{1,0:T(8,128)(2,1)}) custom-call(s32[1]{0:T(128)} %bitcast.me_ref, bf16[48,192]{1,0:T(8,128)(2,1)} %wi_hbm.1, bf16[48]{0:T(256)(128)(2,1)} %b_hbm.1, bf16[48,192]{1,0:T(8,128)(2,1)} %wo_hbm.1, bf16[4,8,8,192]{3,2,1,0:T(8,128)(2,1)} %refs_0_.1), custom_call_target="tpu_custom_call" | custom-call | flops 1000000000 | tf_op jit(solution)/shard_map/pack/pallas_call | solution.py:530
  2.5 4.1 %collective-permute-start = (bf16[160,128]{1,0:T(8,128)(2,1)}, bf16[160,128]{1,0:T(8,128)(2,1)S(1)}, u32[]{:S(2)}, u32[]{:S(2)}) collective-permute-start(bf16[160,128]{1,0:T(8,128)(2,1)} %get-tuple-element.65.refs_8_), channel_id=1, source_target_pairs={{0,8},{1,9},{2,10},{3,11},{4,12},{5,13},{6,14},{7,15},{8,0},{9,1},... | collective-permute-start | bytes 122888 | tf_op jit(solution)/shard_map/ppermute | solution.py:92
  6.6 0.0 collective-permute-start.1
  6.6 0.0 copy-done.1
  6.6 0.0 copy-done.8
  6.6 0.0 copy-done.7
  6.7 0.0 copy-done.6
  6.7 0.0 copy-done.5
  6.7 0.0 copy-done.4
  6.7 0.0 copy-done
  6.7 0.0 copy-done.2
  6.7 0.0 copy-start.3
  6.7 0.8 %copy-done.3 = bf16[160,128]{1,0:T(8,128)(2,1)S(1)} copy-done((bf16[160,128]{1,0:T(8,128)(2,1)S(1)}, bf16[160,128]{1,0:T(8,128)(2,1)}, u32[]{:S(2)}) %copy-start.3) | copy-done | bytes 40984
  7.5 0.0 copy-start.9
  7.5 1.0 %prepare.1 = (bf16[160,128]{1,0:T(8,128)(2,1)S(1)}, f32[2,4,8,8,128]{4,3,2,1,0:T(8,128)S(1)}, f32[16,7,8,128]{3,2,1,0:T(8,128)S(1)}, f32[8,192]{1,0:T(8,128)S(1)...) custom-call(bf16[4,8,8,192]{3,2,1,0:T(8,128)(2,1)S(1)} %copy-done.1, ...), custom_call_target="tpu_custom_call" | custom-call | flops 1000000000 | tf_op jit(solution)/shard_map/prepare/pallas_call | solution.py:530
  8.5 0.8 %collective-permute-done = bf16[160,128]{1,0:T(8,128)(2,1)S(1)} collective-permute-done((bf16[160,128]{1,0:T(8,128)(2,1)}, bf16[160,128]{1,0:T(8,128)(2,1)S(1)}, u32[]{:S(2)}, u32[]{:S(2)}) %collective-permute-start) | collective-permute-done | bytes 40992 | tf_op jit(solution)/shard_map/ppermute | solution.py:92
  9.3 0.0 collective-permute-done.1.p_ref
  9.3 1.5 %collective-permute-start.2 = (bf16[2,160,128]{2,1,0:T(8,128)(2,1)S(1)}, bf16[2,160,128]{2,1,0:T(8,128)(2,1)S(1)}, u32[]{:S(2)}, u32[]{:S(2)}) collective-permute-start(bf16[2,160,128]{2,1,0:T(8,128)(2,1)S(1)} %pad_maximum_fusion.5), channel_id=1, source_target_pairs={{0,4},{1,5},{2,6},{3,7},{4,0},{5,1},{6,2},{7,3},{8,12},{9,13},{10,... | collective-permute-start | bytes 245768 | tf_op jit(solution)/shard_map/ppermute | solution.py:92
  10.8 0.0 copy-done.9
  10.8 1.7 %collective-permute-start.3 = (bf16[288,128]{1,0:T(8,128)(2,1)S(1)}, bf16[288,128]{1,0:T(8,128)(2,1)S(1)}, u32[]{:S(2)}, u32[]{:S(2)}) collective-permute-start(bf16[288,128]{1,0:T(8,128)(2,1)S(1)} %copy-done.9), channel_id=1, source_target_pairs={{0,15},{1,2},{2,1},{3,4},{4,3},{5,6},{6,5},{7,8},{8,7},{9,10},{10,... | collective-permute-start | bytes 221192 | tf_op jit(solution)/shard_map/ppermute | solution.py:97
  12.5 1.3 %collective-permute-done.2 = bf16[2,160,128]{2,1,0:T(8,128)(2,1)S(1)} collective-permute-done((bf16[2,160,128]{2,1,0:T(8,128)(2,1)S(1)}, bf16[2,160,128]{2,1,0:T(8,128)(2,1)S(1)}, u32[]{:S(2)}, u32[]{:S(2)}) %collective-permute-start.2) | collective-permute-done | bytes 81952 | tf_op jit(solution)/shard_map/ppermute | solution.py:92
  13.8 3.6 %collective-permute-done.3.q_ref = bf16[288,128]{1,0:T(8,128)(2,1)S(1)} collective-permute-done((bf16[288,128]{1,0:T(8,128)(2,1)S(1)}, bf16[288,128]{1,0:T(8,128)(2,1)S(1)}, u32[]{:S(2)}, u32[]{:S(2)}) %collective-permute-start.3) | collective-permute-done | bytes 73760 | tf_op jit(solution)/shard_map/ppermute | solution.py:97
  17.5 0.0 collective-permute-start.4
  17.5 2.7 %forward_stencil.1 = (bf16[256,256]{1,0:T(8,128)(2,1)S(1)}, f32[256,256]{1,0:T(8,128)S(1)}, f32[7,15,8,8,128]{4,3,2,1,0:T(8,128)S(1)}) custom-call(s32[1]{0:T(128)} %bitcast.me_ref, f32[2,4,8,8,128]{4,3,2,1,0:T(8,128)S(1)} %get-tuple-element.78.own_ref, bf16[288,128]{1,0:T(8,128)(2,1)S(1)} %collective-permute-done.1.p_ref, ...), custom_call_target="tpu_custom_call" | custom-call | flops 2500000000 | tf_op jit(solution)/shard_map/forward_stencil/pallas_call | solution.py:530
  20.1 2.6 %collective-permute-done.4 = bf16[4,160,128]{2,1,0:T(8,128)(2,1)S(1)} collective-permute-done((bf16[4,160,128]{2,1,0:T(8,128)(2,1)S(1)}, bf16[4,160,128]{2,1,0:T(8,128)(2,1)S(1)}, u32[]{:S(2)}, u32[]{:S(2)}) %collective-permute-start.4) | collective-permute-done | bytes 163872 | tf_op jit(solution)/shard_map/ppermute | solution.py:92
  22.8 0.1 collective-permute-start.5
  22.9 1.6 %collective-permute-done.5.g1_ref = bf16[8,160,128]{2,1,0:T(8,128)(2,1)S(1)} collective-permute-done((bf16[8,160,128]{2,1,0:T(8,128)(2,1)S(1)}, bf16[8,160,128]{2,1,0:T(8,128)(2,1)S(1)}, u32[]{:S(2)}, u32[]{:S(2)}) %collective-permute-start.5) | collective-permute-done | bytes 327712 | tf_op jit(solution)/shard_map/ppermute | solution.py:92
  24.5 2.8 %pointwise.1 = (bf16[4,8,8,192]{3,2,1,0:T(8,128)(2,1)}, bf16[4,8,8,192]{3,2,1,0:T(8,128)(2,1)S(1)}, bf16[288,128]{1,0:T(8,128)(2,1)S(1)}, bf16[288,128]{1,0:T(8,...) custom-call(s32[1]{0:T(128)} %bitcast.me_ref, ...), custom_call_target="tpu_custom_call" | custom-call | flops 2500000000 | tf_op jit(solution)/shard_map/pointwise/pallas_call | solution.py:530
  27.3 0.1 collective-permute-start.7
  27.5 2.2 %kernel_gradient.1 = (f32[320,128]{1,0:T(8,128)S(1)}, bf16[320,128]{1,0:T(8,128)(2,1)S(1)}) custom-call(s32[1]{0:T(128)} %bitcast.me_ref, f32[7,15,8,8,128]{4,3,2,1,0:T(8,128)S(1)} %get-tuple-element.93.s_ref, bf16[4,8,8,192]{3,2,1,0:T(8,128)(2,1)S(1)} %get-tuple-element.94.g_ref, f32[8,256]{1,0:T(8,128)S(1)} %get-tuple-element.95.small_ref), custom_call_target="tpu_custom_call" | custom-call | flops 2000000000 | tf_op jit(solution)/shard_map/kernel_gradient/pallas_call | solution.py:530
  29.7 0.4 collective-permute-start.6
  30.2 0.9 %collective-permute-done.6 = bf16[320,128]{1,0:T(8,128)(2,1)S(1)} collective-permute-done((bf16[320,128]{1,0:T(8,128)(2,1)S(1)}, bf16[320,128]{1,0:T(8,128)(2,1)S(1)}, u32[]{:S(2)}, u32[]{:S(2)}) %collective-permute-start.6) | collective-permute-done | bytes 81952 | tf_op jit(solution)/shard_map/ppermute | solution.py:92
  31.1 0.0 collective-permute-done.7
  31.1 0.1 convert_add_fusion
  31.2 0.1 collective-permute-start.8
  31.3 8.2 %collective-permute-done.8 = bf16[960,128]{1,0:T(8,128)(2,1)S(1)} collective-permute-done((bf16[960,128]{1,0:T(8,128)(2,1)S(1)}, bf16[960,128]{1,0:T(8,128)(2,1)S(1)}, u32[]{:S(2)}, u32[]{:S(2)}) %collective-permute-start.8) | collective-permute-done | bytes 245792 | tf_op jit(solution)/shard_map/ppermute | solution.py:92
  39.6 0.1 collective-permute-start.9
  39.7 0.1 collective-permute-start.10
  39.8 2.8 %collective-permute-start.11 = (bf16[288,128]{1,0:T(8,128)(2,1)S(1)}, bf16[288,128]{1,0:T(8,128)(2,1)S(1)}, u32[]{:S(2)}, u32[]{:S(2)}) collective-permute-start(bf16[288,128]{1,0:T(8,128)(2,1)S(1)} %get-tuple-element.104), channel_id=1, source_target_pairs={{0,15},{1,2},{2,1},{3,4},{4,3},{5,6},{6,5},{7,8},{8,7},{9,10},{10,... | collective-permute-start | bytes 221192 | tf_op jit(solution)/shard_map/ppermute | solution.py:97
  42.6 0.0 collective-permute-done.10.p_ref
  42.6 4.5 %collective-permute-done.11.q_ref = bf16[288,128]{1,0:T(8,128)(2,1)S(1)} collective-permute-done((bf16[288,128]{1,0:T(8,128)(2,1)S(1)}, bf16[288,128]{1,0:T(8,128)(2,1)S(1)}, u32[]{:S(2)}, u32[]{:S(2)}) %collective-permute-start.11) | collective-permute-done | bytes 73760 | tf_op jit(solution)/shard_map/ppermute | solution.py:97
  47.1 0.0 collective-permute-done.9
  47.1 0.1 collective-permute-start.12
  47.2 2.7 %backward_stencil.1 = bf16[4,8,8,192]{3,2,1,0:T(8,128)(2,1)} custom-call(s32[1]{0:T(128)} %bitcast.me_ref, bf16[4,8,8,192]{3,2,1,0:T(8,128)(2,1)S(1)} %get-tuple-element.94.g_ref, bf16[288,128]{1,0:T(8,128)(2,1)S(1)} %collective-permute-done.10.p_ref, bf16[288,128]{1,0:T(8,128)(2,1)S(1)} %collective-permute-done.11.q_ref, ...), custom_call_target="tpu_custom_call" | custom-call | flops 2500000000 | tf_op jit(solution)/shard_map/backward_stencil/pallas_call | solution.py:530
  50.0 4.0 %collective-permute-done.12 = bf16[480,128]{1,0:T(8,128)(2,1)S(1)} collective-permute-done((bf16[480,128]{1,0:T(8,128)(2,1)S(1)}, bf16[480,128]{1,0:T(8,128)(2,1)S(1)}, u32[]{:S(2)}, u32[]{:S(2)}) %collective-permute-start.12) | collective-permute-done | bytes 122912 | tf_op jit(solution)/shard_map/ppermute | solution.py:92
  54.0 0.1 collective-permute-start.13
  54.1 0.7 %finish.1 = (f32[48,192]{1,0:T(8,128)}, f32[1,48]{1,0:T(1,128)}, f32[48,192]{1,0:T(8,128)}) custom-call(f32[160,128]{1,0:T(8,128)S(1)} %slice.63.a_ref, bf16[160,128]{1,0:T(8,128)(2,1)S(1)} %slice.55.b_ref), custom_call_target="tpu_custom_call" | custom-call | flops 700000000 | tf_op jit(solution)/shard_map/finish/pallas_call | solution.py:530
  54.8 0.5 collective-permute-done.13.other_ref
  55.3 0.9 %unpack.1 = (f32[7,7,7,192]{3,2,1,0:T(8,128)}, f32[1,192]{1,0:T(1,128)}, f32[1,192]{1,0:T(1,128)}, f32[1,192]{1,0:T(1,128)}, f32[1,192]{1,0:T(1,128)}, /*index=5*/f32[1,192]{1,0:T(1,128)}) custom-call(s32[1]{0:T(128)} %bitcast.me_ref, bf16[320,128]{1,0:T(8,128)(2,1)S(1)} %add_convert_fusion.mine_ref, bf16[320,128]{1,0:T(8,128)(2,1)S(1)} %collective-permute-done.13.other_ref), custom_call_target="tpu_custom_call" | custom-call | flops 900000000 | tf_op jit(solution)/shard_map/unpack/pallas_call | solution.py:530
  (17 shorter events, 0.3 us)
Async XLA Ops:
  0.6 6.0 %copy-start.1 = (bf16[4,8,8,192]{3,2,1,0:T(8,128)(2,1)S(1)}, bf16[4,8,8,192]{3,2,1,0:T(8,128)(2,1)}, u32[]{:S(2)}) copy-start(bf16[4,8,8,192]{3,2,1,0:T(8,128)(2,1)} %refs_0_.1) | copy-start | bytes 294916
  0.7 6.0 %copy-start.8 = (f32[192]{0:T(256)S(1)}, f32[192]{0:T(256)}, u32[]{:S(2)}) copy-start(f32[192]{0:T(256)} %refs_7_.1) | copy-start | bytes 2308
  0.7 6.0 %copy-start.7 = (f32[192]{0:T(256)S(1)}, f32[192]{0:T(256)}, u32[]{:S(2)}) copy-start(f32[192]{0:T(256)} %refs_6_.1) | copy-start | bytes 2308
  0.7 6.0 %copy-start.6 = (f32[192]{0:T(256)S(1)}, f32[192]{0:T(256)}, u32[]{:S(2)}) copy-start(f32[192]{0:T(256)} %refs_5_.1) | copy-start | bytes 2308
  0.7 6.0 %copy-start.5 = (f32[192]{0:T(256)S(1)}, f32[192]{0:T(256)}, u32[]{:S(2)}) copy-start(f32[192]{0:T(256)} %refs_4_.1) | copy-start | bytes 2308
  0.7 6.0 %copy-start.4 = (f32[192]{0:T(256)S(1)}, f32[192]{0:T(256)}, u32[]{:S(2)}) copy-start(f32[192]{0:T(256)} %refs_3_.1) | copy-start | bytes 2308
  0.7 6.0 %copy-start = (f32[7,7,7,192]{3,2,1,0:T(8,128)S(1)}, f32[7,7,7,192]{3,2,1,0:T(8,128)}, u32[]{:S(2)}) copy-start(f32[7,7,7,192]{3,2,1,0:T(8,128)} %refs_2_.1) | copy-start | bytes 790276
  0.7 6.0 %copy-start.2 = (bf16[4,8,8,192]{3,2,1,0:T(8,128)(2,1)S(1)}, bf16[4,8,8,192]{3,2,1,0:T(8,128)(2,1)}, u32[]{:S(2)}) copy-start(bf16[4,8,8,192]{3,2,1,0:T(8,128)(2,1)} %refs_1_.1) | copy-start | bytes 294916
  2.5 6.7 %collective-permute-start = (bf16[160,128]{1,0:T(8,128)(2,1)}, bf16[160,128]{1,0:T(8,128)(2,1)S(1)}, u32[]{:S(2)}, u32[]{:S(2)}) collective-permute-start(bf16[160,128]{1,0:T(8,128)(2,1)} %get-tuple-element.65.refs_8_), channel_id=1, source_target_pairs={{0,8},{1,9},{2,10},{3,11},{4,12},{5,13},{6,14},{7,15},{8,0},{9,1},... | collective-permute-start | bytes 122888 | tf_op jit(solution)/shard_map/ppermute | solution.py:92
  6.6 2.6 %collective-permute-start.1 = (bf16[288,128]{1,0:T(8,128)(2,1)}, bf16[288,128]{1,0:T(8,128)(2,1)S(1)}, u32[]{:S(2)}, u32[]{:S(2)}) collective-permute-start(bf16[288,128]{1,0:T(8,128)(2,1)} %get-tuple-element.66), channel_id=1, source_target_pairs={{0,1},{1,0},{2,3},{3,2},{4,5},{5,4},{6,7},{7,6},{8,9},{9,8},{10,11... | collective-permute-start | bytes 221192 | tf_op jit(solution)/shard_map/ppermute | solution.py:92
  6.7 0.8 %copy-start.3 = (bf16[160,128]{1,0:T(8,128)(2,1)S(1)}, bf16[160,128]{1,0:T(8,128)(2,1)}, u32[]{:S(2)}) copy-start(bf16[160,128]{1,0:T(8,128)(2,1)} %get-tuple-element.65.refs_8_) | copy-start | bytes 122884
  7.5 3.3 %copy-start.9 = (bf16[288,128]{1,0:T(8,128)(2,1)S(1)}, bf16[288,128]{1,0:T(8,128)(2,1)}, u32[]{:S(2)}) copy-start(bf16[288,128]{1,0:T(8,128)(2,1)} %get-tuple-element.76) | copy-start | bytes 221188
  9.3 4.5 %collective-permute-start.2 = (bf16[2,160,128]{2,1,0:T(8,128)(2,1)S(1)}, bf16[2,160,128]{2,1,0:T(8,128)(2,1)S(1)}, u32[]{:S(2)}, u32[]{:S(2)}) collective-permute-start(bf16[2,160,128]{2,1,0:T(8,128)(2,1)S(1)} %pad_maximum_fusion.5), channel_id=1, source_target_pairs={{0,4},{1,5},{2,6},{3,7},{4,0},{5,1},{6,2},{7,3},{8,12},{9,13},{10,... | collective-permute-start | bytes 245768 | tf_op jit(solution)/shard_map/ppermute | solution.py:92
  10.8 6.6 %collective-permute-start.3 = (bf16[288,128]{1,0:T(8,128)(2,1)S(1)}, bf16[288,128]{1,0:T(8,128)(2,1)S(1)}, u32[]{:S(2)}, u32[]{:S(2)}) collective-permute-start(bf16[288,128]{1,0:T(8,128)(2,1)S(1)} %copy-done.9), channel_id=1, source_target_pairs={{0,15},{1,2},{2,1},{3,4},{4,3},{5,6},{6,5},{7,8},{8,7},{9,10},{10,... | collective-permute-start | bytes 221192 | tf_op jit(solution)/shard_map/ppermute | solution.py:97
  17.5 5.3 %collective-permute-start.4 = (bf16[4,160,128]{2,1,0:T(8,128)(2,1)S(1)}, bf16[4,160,128]{2,1,0:T(8,128)(2,1)S(1)}, u32[]{:S(2)}, u32[]{:S(2)}) collective-permute-start(bf16[4,160,128]{2,1,0:T(8,128)(2,1)S(1)} %pad_maximum_fusion.2), channel_id=1, source_target_pairs={{0,2},{1,3},{2,0},{3,1},{4,6},{5,7},{6,4},{7,5},{8,10},{9,11},{10,... | collective-permute-start | bytes 491528 | tf_op jit(solution)/shard_map/ppermute | solution.py:92
  22.8 1.7 %collective-permute-start.5 = (bf16[8,160,128]{2,1,0:T(8,128)(2,1)S(1)}, bf16[8,160,128]{2,1,0:T(8,128)(2,1)S(1)}, u32[]{:S(2)}, u32[]{:S(2)}) collective-permute-start(bf16[8,160,128]{2,1,0:T(8,128)(2,1)S(1)} %pad_maximum_fusion.g0_ref), channel_id=1, source_target_pairs={{0,1},{1,0},{2,3},{3,2},{4,5},{5,4},{6,7},{7,6},{8,9},{9,8},{10,11... | collective-permute-start | bytes 983048 | tf_op jit(solution)/shard_map/ppermute | solution.py:92
  27.3 3.8 %collective-permute-start.7 = (bf16[8,160,128]{2,1,0:T(8,128)(2,1)S(1)}, bf16[8,160,128]{2,1,0:T(8,128)(2,1)S(1)}, u32[]{:S(2)}, u32[]{:S(2)}) collective-permute-start(bf16[8,160,128]{2,1,0:T(8,128)(2,1)S(1)} %get-tuple-element.102), channel_id=1, source_target_pairs={{0,1},{1,0},{2,3},{3,2},{4,5},{5,4},{6,7},{7,6},{8,9},{9,8},{10,11... | collective-permute-start | bytes 983048 | tf_op jit(solution)/shard_map/ppermute | solution.py:92
  29.7 1.4 %collective-permute-start.6 = (bf16[320,128]{1,0:T(8,128)(2,1)S(1)}, bf16[320,128]{1,0:T(8,128)(2,1)S(1)}, u32[]{:S(2)}, u32[]{:S(2)}) collective-permute-start(bf16[320,128]{1,0:T(8,128)(2,1)S(1)} %get-tuple-element.97), channel_id=1, source_target_pairs={{0,1},{1,0},{2,3},{3,2},{4,5},{5,4},{6,7},{7,6},{8,9},{9,8},{10,11... | collective-permute-start | bytes 245768 | tf_op jit(solution)/shard_map/ppermute | solution.py:92
  31.2 8.3 %collective-permute-start.8 = (bf16[960,128]{1,0:T(8,128)(2,1)S(1)}, bf16[960,128]{1,0:T(8,128)(2,1)S(1)}, u32[]{:S(2)}, u32[]{:S(2)}) collective-permute-start(bf16[960,128]{1,0:T(8,128)(2,1)S(1)} %pad_maximum_fusion.1), channel_id=1, source_target_pairs={{0,2},{1,3},{2,0},{3,1},{4,6},{5,7},{6,4},{7,5},{8,10},{9,11},{10,... | collective-permute-start | bytes 737288 | tf_op jit(solution)/shard_map/ppermute | solution.py:92
  39.6 7.4 %collective-permute-start.9 = (bf16[640,128]{1,0:T(8,128)(2,1)S(1)}, bf16[640,128]{1,0:T(8,128)(2,1)S(1)}, u32[]{:S(2)}, u32[]{:S(2)}) collective-permute-start(bf16[640,128]{1,0:T(8,128)(2,1)S(1)} %pad_maximum_fusion.3), channel_id=1, source_target_pairs={{0,4},{1,5},{2,6},{3,7},{4,0},{5,1},{6,2},{7,3},{8,12},{9,13},{10,... | collective-permute-start | bytes 491528 | tf_op jit(solution)/shard_map/ppermute | solution.py:92
  39.7 2.9 %collective-permute-start.10 = (bf16[288,128]{1,0:T(8,128)(2,1)S(1)}, bf16[288,128]{1,0:T(8,128)(2,1)S(1)}, u32[]{:S(2)}, u32[]{:S(2)}) collective-permute-start(bf16[288,128]{1,0:T(8,128)(2,1)S(1)} %get-tuple-element.103), channel_id=1, source_target_pairs={{0,1},{1,0},{2,3},{3,2},{4,5},{5,4},{6,7},{7,6},{8,9},{9,8},{10,11... | collective-permute-start | bytes 221192 | tf_op jit(solution)/shard_map/ppermute | solution.py:92
  39.8 7.3 %collective-permute-start.11 = (bf16[288,128]{1,0:T(8,128)(2,1)S(1)}, bf16[288,128]{1,0:T(8,128)(2,1)S(1)}, u32[]{:S(2)}, u32[]{:S(2)}) collective-permute-start(bf16[288,128]{1,0:T(8,128)(2,1)S(1)} %get-tuple-element.104), channel_id=1, source_target_pairs={{0,15},{1,2},{2,1},{3,4},{4,3},{5,6},{6,5},{7,8},{8,7},{9,10},{10,... | collective-permute-start | bytes 221192 | tf_op jit(solution)/shard_map/ppermute | solution.py:97
  47.1 6.8 %collective-permute-start.12 = (bf16[480,128]{1,0:T(8,128)(2,1)S(1)}, bf16[480,128]{1,0:T(8,128)(2,1)S(1)}, u32[]{:S(2)}, u32[]{:S(2)}) collective-permute-start(bf16[480,128]{1,0:T(8,128)(2,1)S(1)} %pad_maximum_fusion.4), channel_id=1, source_target_pairs={{0,8},{1,9},{2,10},{3,11},{4,12},{5,13},{6,14},{7,15},{8,0},{9,1},... | collective-permute-start | bytes 368648 | tf_op jit(solution)/shard_map/ppermute | solution.py:92
  54.0 1.3 %collective-permute-start.13 = (bf16[320,128]{1,0:T(8,128)(2,1)S(1)}, bf16[320,128]{1,0:T(8,128)(2,1)S(1)}, u32[]{:S(2)}, u32[]{:S(2)}) collective-permute-start(bf16[320,128]{1,0:T(8,128)(2,1)S(1)} %add_convert_fusion.mine_ref), channel_id=1, source_target_pairs={{0,1},{1,0},{2,3},{3,2},{4,5},{5,4},{6,7},{7,6},{8,9},{9,8},{10,11... | collective-permute-start | bytes 245768 | tf_op jit(solution)/shard_map/ppermute | solution.py:92

commit v3 on v2

--- a/solution.py
+++ b/solution.py
@@ -309,7 +309,7 @@
     unit_ref[:, chans:256] = jnp.broadcast_to(inverse, (rows, 256 - chans))
 
 
-def pointwise_kernel(me_ref, g0_ref, g1_ref, na_ref, unit_ref, xf_ref, cf_ref, db_ref, vec_ref, out_ref, dm_ref, core_ref, far_ref, w0_ref, w1_ref, small_ref, wi_ref, wo_ref, di_ref, do_ref, m_ref):
+def pointwise_kernel(me_ref, g0_ref, g1_ref, na_ref, unit_ref, xf_ref, cf_ref, db_ref, vec_ref, branch_ref, dm_ref, core_ref, far_ref, w0_ref, w1_ref, small_ref, wi_ref, wo_ref, di_ref, do_ref, m_ref):
     rows, chans = xf_ref.shape
     normed = na_ref[...]
     d_b = db_ref[...]
@@ -358,7 +358,7 @@
             line = jnp.where(first_row, jnp.broadcast_to(line[0:1], (16, LANE)), 0.0)
             w_ref[i, 3 * high : 3 * high + 16] = line.astype(w_ref.dtype)
     branch = branch[:, 0:chans] + vec_ref[3:4]
-    out_ref[...] = (xf_ref[...] + gamma * branch).reshape(out_ref.shape).astype(BF16)
+    branch_ref[...] = gamma * branch
     d_normed = d_normed[:, 0:chans]
     unit = unit_ref[:, 0:chans]
     inverse = unit_ref[:, chans : chans + 1]
@@ -397,7 +397,19 @@
     return v[0]
 
 
-HALF = 320
+HALF = 272
+
+
+def block(g):
+    return 64 * (g // 7) + 8 * (g % 7)
+
+
+def main_at(g):
+    return (0, 7 * g) if g < 38 else (1, 7 * (g - 38))
+
+
+def rest_at(g):
+    return 77 + 7 * (g % 25), 64 * (g // 25)
 
 
 def grad_kernel(me_ref, s_ref, g_ref, small_ref, keep_ref, send_ref, z_ref, t_ref, o_ref, wa_ref, wb_ref, w_ref):
@@ -441,19 +453,20 @@
             one = jnp.where(low_lanes((8, LANE)), rest[a], pltpu.roll(rest[a], 64, axis=1))
             wb_ref[pl.ds(a * 64 + e, 8, stride=8), :] = one
 
-    low = lax.broadcasted_iota(jnp.int32, (56, LANE), 1) < 64
-    for a in range(5):
-        w_ref[0, 56 * a : 56 * a + 56] = wa_ref[64 * a : 64 * a + 56]
-    w_ref[0, 280:288] = small_ref[:, 0:LANE]
-    w_ref[0, 288:HALF] = jnp.zeros((HALF - 288, LANE), F32)
-    for a in range(5, 7):
-        w_ref[1, 56 * (a - 5) : 56 * (a - 5) + 56] = wa_ref[64 * a : 64 * a + 56]
-    for a in range(3):
-        w_ref[1, 112 + 56 * a : 168 + 56 * a] = jnp.where(
-            low, wb_ref[64 * a : 64 * a + 56], wb_ref[64 * (a + 4) : 64 * (a + 4) + 56]
-        )
-    w_ref[1, 280:312] = jnp.where(low[0:32], wb_ref[192:224], wb_ref[224:256])
-    w_ref[1, 312:320] = small_ref[:, LANE:256]
+    w_ref[0, HALF - 16 : HALF] = jnp.zeros((16, LANE), F32)
+    w_ref[1, HALF - 16 : HALF] = jnp.zeros((16, LANE), F32)
+    low = low_lanes((8, LANE))[0:7]
+    for g in range(49):
+        half, row = main_at(g)
+        w_ref[half, row : row + 7] = wa_ref[block(g) : block(g) + 7]
+        row, lane = rest_at(g)
+        if lane == 0:
+            pair = min(g + 25, 48)
+            w_ref[1, row : row + 7] = jnp.where(
+                low, wb_ref[block(g) : block(g) + 7], wb_ref[block(pair) : block(pair) + 7]
+            )
+    w_ref[0, 266:271] = small_ref[0:5, 0:LANE]
+    w_ref[1, 252:257] = small_ref[0:5, LANE:256]
     keep_ref[...] = w_ref[odd]
     send_ref[...] = w_ref[1 - odd].astype(BF16)
 
@@ -462,20 +475,14 @@
     odd, small_refs, w_ref = lax.rem(me_ref[0], 2), refs[:5], refs[5]
     w_ref[odd] = mine_ref[...].astype(F32) * scale
     w_ref[1 - odd] = other_ref[...].astype(F32) * scale
-    for a in range(7):
-        for b in range(7):
-            row = 56 * a + 8 * b if a < 5 else 56 * (a - 5) + 8 * b
-            main = w_ref[0 if a < 5 else 1, row : row + 7]
-            if a == 3:
-                at, lane = 280 + 8 * (b % 4), 64 * (b // 4)
-            else:
-                at, lane = 112 + 56 * (a % 4) + 8 * b, 64 * (a // 4)
-            rest = w_ref[1, at : at + 7]
-            dk_ref[a, b, :, 0:LANE] = main
-            dk_ref[a, b, :, LANE : LANE + 64] = rest[:, lane : lane + 64]
+    for g in range(49):
+        half, row = main_at(g)
+        dk_ref[g // 7, g % 7, :, 0:LANE] = w_ref[half, row : row + 7]
+        row, lane = rest_at(g)
+        dk_ref[g // 7, g % 7, :, LANE : LANE + 64] = w_ref[1, row : row + 7][:, lane : lane + 64]
     for i, ref in enumerate(small_refs):
-        ref[:, 0:LANE] = w_ref[0, 280 + i : 281 + i]
-        ref[:, LANE : LANE + 64] = w_ref[1, 312 + i : 313 + i, 0:64]
+        ref[:, 0:LANE] = w_ref[0, 266 + i : 267 + i]
+        ref[:, LANE : LANE + 64] = w_ref[1, 252 + i : 253 + i, 0:64]
 
 
 def finish_kernel(scale, a_ref, b_ref, wi_ref, bi_ref, wo_ref):
@@ -490,10 +497,11 @@
     bi_ref[...] = total[3 * high : 3 * high + 1, 0:units]
 
 
-def back_kernel(last, me_ref, g_ref, p_ref, q_ref, t_ref, c_ref, dx_ref, z_ref, s_ref, u_ref):
+def back_kernel(last, me_ref, g_ref, p_ref, q_ref, t_ref, c_ref, xf_ref, branch_ref, dx_ref, out_ref, z_ref, s_ref, u_ref):
     fill_rim(last, me_ref, p_ref, q_ref, z_ref)
     for i in range(4):
         split(g_ref[i].astype(F32), z_ref, 3 + i)
+    out_ref[...] = (xf_ref[...] + branch_ref[...]).reshape(out_ref.shape).astype(BF16)
     stencil(z_ref, t_ref, s_ref, u_ref, True)
     main, rest = from_points(4, lambda u: u_ref[u], 6)
     for i in range(4):
@@ -523,7 +531,7 @@
     rows = size_x * size_y * size_z
     units = w_in_t.shape[0]
     bits = [1 << i for i in range(devices.bit_length() - 1)]
-    order = bits
+    order, sums_order = bits, [bits[0], bits[-1], bits[1]] + bits[2:-1]
     me = lax.axis_index("space").astype(jnp.int32).reshape(1)
     def call(body, name, us, mib, out_shape, operands, scratch=(), spec=VMEM):
         specs = [SMEM if x is me else spec for x in operands]
@@ -583,10 +591,13 @@
     weights, x_core, prepared = lax.optimization_barrier((weights, x_core, prepared))
     piece, own, taps, vecs, x_f32, cot_f32, d_branch = prepared
     weights = jnp.stack([piece, weights])
-    for bit in order[-2:1:-1]:
+    for bit in order[-2:2:-1]:
         weights = jnp.concatenate([weights, swap(weights, bit)], axis=0)
-    weights, x_far = lax.optimization_barrier((weights, x_far))
-    weights = jnp.concatenate([weights, swap(weights, order[1])], axis=0)
+    over_z, over_x = swap(weights, order[2]), swap(weights, order[1])
+    over_z, over_x, x_far = lax.optimization_barrier((over_z, over_x, x_far))
+    n = over_z.shape[0] // 2
+    corner = swap(over_z[:n], order[1]), swap(over_x[n:], order[2])
+    weights = jnp.concatenate([weights, over_z, over_x, *corner], axis=0)
     forward = call(
         functools.partial(forward_kernel, devices - 1),
         "forward_stencil",
@@ -601,13 +612,13 @@
     weights_other = swap(weights, 1)
 
     pieces = weights.shape[0]
-    output, d_mixed, to_core, to_far, grad_keep, grad_send, small = call(
+    branch, d_mixed, to_core, to_far, grad_keep, grad_send, small = call(
         pointwise_kernel,
         "pointwise",
         2.5,
         16,
         (
-            struct(features.shape, BF16),
+            cells,
             struct(features.shape, BF16),
             rim,
             rim,
@@ -638,28 +649,30 @@
     )
 
     total = (grad_keep + swap(grad_send, 1).astype(F32)).reshape(pieces * lines, LANE)
+    send, to_core, to_far = lax.optimization_barrier((send, to_core, to_far))
     sums = keep + swap(send, 1).astype(F32)
-    sums, to_core, to_far = lax.optimization_barrier((sums, to_core, to_far))
     g_core, g_far = swap(to_core, 1), swap_odd(to_far)
-    for step, bit in enumerate(order[1:]):
+    for step, (bit, sums_bit) in enumerate(zip(order[1:], sums_order[1:])):
         n = total.shape[0] // 2
         mine, kept = sums.astype(BF16), total[:n]
-        got = swap(jnp.concatenate([mine, total[n:].astype(BF16)], axis=0), bit)
+        theirs = swap(mine, sums_bit)
+        got = swap(total[n:].astype(BF16), bit)
+        if step == 0:
+            theirs, g_core, g_far = lax.optimization_barrier((theirs, g_core, g_far))
         if step == len(order) - 3:
-            got, g_core, g_far = lax.optimization_barrier((got, g_core, g_far))
-            d_x = call(
+            d_x, output = call(
                 functools.partial(back_kernel, devices - 1),
                 "backward_stencil",
                 2.5,
                 10,
-                struct(features.shape, BF16),
-                (me, d_mixed, g_core, g_far, taps, cot_f32),
+                (struct(features.shape, BF16),) * 2,
+                (me, d_mixed, g_core, g_far, taps, cot_f32, x_f32, branch),
                 [z_scratch, pltpu.VMEM(shifts, F32), u_scratch],
             )
-        if step == len(order) - 2:
-            got, d_x = lax.optimization_barrier((got, d_x))
-        sums = mine.astype(F32) + got[:HALF].astype(F32)
-        got = got[HALF:]
+            theirs, d_x, output = lax.optimization_barrier((theirs, d_x, output))
+        if step < len(order) - 2:
+            theirs, got = lax.optimization_barrier((theirs, got))
+        sums = mine.astype(F32) + theirs.astype(F32)
         total = kept + got.astype(F32)
     mine = sums.astype(BF16)
     other = swap(mine, 1)

time: 56.4 us -> 50.8 us (0.901)
  waiting for transfers between devices: 28.1 us -> 13.5 us
  starting transfers between devices: 11.1 us -> 20.7 us
  Pallas kernels: 14.8 us -> 14.2 us
    ppermute x12 -> x17, starting transfers between devices: 6.65 us -> 15.1 us  [swap(): return lax.ppermute(x, 'space', [(i, i ^ bit) for i in range(size)])]
    ppermute x12 -> x17, waiting for transfers between devices: 20 us -> 11.6 us  [swap(): return lax.ppermute(x, 'space', [(i, i ^ bit) for i in range(size)])]
    ppermute x2, waiting for transfers between devices: 8.11 us -> 1.93 us  [swap_odd(): lax.ppermute(x, 'space', [(i, (i + 1 if i % 2 else i - 1) % size) for i i...]
    ppermute x2, starting transfers between devices: 4.46 us -> 5.57 us  [swap_odd(): lax.ppermute(x, 'space', [(i, (i + 1 if i % 2 else i - 1) % size) for i i...]
    pallas_call x8, Pallas kernels: 14.8 us -> 14.2 us  [call(): pl.pallas_call(body, out_shape=out_shape, in_specs=specs, out_specs=jax.t...]
  transfers between devices with their start and end apart: 14 -> 19, of which waited for: 10 -> 11; matrix products, arithmetic and copies ran while one was open for 0% -> 1% of each run, Pallas kernels for 17% -> 18%
where the time goes in v3:
time: 50.8 us; the launch traced here: 50.6 us
  starting transfers between devices  20.7 us (41%)
  Pallas kernels  14.2 us (28%)
  waiting for transfers between devices  13.5 us (27%)
  between operations  0.96 us (2%)
  local copies, waits for them, and re-layouts  0.95 us (2%)
    ppermute x17, starting transfers between devices, swap(): return lax.ppermute(x, 'space', [(i, i ^ bit) for i in range(size)])  15.1 us
    pallas_call x8, Pallas kernels, call(): pl.pallas_call(body, out_shape=out_shape, in_specs=specs, out_specs=jax.t...  14.2 us
    ppermute x17, waiting for transfers between devices, swap(): return lax.ppermute(x, 'space', [(i, i ^ bit) for i in range(size)])  11.6 us
    ppermute x2, starting transfers between devices, swap_odd(): lax.ppermute(x, 'space', [(i, (i + 1 if i % 2 else i - 1) % size) for i i...  5.57 us
    ppermute x2, waiting for transfers between devices, swap_odd(): lax.ppermute(x, 'space', [(i, (i + 1 if i % 2 else i - 1) % size) for i i...  1.93 us
  transfers between devices with their start and end apart: 19, of which 11 were waited for; matrix products, arithmetic and copies ran while one was open for 1% of the time, Pallas kernels for 18%

profile of v3, /device:TPU:0, one launch (start us, length us, event | category | flops | bytes accessed | tf_op | source)
XLA Modules:
  0.0 50.6 jit_solution(3338066018528424950)
XLA Ops:
  0.6 0.0 copy-start.1
  0.7 0.0 copy-start.8
  0.7 0.0 copy-start.7
  0.7 0.0 copy-start.6
  0.7 0.0 copy-start.5
  0.7 0.0 copy-start.4
  0.7 0.0 copy-start
  0.7 0.0 copy-start.2
  0.7 1.8 %pack.1 = (bf16[160,128]{1,0:T(8,128)(2,1)}, bf16[288,128]{1,0:T(8,128)(2,1)}, bf16[288,128]{1,0:T(8,128)(2,1)}) custom-call(s32[1]{0:T(128)} %bitcast.me_ref, bf16[48,192]{1,0:T(8,128)(2,1)} %wi_hbm.1, bf16[48]{0:T(256)(128)(2,1)} %b_hbm.1, bf16[48,192]{1,0:T(8,128)(2,1)} %wo_hbm.1, bf16[4,8,8,192]{3,2,1,0:T(8,128)(2,1)} %refs_0_.1), custom_call_target="tpu_custom_call" | custom-call | flops 1000000000 | tf_op jit(solution)/shard_map/pack/pallas_call | solution.py:538
  2.5 4.1 %collective-permute-start = (bf16[160,128]{1,0:T(8,128)(2,1)}, bf16[160,128]{1,0:T(8,128)(2,1)S(1)}, u32[]{:S(2)}, u32[]{:S(2)}) collective-permute-start(bf16[160,128]{1,0:T(8,128)(2,1)} %get-tuple-element.73.refs_8_), channel_id=1, source_target_pairs={{0,8},{1,9},{2,10},{3,11},{4,12},{5,13},{6,14},{7,15},{8,0},{9,1},... | collective-permute-start | bytes 122888 | tf_op jit(solution)/shard_map/ppermute | solution.py:92
  6.6 0.0 collective-permute-start.1
  6.6 2.4 %collective-permute-start.4 = (bf16[288,128]{1,0:T(8,128)(2,1)}, bf16[288,128]{1,0:T(8,128)(2,1)S(1)}, u32[]{:S(2)}, u32[]{:S(2)}) collective-permute-start(bf16[288,128]{1,0:T(8,128)(2,1)} %get-tuple-element.84), channel_id=1, source_target_pairs={{0,15},{1,2},{2,1},{3,4},{4,3},{5,6},{6,5},{7,8},{8,7},{9,10},{10,... | collective-permute-start | bytes 221192 | tf_op jit(solution)/shard_map/ppermute | solution.py:97
  9.0 0.0 copy-done.1
  9.0 0.0 copy-done.8
  9.0 0.0 copy-done.7
  9.0 0.0 copy-done.5
  9.0 0.0 copy-done.4
  9.1 0.0 copy-done
  9.1 0.0 copy-done.2
  9.1 0.0 copy-start.3
  9.1 0.8 %copy-done.3 = bf16[160,128]{1,0:T(8,128)(2,1)S(1)} copy-done((bf16[160,128]{1,0:T(8,128)(2,1)S(1)}, bf16[160,128]{1,0:T(8,128)(2,1)}, u32[]{:S(2)}) %copy-start.3) | copy-done | bytes 40984
  9.9 1.0 %prepare.1 = (bf16[160,128]{1,0:T(8,128)(2,1)S(1)}, f32[2,4,8,8,128]{4,3,2,1,0:T(8,128)S(1)}, f32[16,7,8,128]{3,2,1,0:T(8,128)S(1)}, f32[8,192]{1,0:T(8,128)S(1)...) custom-call(bf16[4,8,8,192]{3,2,1,0:T(8,128)(2,1)S(1)} %copy-done.1, ...), custom_call_target="tpu_custom_call" | custom-call | flops 1000000000 | tf_op jit(solution)/shard_map/prepare/pallas_call | solution.py:538
  10.9 0.0 collective-permute-done
  10.9 0.0 collective-permute-done.1.p_ref
  10.9 0.1 collective-permute-start.3
  11.0 1.4 %collective-permute-start.2 = (bf16[2,160,128]{2,1,0:T(8,128)(2,1)S(1)}, bf16[2,160,128]{2,1,0:T(8,128)(2,1)S(1)}, u32[]{:S(2)}, u32[]{:S(2)}) collective-permute-start(bf16[2,160,128]{2,1,0:T(8,128)(2,1)S(1)} %pad_maximum_fusion), channel_id=1, source_target_pairs={{0,4},{1,5},{2,6},{3,7},{4,0},{5,1},{6,2},{7,3},{8,12},{9,13},{10,... | collective-permute-start | bytes 245768 | tf_op jit(solution)/shard_map/ppermute | solution.py:92
  12.5 0.9 %collective-permute-done.4.q_ref = bf16[288,128]{1,0:T(8,128)(2,1)S(1)} collective-permute-done((bf16[288,128]{1,0:T(8,128)(2,1)}, bf16[288,128]{1,0:T(8,128)(2,1)S(1)}, u32[]{:S(2)}, u32[]{:S(2)}) %collective-permute-start.4) | collective-permute-done | bytes 73760 | tf_op jit(solution)/shard_map/ppermute | solution.py:97
  13.4 2.0 %collective-permute-done.3 = bf16[2,160,128]{2,1,0:T(8,128)(2,1)S(1)} collective-permute-done((bf16[2,160,128]{2,1,0:T(8,128)(2,1)S(1)}, bf16[2,160,128]{2,1,0:T(8,128)(2,1)S(1)}, u32[]{:S(2)}, u32[]{:S(2)}) %collective-permute-start.3) | collective-permute-done | bytes 81952 | tf_op jit(solution)/shard_map/ppermute | solution.py:92
  15.4 0.4 collective-permute-done.2
  15.8 1.2 %collective-permute-start.6 = (bf16[1,160,128]{2,1,0:T(8,128)(2,1)S(1)}, bf16[1,160,128]{2,1,0:T(8,128)(2,1)S(1)}, u32[]{:S(2)}, u32[]{:S(2)}) collective-permute-start(bf16[1,160,128]{2,1,0:T(8,128)(2,1)S(1)} %slice.32), channel_id=1, source_target_pairs={{0,4},{1,5},{2,6},{3,7},{4,0},{5,1},{6,2},{7,3},{8,12},{9,13},{10,... | collective-permute-start | bytes 122888 | tf_op jit(solution)/shard_map/ppermute | solution.py:92
  17.0 1.2 %collective-permute-start.5 = (bf16[1,160,128]{2,1,0:T(8,128)(2,1)S(1)}, bf16[1,160,128]{2,1,0:T(8,128)(2,1)S(1)}, u32[]{:S(2)}, u32[]{:S(2)}) collective-permute-start(bf16[1,160,128]{2,1,0:T(8,128)(2,1)S(1)} %slice.31), channel_id=1, source_target_pairs={{0,2},{1,3},{2,0},{3,1},{4,6},{5,7},{6,4},{7,5},{8,10},{9,11},{10,... | collective-permute-start | bytes 122888 | tf_op jit(solution)/shard_map/ppermute | solution.py:92
  18.2 2.7 %forward_stencil.1 = (bf16[256,256]{1,0:T(8,128)(2,1)S(1)}, f32[256,256]{1,0:T(8,128)S(1)}, f32[7,15,8,8,128]{4,3,2,1,0:T(8,128)S(1)}) custom-call(s32[1]{0:T(128)} %bitcast.me_ref, f32[2,4,8,8,128]{4,3,2,1,0:T(8,128)S(1)} %get-tuple-element.87.own_ref, bf16[288,128]{1,0:T(8,128)(2,1)S(1)} %collective-permute-done.1.p_ref, ...), custom_call_target="tpu_custom_call" | custom-call | flops 2500000000 | tf_op jit(solution)/shard_map/forward_stencil/pallas_call | solution.py:538
  20.9 0.1 collective-permute-done.5
  21.0 0.0 collective-permute-done.6
  21.0 0.1 collective-permute-start.7
  21.1 1.6 %collective-permute-done.7.g1_ref = bf16[8,160,128]{2,1,0:T(8,128)(2,1)S(1)} collective-permute-done((bf16[8,160,128]{2,1,0:T(8,128)(2,1)S(1)}, bf16[8,160,128]{2,1,0:T(8,128)(2,1)S(1)}, u32[]{:S(2)}, u32[]{:S(2)}) %collective-permute-start.7) | collective-permute-done | bytes 327712 | tf_op jit(solution)/shard_map/ppermute | solution.py:92
  22.7 2.2 %pointwise.1 = (f32[256,192]{1,0:T(8,128)S(1)}, bf16[4,8,8,192]{3,2,1,0:T(8,128)(2,1)S(1)}, bf16[288,128]{1,0:T(8,128)(2,1)S(1)}, bf16[288,128]{1,0:T(8,128)(2,1...) custom-call(s32[1]{0:T(128)} %bitcast.me_ref, ...), custom_call_target="tpu_custom_call" | custom-call | flops 2500000000 | tf_op jit(solution)/shard_map/pointwise/pallas_call | solution.py:538
  25.0 0.2 collective-permute-start.12
  25.2 2.3 %kernel_gradient.1 = (f32[272,128]{1,0:T(8,128)S(1)}, bf16[272,128]{1,0:T(8,128)(2,1)S(1)}) custom-call(s32[1]{0:T(128)} %bitcast.me_ref, f32[7,15,8,8,128]{4,3,2,1,0:T(8,128)S(1)} %get-tuple-element.95.s_ref, bf16[4,8,8,192]{3,2,1,0:T(8,128)(2,1)S(1)} %get-tuple-element.102.g_ref, f32[8,256]{1,0:T(8,128)S(1)} %get-tuple-element.103.small_ref), custom_call_target="tpu_custom_call" | custom-call | flops 2000000000 | tf_op jit(solution)/shard_map/kernel_gradient/pallas_call | solution.py:538
  27.4 0.4 collective-permute-start.8
  27.9 0.1 collective-permute-start.10
  28.0 3.2 %collective-permute-start.11 = (bf16[288,128]{1,0:T(8,128)(2,1)S(1)}, bf16[288,128]{1,0:T(8,128)(2,1)S(1)}, u32[]{:S(2)}, u32[]{:S(2)}) collective-permute-start(bf16[288,128]{1,0:T(8,128)(2,1)S(1)} %get-tuple-element.110), channel_id=1, source_target_pairs={{0,15},{1,2},{2,1},{3,4},{4,3},{5,6},{6,5},{7,8},{8,7},{9,10},{10,... | collective-permute-start | bytes 221192 | tf_op jit(solution)/shard_map/ppermute | solution.py:97
  31.2 0.0 collective-permute-done.12
  31.2 0.1 convert_add_fusion
  31.3 0.1 collective-permute-start.13
  31.4 0.0 collective-permute-done.8
  31.4 2.1 %collective-permute-start.9 = (bf16[272,128]{1,0:T(8,128)(2,1)S(1)}, bf16[272,128]{1,0:T(8,128)(2,1)S(1)}, u32[]{:S(2)}, u32[]{:S(2)}) collective-permute-start(bf16[272,128]{1,0:T(8,128)(2,1)S(1)} %add_convert_fusion.3), channel_id=1, source_target_pairs={{0,8},{1,9},{2,10},{3,11},{4,12},{5,13},{6,14},{7,15},{8,0},{9,1},... | collective-permute-start | bytes 208904 | tf_op jit(solution)/shard_map/ppermute | solution.py:92
  33.5 0.0 collective-permute-done.10.p_ref
  33.5 1.1 %collective-permute-done.11.q_ref = bf16[288,128]{1,0:T(8,128)(2,1)S(1)} collective-permute-done((bf16[288,128]{1,0:T(8,128)(2,1)S(1)}, bf16[288,128]{1,0:T(8,128)(2,1)S(1)}, u32[]{:S(2)}, u32[]{:S(2)}) %collective-permute-start.11) | collective-permute-done | bytes 73760 | tf_op jit(solution)/shard_map/ppermute | solution.py:97
  34.6 3.1 %collective-permute-done.9 = bf16[272,128]{1,0:T(8,128)(2,1)S(1)} collective-permute-done((bf16[272,128]{1,0:T(8,128)(2,1)S(1)}, bf16[272,128]{1,0:T(8,128)(2,1)S(1)}, u32[]{:S(2)}, u32[]{:S(2)}) %collective-permute-start.9) | collective-permute-done | bytes 69664 | tf_op jit(solution)/shard_map/ppermute | solution.py:92
  37.7 0.0 collective-permute-done.13
  37.7 1.3 %collective-permute-start.14 = (bf16[272,128]{1,0:T(8,128)(2,1)S(1)}, bf16[272,128]{1,0:T(8,128)(2,1)S(1)}, u32[]{:S(2)}, u32[]{:S(2)}) collective-permute-start(bf16[272,128]{1,0:T(8,128)(2,1)S(1)} %add_convert_fusion.2), channel_id=1, source_target_pairs={{0,2},{1,3},{2,0},{3,1},{4,6},{5,7},{6,4},{7,5},{8,10},{9,11},{10,... | collective-permute-start | bytes 208904 | tf_op jit(solution)/shard_map/ppermute | solution.py:92
  39.1 0.1 collective-permute-start.15
  39.1 2.7 %backward_stencil.1 = (bf16[4,8,8,192]{3,2,1,0:T(8,128)(2,1)}, bf16[4,8,8,192]{3,2,1,0:T(8,128)(2,1)}) custom-call(s32[1]{0:T(128)} %bitcast.me_ref, bf16[4,8,8,192]{3,2,1,0:T(8,128)(2,1)S(1)} %get-tuple-element.102.g_ref, bf16[288,128]{1,0:T(8,128)(2,1)S(1)} %collective-permute-done.10.p_ref, bf16[288,128]{1,0:T(8,128)(2,1)S(1)} %collective-permute-done.11.q_ref, ...), custom_call_target="tpu_custom_call" | custom-call | flops 2500000000 | tf_op jit(solution)/shard_map/backward_stencil/pallas_call | solution.py:538
  41.9 0.2 collective-permute-done.14
  42.1 1.5 %collective-permute-done.15 = bf16[320,128]{1,0:T(8,128)(2,1)S(1)} collective-permute-done((bf16[320,128]{1,0:T(8,128)(2,1)S(1)}, bf16[320,128]{1,0:T(8,128)(2,1)S(1)}, u32[]{:S(2)}, u32[]{:S(2)}) %collective-permute-start.15) | collective-permute-done | bytes 81952 | tf_op jit(solution)/shard_map/ppermute | solution.py:92
  43.6 0.4 collective-permute-start.16
  44.0 2.2 %collective-permute-start.18 = (bf16[160,128]{1,0:T(8,128)(2,1)S(1)}, bf16[160,128]{1,0:T(8,128)(2,1)S(1)}, u32[]{:S(2)}, u32[]{:S(2)}) collective-permute-start(bf16[160,128]{1,0:T(8,128)(2,1)S(1)} %slice.52), channel_id=1, source_target_pairs={{0,8},{1,9},{2,10},{3,11},{4,12},{5,13},{6,14},{7,15},{8,0},{9,1},... | collective-permute-start | bytes 122888 | tf_op jit(solution)/shard_map/ppermute | solution.py:92
  46.2 1.7 %collective-permute-done.16 = bf16[272,128]{1,0:T(8,128)(2,1)S(1)} collective-permute-done((bf16[272,128]{1,0:T(8,128)(2,1)S(1)}, bf16[272,128]{1,0:T(8,128)(2,1)S(1)}, u32[]{:S(2)}, u32[]{:S(2)}) %collective-permute-start.16) | collective-permute-done | bytes 69664 | tf_op jit(solution)/shard_map/ppermute | solution.py:92
  48.0 0.1 collective-permute-start.17
  48.1 0.9 %collective-permute-done.18.b_ref = bf16[160,128]{1,0:T(8,128)(2,1)S(1)} collective-permute-done((bf16[160,128]{1,0:T(8,128)(2,1)S(1)}, bf16[160,128]{1,0:T(8,128)(2,1)S(1)}, u32[]{:S(2)}, u32[]{:S(2)}) %collective-permute-start.18) | collective-permute-done | bytes 40992 | tf_op jit(solution)/shard_map/ppermute | solution.py:92
  49.0 0.7 %finish.1 = (f32[48,192]{1,0:T(8,128)}, f32[1,48]{1,0:T(1,128)}, f32[48,192]{1,0:T(8,128)}) custom-call(f32[160,128]{1,0:T(8,128)S(1)} %slice.44.a_ref, bf16[160,128]{1,0:T(8,128)(2,1)S(1)} %collective-permute-done.18.b_ref), custom_call_target="tpu_custom_call" | custom-call | flops 700000000 | tf_op jit(solution)/shard_map/finish/pallas_call | solution.py:538
  49.7 0.0 collective-permute-done.17.other_ref
  49.7 0.9 %unpack.1 = (f32[7,7,7,192]{3,2,1,0:T(8,128)}, f32[1,192]{1,0:T(1,128)}, f32[1,192]{1,0:T(1,128)}, f32[1,192]{1,0:T(1,128)}, f32[1,192]{1,0:T(1,128)}, /*index=5*/f32[1,192]{1,0:T(1,128)}) custom-call(s32[1]{0:T(128)} %bitcast.me_ref, bf16[272,128]{1,0:T(8,128)(2,1)S(1)} %add_convert_fusion.mine_ref, bf16[272,128]{1,0:T(8,128)(2,1)S(1)} %collective-permute-done.17.other_ref), custom_call_target="tpu_custom_call" | custom-call | flops 900000000 | tf_op jit(solution)/shard_map/unpack/pallas_call | solution.py:538
  (21 shorter events, 0.3 us)
Async XLA Ops:
  0.6 8.4 %copy-start.1 = (bf16[4,8,8,192]{3,2,1,0:T(8,128)(2,1)S(1)}, bf16[4,8,8,192]{3,2,1,0:T(8,128)(2,1)}, u32[]{:S(2)}) copy-start(bf16[4,8,8,192]{3,2,1,0:T(8,128)(2,1)} %refs_0_.1) | copy-start | bytes 294916
  0.7 8.4 %copy-start.8 = (f32[192]{0:T(256)S(1)}, f32[192]{0:T(256)}, u32[]{:S(2)}) copy-start(f32[192]{0:T(256)} %refs_7_.1) | copy-start | bytes 2308
  0.7 8.4 %copy-start.7 = (f32[192]{0:T(256)S(1)}, f32[192]{0:T(256)}, u32[]{:S(2)}) copy-start(f32[192]{0:T(256)} %refs_6_.1) | copy-start | bytes 2308
  0.7 8.4 %copy-start.6 = (f32[192]{0:T(256)S(1)}, f32[192]{0:T(256)}, u32[]{:S(2)}) copy-start(f32[192]{0:T(256)} %refs_5_.1) | copy-start | bytes 2308
  0.7 8.4 %copy-start.5 = (f32[192]{0:T(256)S(1)}, f32[192]{0:T(256)}, u32[]{:S(2)}) copy-start(f32[192]{0:T(256)} %refs_4_.1) | copy-start | bytes 2308
  0.7 8.4 %copy-start.4 = (f32[192]{0:T(256)S(1)}, f32[192]{0:T(256)}, u32[]{:S(2)}) copy-start(f32[192]{0:T(256)} %refs_3_.1) | copy-start | bytes 2308
  0.7 8.4 %copy-start = (f32[7,7,7,192]{3,2,1,0:T(8,128)S(1)}, f32[7,7,7,192]{3,2,1,0:T(8,128)}, u32[]{:S(2)}) copy-start(f32[7,7,7,192]{3,2,1,0:T(8,128)} %refs_2_.1) | copy-start | bytes 790276
  0.7 8.4 %copy-start.2 = (bf16[4,8,8,192]{3,2,1,0:T(8,128)(2,1)S(1)}, bf16[4,8,8,192]{3,2,1,0:T(8,128)(2,1)}, u32[]{:S(2)}) copy-start(bf16[4,8,8,192]{3,2,1,0:T(8,128)(2,1)} %refs_1_.1) | copy-start | bytes 294916
  2.5 8.3 %collective-permute-start = (bf16[160,128]{1,0:T(8,128)(2,1)}, bf16[160,128]{1,0:T(8,128)(2,1)S(1)}, u32[]{:S(2)}, u32[]{:S(2)}) collective-permute-start(bf16[160,128]{1,0:T(8,128)(2,1)} %get-tuple-element.73.refs_8_), channel_id=1, source_target_pairs={{0,8},{1,9},{2,10},{3,11},{4,12},{5,13},{6,14},{7,15},{8,0},{9,1},... | collective-permute-start | bytes 122888 | tf_op jit(solution)/shard_map/ppermute | solution.py:92
  6.6 4.2 %collective-permute-start.1 = (bf16[288,128]{1,0:T(8,128)(2,1)}, bf16[288,128]{1,0:T(8,128)(2,1)S(1)}, u32[]{:S(2)}, u32[]{:S(2)}) collective-permute-start(bf16[288,128]{1,0:T(8,128)(2,1)} %get-tuple-element.74), channel_id=1, source_target_pairs={{0,1},{1,0},{2,3},{3,2},{4,5},{5,4},{6,7},{7,6},{8,9},{9,8},{10,11... | collective-permute-start | bytes 221192 | tf_op jit(solution)/shard_map/ppermute | solution.py:92
  6.6 6.7 %collective-permute-start.4 = (bf16[288,128]{1,0:T(8,128)(2,1)}, bf16[288,128]{1,0:T(8,128)(2,1)S(1)}, u32[]{:S(2)}, u32[]{:S(2)}) collective-permute-start(bf16[288,128]{1,0:T(8,128)(2,1)} %get-tuple-element.84), channel_id=1, source_target_pairs={{0,15},{1,2},{2,1},{3,4},{4,3},{5,6},{6,5},{7,8},{8,7},{9,10},{10,... | collective-permute-start | bytes 221192 | tf_op jit(solution)/shard_map/ppermute | solution.py:97
  9.1 0.8 %copy-start.3 = (bf16[160,128]{1,0:T(8,128)(2,1)S(1)}, bf16[160,128]{1,0:T(8,128)(2,1)}, u32[]{:S(2)}) copy-start(bf16[160,128]{1,0:T(8,128)(2,1)} %get-tuple-element.73.refs_8_) | copy-start | bytes 122884
  10.9 4.5 %collective-permute-start.3 = (bf16[2,160,128]{2,1,0:T(8,128)(2,1)S(1)}, bf16[2,160,128]{2,1,0:T(8,128)(2,1)S(1)}, u32[]{:S(2)}, u32[]{:S(2)}) collective-permute-start(bf16[2,160,128]{2,1,0:T(8,128)(2,1)S(1)} %pad_maximum_fusion), channel_id=1, source_target_pairs={{0,2},{1,3},{2,0},{3,1},{4,6},{5,7},{6,4},{7,5},{8,10},{9,11},{10,... | collective-permute-start | bytes 245768 | tf_op jit(solution)/shard_map/ppermute | solution.py:92
  11.0 4.8 %collective-permute-start.2 = (bf16[2,160,128]{2,1,0:T(8,128)(2,1)S(1)}, bf16[2,160,128]{2,1,0:T(8,128)(2,1)S(1)}, u32[]{:S(2)}, u32[]{:S(2)}) collective-permute-start(bf16[2,160,128]{2,1,0:T(8,128)(2,1)S(1)} %pad_maximum_fusion), channel_id=1, source_target_pairs={{0,4},{1,5},{2,6},{3,7},{4,0},{5,1},{6,2},{7,3},{8,12},{9,13},{10,... | collective-permute-start | bytes 245768 | tf_op jit(solution)/shard_map/ppermute | solution.py:92
  15.8 5.2 %collective-permute-start.6 = (bf16[1,160,128]{2,1,0:T(8,128)(2,1)S(1)}, bf16[1,160,128]{2,1,0:T(8,128)(2,1)S(1)}, u32[]{:S(2)}, u32[]{:S(2)}) collective-permute-start(bf16[1,160,128]{2,1,0:T(8,128)(2,1)S(1)} %slice.32), channel_id=1, source_target_pairs={{0,4},{1,5},{2,6},{3,7},{4,0},{5,1},{6,2},{7,3},{8,12},{9,13},{10,... | collective-permute-start | bytes 122888 | tf_op jit(solution)/shard_map/ppermute | solution.py:92
  17.0 4.0 %collective-permute-start.5 = (bf16[1,160,128]{2,1,0:T(8,128)(2,1)S(1)}, bf16[1,160,128]{2,1,0:T(8,128)(2,1)S(1)}, u32[]{:S(2)}, u32[]{:S(2)}) collective-permute-start(bf16[1,160,128]{2,1,0:T(8,128)(2,1)S(1)} %slice.31), channel_id=1, source_target_pairs={{0,2},{1,3},{2,0},{3,1},{4,6},{5,7},{6,4},{7,5},{8,10},{9,11},{10,... | collective-permute-start | bytes 122888 | tf_op jit(solution)/shard_map/ppermute | solution.py:92
  21.0 1.7 %collective-permute-start.7 = (bf16[8,160,128]{2,1,0:T(8,128)(2,1)S(1)}, bf16[8,160,128]{2,1,0:T(8,128)(2,1)S(1)}, u32[]{:S(2)}, u32[]{:S(2)}) collective-permute-start(bf16[8,160,128]{2,1,0:T(8,128)(2,1)S(1)} %constant_dynamic-update-slice_fusion.g0_ref), channel_id=1, source_target_pairs={{0,1},{1,0},{2,3},{3,2},{4,5},{5,4},{6,7},{7,6},{8,9},{9,8},{10,11... | collective-permute-start | bytes 983048 | tf_op jit(solution)/shard_map/ppermute | solution.py:92
  25.0 6.2 %collective-permute-start.12 = (bf16[8,160,128]{2,1,0:T(8,128)(2,1)S(1)}, bf16[8,160,128]{2,1,0:T(8,128)(2,1)S(1)}, u32[]{:S(2)}, u32[]{:S(2)}) collective-permute-start(bf16[8,160,128]{2,1,0:T(8,128)(2,1)S(1)} %get-tuple-element.113), channel_id=1, source_target_pairs={{0,1},{1,0},{2,3},{3,2},{4,5},{5,4},{6,7},{7,6},{8,9},{9,8},{10,11... | collective-permute-start | bytes 983048 | tf_op jit(solution)/shard_map/ppermute | solution.py:92
  27.4 3.9 %collective-permute-start.8 = (bf16[272,128]{1,0:T(8,128)(2,1)S(1)}, bf16[272,128]{1,0:T(8,128)(2,1)S(1)}, u32[]{:S(2)}, u32[]{:S(2)}) collective-permute-start(bf16[272,128]{1,0:T(8,128)(2,1)S(1)} %get-tuple-element.108), channel_id=1, source_target_pairs={{0,1},{1,0},{2,3},{3,2},{4,5},{5,4},{6,7},{7,6},{8,9},{9,8},{10,11... | collective-permute-start | bytes 208904 | tf_op jit(solution)/shard_map/ppermute | solution.py:92
  27.9 5.7 %collective-permute-start.10 = (bf16[288,128]{1,0:T(8,128)(2,1)S(1)}, bf16[288,128]{1,0:T(8,128)(2,1)S(1)}, u32[]{:S(2)}, u32[]{:S(2)}) collective-permute-start(bf16[288,128]{1,0:T(8,128)(2,1)S(1)} %get-tuple-element.109), channel_id=1, source_target_pairs={{0,1},{1,0},{2,3},{3,2},{4,5},{5,4},{6,7},{7,6},{8,9},{9,8},{10,11... | collective-permute-start | bytes 221192 | tf_op jit(solution)/shard_map/ppermute | solution.py:92
  28.0 6.6 %collective-permute-start.11 = (bf16[288,128]{1,0:T(8,128)(2,1)S(1)}, bf16[288,128]{1,0:T(8,128)(2,1)S(1)}, u32[]{:S(2)}, u32[]{:S(2)}) collective-permute-start(bf16[288,128]{1,0:T(8,128)(2,1)S(1)} %get-tuple-element.110), channel_id=1, source_target_pairs={{0,15},{1,2},{2,1},{3,4},{4,3},{5,6},{6,5},{7,8},{8,7},{9,10},{10,... | collective-permute-start | bytes 221192 | tf_op jit(solution)/shard_map/ppermute | solution.py:97
  31.3 6.4 %collective-permute-start.13 = (bf16[640,128]{1,0:T(8,128)(2,1)S(1)}, bf16[640,128]{1,0:T(8,128)(2,1)S(1)}, u32[]{:S(2)}, u32[]{:S(2)}) collective-permute-start(bf16[640,128]{1,0:T(8,128)(2,1)S(1)} %bitcast.16), channel_id=1, source_target_pairs={{0,2},{1,3},{2,0},{3,1},{4,6},{5,7},{6,4},{7,5},{8,10},{9,11},{10,... | collective-permute-start | bytes 491528 | tf_op jit(solution)/shard_map/ppermute | solution.py:92
  31.4 6.3 %collective-permute-start.9 = (bf16[272,128]{1,0:T(8,128)(2,1)S(1)}, bf16[272,128]{1,0:T(8,128)(2,1)S(1)}, u32[]{:S(2)}, u32[]{:S(2)}) collective-permute-start(bf16[272,128]{1,0:T(8,128)(2,1)S(1)} %add_convert_fusion.3), channel_id=1, source_target_pairs={{0,8},{1,9},{2,10},{3,11},{4,12},{5,13},{6,14},{7,15},{8,0},{9,1},... | collective-permute-start | bytes 208904 | tf_op jit(solution)/shard_map/ppermute | solution.py:92
  37.7 4.4 %collective-permute-start.14 = (bf16[272,128]{1,0:T(8,128)(2,1)S(1)}, bf16[272,128]{1,0:T(8,128)(2,1)S(1)}, u32[]{:S(2)}, u32[]{:S(2)}) collective-permute-start(bf16[272,128]{1,0:T(8,128)(2,1)S(1)} %add_convert_fusion.2), channel_id=1, source_target_pairs={{0,2},{1,3},{2,0},{3,1},{4,6},{5,7},{6,4},{7,5},{8,10},{9,11},{10,... | collective-permute-start | bytes 208904 | tf_op jit(solution)/shard_map/ppermute | solution.py:92
  39.1 4.5 %collective-permute-start.15 = (bf16[320,128]{1,0:T(8,128)(2,1)S(1)}, bf16[320,128]{1,0:T(8,128)(2,1)S(1)}, u32[]{:S(2)}, u32[]{:S(2)}) collective-permute-start(bf16[320,128]{1,0:T(8,128)(2,1)S(1)} %slice.51), channel_id=1, source_target_pairs={{0,4},{1,5},{2,6},{3,7},{4,0},{5,1},{6,2},{7,3},{8,12},{9,13},{10,... | collective-permute-start | bytes 245768 | tf_op jit(solution)/shard_map/ppermute | solution.py:92
  43.6 4.4 %collective-permute-start.16 = (bf16[272,128]{1,0:T(8,128)(2,1)S(1)}, bf16[272,128]{1,0:T(8,128)(2,1)S(1)}, u32[]{:S(2)}, u32[]{:S(2)}) collective-permute-start(bf16[272,128]{1,0:T(8,128)(2,1)S(1)} %add_convert_fusion.1), channel_id=1, source_target_pairs={{0,4},{1,5},{2,6},{3,7},{4,0},{5,1},{6,2},{7,3},{8,12},{9,13},{10,... | collective-permute-start | bytes 208904 | tf_op jit(solution)/shard_map/ppermute | solution.py:92
  44.0 5.0 %collective-permute-start.18 = (bf16[160,128]{1,0:T(8,128)(2,1)S(1)}, bf16[160,128]{1,0:T(8,128)(2,1)S(1)}, u32[]{:S(2)}, u32[]{:S(2)}) collective-permute-start(bf16[160,128]{1,0:T(8,128)(2,1)S(1)} %slice.52), channel_id=1, source_target_pairs={{0,8},{1,9},{2,10},{3,11},{4,12},{5,13},{6,14},{7,15},{8,0},{9,1},... | collective-permute-start | bytes 122888 | tf_op jit(solution)/shard_map/ppermute | solution.py:92
  48.0 1.7 %collective-permute-start.17 = (bf16[272,128]{1,0:T(8,128)(2,1)S(1)}, bf16[272,128]{1,0:T(8,128)(2,1)S(1)}, u32[]{:S(2)}, u32[]{:S(2)}) collective-permute-start(bf16[272,128]{1,0:T(8,128)(2,1)S(1)} %add_convert_fusion.mine_ref), channel_id=1, source_target_pairs={{0,1},{1,0},{2,3},{3,2},{4,5},{5,4},{6,7},{7,6},{8,9},{9,8},{10,11... | collective-permute-start | bytes 208904 | tf_op jit(solution)/shard_map/ppermute | solution.py:92

commit v4 on v3

--- a/solution.py
+++ b/solution.py
@@ -111,11 +111,11 @@
     z_ref[1, plane, ..., 64:128] = v[..., LANE:]
 
 
-def pack_planes(first, load, out_ref):
+def pack_planes(first, load, out_ref, base=0):
     for k in range(3):
         v = load(first + k)
         cells = v.shape[0]
-        at = k * cells * 3 // 2
+        at = base + k * cells * 3 // 2
         out_ref[at : at + cells] = v[:, :LANE].astype(BF16)
         pair = jnp.concatenate([v[: cells // 2, LANE:], v[cells // 2 :, LANE:]], axis=1)
         out_ref[at + cells : at + cells * 3 // 2] = pair.astype(BF16)
@@ -173,7 +173,7 @@
         to_points(analysis(), lambda k: z_ref[0, k, j], lambda k: z_ref[1, k, j], store)
         return carry
 
-    lax.fori_loop(0, 8, row, 0)
+    lax.fori_loop(0, 8, row, 0, unroll=8)
 
     def unit(u, carry):
         taps_at = reversed_unit(u) if flip else u
@@ -199,7 +199,7 @@
             u_ref[u, j] = acc[j]
         return carry
 
-    lax.fori_loop(0, 3 * (PAIRS + 1), unit, 0)
+    lax.fori_loop(0, 3 * (PAIRS + 1), unit, 0, unroll=3)
 
 
 def fetch(sources, targets, sem):
@@ -295,7 +295,7 @@
             m_ref[at, LANE : LANE + 64] = rest[i][:, 0:64]
         return carry
 
-    lax.fori_loop(0, 8, row, 0)
+    lax.fori_loop(0, 8, row, 0, unroll=8)
     chans = m_ref.shape[1]
     mixed = m_ref[...] + vec_ref[0:1]
     centred = mixed - jnp.mean(mixed, axis=-1, keepdims=True)
@@ -309,7 +309,7 @@
     unit_ref[:, chans:256] = jnp.broadcast_to(inverse, (rows, 256 - chans))
 
 
-def pointwise_kernel(me_ref, g0_ref, g1_ref, na_ref, unit_ref, xf_ref, cf_ref, db_ref, vec_ref, branch_ref, dm_ref, core_ref, far_ref, w0_ref, w1_ref, small_ref, wi_ref, wo_ref, di_ref, do_ref, m_ref):
+def pointwise_kernel(me_ref, g0_ref, g1_ref, na_ref, unit_ref, xf_ref, cf_ref, db_ref, vec_ref, branch_ref, dm_ref, far_ref, w0_ref, w1_ref, small_ref, wi_ref, wo_ref, di_ref, do_ref, m_ref):
     rows, chans = xf_ref.shape
     normed = na_ref[...]
     d_b = db_ref[...]
@@ -321,42 +321,48 @@
     pieces, high = g0_ref.shape[0], (g0_ref.shape[1] - 16) // 3
     low = low_lanes((high, LANE))
     first_row = lax.broadcasted_iota(jnp.int32, (16, LANE), 0) == 0
-    for g_ref, w_ref in ((g0_ref, w0_ref), (g1_ref, w1_ref)):
-        lines = []
-        for i in range(pieces):
-            here = slice(i * high, i * high + high)
-            rest = g_ref[i, high : 2 * high].astype(F32)
-            wi_ref[here, 0:LANE] = g_ref[i, 0:high]
-            wi_ref[here, LANE:256] = jnp.where(low, rest, 0.0).astype(BF16)
-            wo_ref[here, 0:LANE] = g_ref[i, 2 * high : 3 * high]
-            wo_ref[here, LANE:256] = jnp.where(low, pltpu.roll(rest, 64, axis=1), 0.0).astype(BF16)
-            line = g_ref[i, 3 * high : 3 * high + 16].astype(F32)[0:1]
-            lines.append(jnp.broadcast_to(line, (8, LANE)))
-        bias = gather_lines(lines, high)
-        d_bias = []
-        for c in range(pieces * high // LANE):
-            here = slice(c * LANE, c * LANE + LANE)
-            w_in, w_out = wi_ref[here], wo_ref[here]
-            pre = lax.dot_general(normed, w_in, over_c, preferred_element_type=F32) + bias[c][0:1]
-            d_hidden = lax.dot_general(d_b, w_out, over_c, preferred_element_type=F32)
-            cdf = 0.5 * (1.0 + lax.erf(pre * root_half))
-            hidden = (pre * cdf).astype(BF16)
-            slope = cdf + pre * jnp.exp(-0.5 * pre * pre) * inv_root_tau
-            d_pre = d_hidden * slope
-            d_bias.append(jnp.broadcast_to(jnp.sum(d_pre, axis=0, keepdims=True), (8, LANE)))
-            d_pre = d_pre.astype(BF16)
-            branch = branch + jnp.dot(hidden, w_out, preferred_element_type=F32)
-            d_normed = d_normed + jnp.dot(d_pre, w_in, preferred_element_type=F32)
-            di_ref[here] = lax.dot_general(d_pre, normed, over_rows, preferred_element_type=F32)
-            do_ref[here] = lax.dot_general(hidden, d_b, over_rows, preferred_element_type=F32)
-        for i, line in enumerate(scatter_lines(d_bias, pieces, high)):
-            here = slice(i * high, i * high + high)
-            rest = jnp.where(low, di_ref[here, LANE:256], pltpu.roll(do_ref[here, LANE:256], 64, axis=1))
-            w_ref[i, 0:high] = di_ref[here, 0:LANE].astype(w_ref.dtype)
-            w_ref[i, high : 2 * high] = rest.astype(w_ref.dtype)
-            w_ref[i, 2 * high : 3 * high] = do_ref[here, 0:LANE].astype(w_ref.dtype)
-            line = jnp.where(first_row, jnp.broadcast_to(line[0:1], (16, LANE)), 0.0)
-            w_ref[i, 3 * high : 3 * high + 16] = line.astype(w_ref.dtype)
+    lines, d_bias = [], []
+    for i in range(2 * pieces):
+        here = slice(i * high, i * high + high)
+        g_ref, k = (g0_ref, i) if i < pieces else (g1_ref, i - pieces)
+        rest = g_ref[k, high : 2 * high].astype(F32)
+        wi_ref[here, 0:LANE] = g_ref[k, 0:high]
+        wi_ref[here, LANE:256] = jnp.where(low, rest, 0.0).astype(BF16)
+        wo_ref[here, 0:LANE] = g_ref[k, 2 * high : 3 * high]
+        wo_ref[here, LANE:256] = jnp.where(low, pltpu.roll(rest, 64, axis=1), 0.0).astype(BF16)
+        line = g_ref[k, 3 * high : 3 * high + 16].astype(F32)[0:1]
+        lines.append(jnp.broadcast_to(line, (8, LANE)))
+    bias = gather_lines(lines, high)
+    total = 2 * pieces * high
+    step = next(n for n in (768, 512, 256) if total % n == 0)
+    for first in range(0, total, step):
+        here = slice(first, first + step)
+        w_in, w_out = wi_ref[here], wo_ref[here]
+        line = jnp.concatenate([v[0:1] for v in bias[first // LANE : (first + step) // LANE]], axis=1)
+        pre = lax.dot_general(normed, w_in, over_c, preferred_element_type=F32) + line
+        d_hidden = lax.dot_general(d_b, w_out, over_c, preferred_element_type=F32)
+        cdf = 0.5 * (1.0 + lax.erf(pre * root_half))
+        hidden = (pre * cdf).astype(BF16)
+        slope = cdf + pre * jnp.exp(-0.5 * pre * pre) * inv_root_tau
+        d_pre = d_hidden * slope
+        line = jnp.sum(d_pre, axis=0, keepdims=True)
+        for at in range(0, step, LANE):
+            d_bias.append(jnp.broadcast_to(line[:, at : at + LANE], (8, LANE)))
+        d_pre = d_pre.astype(BF16)
+        branch = branch + jnp.dot(hidden, w_out, preferred_element_type=F32)
+        d_normed = d_normed + jnp.dot(d_pre, w_in, preferred_element_type=F32)
+        di_ref[here] = lax.dot_general(d_pre, normed, over_rows, preferred_element_type=F32)
+        do_ref[here] = lax.dot_general(hidden, d_b, over_rows, preferred_element_type=F32)
+    for i, line in enumerate(scatter_lines(d_bias, 2 * pieces, high)):
+        here = slice(i * high, i * high + high)
+        w_ref, k = (w0_ref, i) if i < pieces else (w1_ref, i - pieces)
+        rest = jnp.where(low, di_ref[here, LANE:256], pltpu.roll(do_ref[here, LANE:256], 64, axis=1))
+        at = k * (3 * high + 16)
+        w_ref[at : at + high] = di_ref[here, 0:LANE].astype(w_ref.dtype)
+        w_ref[at + high : at + 2 * high] = rest.astype(w_ref.dtype)
+        w_ref[at + 2 * high : at + 3 * high] = do_ref[here, 0:LANE].astype(w_ref.dtype)
+        line = jnp.where(first_row, jnp.broadcast_to(line[0:1], (16, LANE)), 0.0)
+        w_ref[at + 3 * high : at + 3 * high + 16] = line.astype(w_ref.dtype)
     branch = branch[:, 0:chans] + vec_ref[3:4]
     branch_ref[...] = gamma * branch
     d_normed = d_normed[:, 0:chans]
@@ -371,7 +377,7 @@
     dm_ref[...] = d_mixed.reshape(dm_ref.shape).astype(BF16)
     m_ref[...] = d_mixed.reshape(m_ref.shape)
     odd = lax.rem(me_ref[0], 2)
-    pack_planes(1 - odd, lambda i: m_ref[i], core_ref)
+    pack_planes(1 - odd, lambda i: m_ref[i], w1_ref, w0_ref.shape[0])
     pack_planes(odd, lambda i: m_ref[i], far_ref)
     small_ref[...] = jnp.zeros(small_ref.shape, F32)
     sums = (d_mixed, d_normed * unit, d_normed, None, cf_ref[...] * branch)
@@ -380,21 +386,13 @@
         small_ref[i : i + 1, 0:chans] = total
 
 
-def rows_to_one(v):
-    row = lax.broadcasted_iota(jnp.int32, (8, LANE), 0)
-    v = list(v) + [jnp.zeros((8, LANE), F32)]
-    for half in (4, 2, 1):
-        low = (row & half) == 0
-        v = [
-            jnp.where(low, v[i], v[i + half])
-            + jnp.where(
-                low,
-                pltpu.roll(v[i], 8 - half, axis=0),
-                pltpu.roll(v[i + half], half, axis=0),
-            )
-            for i in range(half)
-        ]
-    return v[0]
+def rows_to_one(v, p_ref):
+    for b, x in enumerate(v):
+        p_ref[8 * b : 8 * b + 8] = x
+    total = p_ref[pl.ds(0, 8, stride=8), :]
+    for k in range(1, 8):
+        total = total + p_ref[pl.ds(k, 8, stride=8), :]
+    return total
 
 
 HALF = 272
@@ -412,7 +410,8 @@
     return 77 + 7 * (g % 25), 64 * (g // 25)
 
 
-def grad_kernel(me_ref, s_ref, g_ref, small_ref, keep_ref, send_ref, z_ref, t_ref, o_ref, wa_ref, wb_ref, w_ref):
+def grad_kernel(me_ref, s_ref, g_ref, small_ref, keep_ref, send_ref, z_ref, t_ref, o_ref, wa_ref, wb_ref, w_ref, p_ref):
+    p_ref[:, 56:64] = jnp.zeros((7, 8, LANE), F32)
     odd = lax.rem(me_ref[0], 2)
     for i in range(4):
         split(g_ref[i].astype(F32), z_ref, i)
@@ -424,7 +423,7 @@
         to_points(evaluation(4), lambda k: z_ref[0, k, j], lambda k: z_ref[1, k, j], store)
         return carry
 
-    lax.fori_loop(0, 8, row, 0)
+    lax.fori_loop(0, 8, row, 0, unroll=8)
 
     def unit(u, carry):
         grads = [t_ref[u, j] for j in range(8)]
@@ -437,15 +436,11 @@
                     if 0 <= j < 8:
                         term = x * grads[j]
                         acc[b] = term if acc[b] is None else acc[b] + term
-            o_ref[u, e] = rows_to_one(acc)
+            o_ref[u, e] = rows_to_one(acc, p_ref.at[e])
         return carry
 
-    lax.fori_loop(0, 3 * (PAIRS + 1), unit, 0)
-
-    for b in range(49):
-        at = 64 * (b // 7) + 8 * (b % 7)
-        wa_ref[at : at + 8] = jnp.zeros((8, LANE), F32)
-        wb_ref[at : at + 8] = jnp.zeros((8, LANE), F32)
+    lax.fori_loop(0, 3 * (PAIRS + 1), unit, 0, unroll=3)
+
     for e in range(7):
         main, rest = from_points(7, lambda u: o_ref[u, e])
         for a in range(7):
@@ -471,8 +466,17 @@
     send_ref[...] = w_ref[1 - odd].astype(BF16)
 
 
-def unpack_kernel(scale, me_ref, mine_ref, other_ref, dk_ref, *refs):
-    odd, small_refs, w_ref = lax.rem(me_ref[0], 2), refs[:5], refs[5]
+def final_kernel(scale, me_ref, mine_ref, other_ref, total_ref, dk_ref, *refs):
+    odd, small_refs, (wi_ref, bi_ref, wo_ref, w_ref) = lax.rem(me_ref[0], 2), refs[:5], refs[5:]
+    total = total_ref[...] * scale
+    units = wi_ref.shape[0]
+    high = (total.shape[0] - 16) // 3
+    rest = total[high : high + units]
+    wi_ref[:, 0:LANE] = total[0:units]
+    wi_ref[:, LANE : LANE + 64] = rest[:, 0:64]
+    wo_ref[:, 0:LANE] = total[2 * high : 2 * high + units]
+    wo_ref[:, LANE : LANE + 64] = rest[:, 64:LANE]
+    bi_ref[...] = total[3 * high : 3 * high + 1, 0:units]
     w_ref[odd] = mine_ref[...].astype(F32) * scale
     w_ref[1 - odd] = other_ref[...].astype(F32) * scale
     for g in range(49):
@@ -483,18 +487,6 @@
     for i, ref in enumerate(small_refs):
         ref[:, 0:LANE] = w_ref[0, 266 + i : 267 + i]
         ref[:, LANE : LANE + 64] = w_ref[1, 252 + i : 253 + i, 0:64]
-
-
-def finish_kernel(scale, a_ref, b_ref, wi_ref, bi_ref, wo_ref):
-    total = (a_ref[...] + b_ref[...].astype(F32)) * scale
-    units = wi_ref.shape[0]
-    high = (total.shape[0] - 16) // 3
-    rest = total[high : high + units]
-    wi_ref[:, 0:LANE] = total[0:units]
-    wi_ref[:, LANE : LANE + 64] = rest[:, 0:64]
-    wo_ref[:, 0:LANE] = total[2 * high : 2 * high + units]
-    wo_ref[:, LANE : LANE + 64] = rest[:, 64:LANE]
-    bi_ref[...] = total[3 * high : 3 * high + 1, 0:units]
 
 
 def back_kernel(last, me_ref, g_ref, p_ref, q_ref, t_ref, c_ref, xf_ref, branch_ref, dx_ref, out_ref, z_ref, s_ref, u_ref):
@@ -612,7 +604,7 @@
     weights_other = swap(weights, 1)
 
     pieces = weights.shape[0]
-    branch, d_mixed, to_core, to_far, grad_keep, grad_send, small = call(
+    branch, d_mixed, to_far, grad_keep, to_core, small = call(
         pointwise_kernel,
         "pointwise",
         2.5,
@@ -621,14 +613,13 @@
             cells,
             struct(features.shape, BF16),
             rim,
-            rim,
-            struct((pieces, lines, LANE), F32),
-            struct((pieces, lines, LANE), BF16),
+            struct((pieces * lines, LANE), F32),
+            struct((pieces * lines + rim.shape[0], LANE), BF16),
             struct((8, 256), F32),
         ),
         (me, weights, weights_other, normed, unit, x_f32, cot_f32, d_branch, vecs),
-        [pltpu.VMEM((pieces * high, 256), BF16)] * 2
-        + [pltpu.VMEM((pieces * high, 256), F32)] * 2
+        [pltpu.VMEM((2 * pieces * high, 256), BF16)] * 2
+        + [pltpu.VMEM((2 * pieces * high, 256), F32)] * 2
         + [pltpu.VMEM((size_x, size_y * size_z, chans), F32)],
     )
     keep, send = call(
@@ -645,20 +636,23 @@
             pltpu.VMEM((448, LANE), F32),
             pltpu.VMEM((448, LANE), F32),
             pltpu.VMEM((2, HALF, LANE), F32),
+            pltpu.VMEM((7, 64, LANE), F32),
         ],
     )
 
-    total = (grad_keep + swap(grad_send, 1).astype(F32)).reshape(pieces * lines, LANE)
-    send, to_core, to_far = lax.optimization_barrier((send, to_core, to_far))
+    from_core = swap(to_core, 1)
+    total = grad_keep + from_core[: pieces * lines].astype(F32)
+    g_core = from_core[pieces * lines :]
+    send, to_far = lax.optimization_barrier((send, to_far))
     sums = keep + swap(send, 1).astype(F32)
-    g_core, g_far = swap(to_core, 1), swap_odd(to_far)
+    g_far = swap_odd(to_far)
     for step, (bit, sums_bit) in enumerate(zip(order[1:], sums_order[1:])):
         n = total.shape[0] // 2
         mine, kept = sums.astype(BF16), total[:n]
         theirs = swap(mine, sums_bit)
         got = swap(total[n:].astype(BF16), bit)
         if step == 0:
-            theirs, g_core, g_far = lax.optimization_barrier((theirs, g_core, g_far))
+            theirs, g_far = lax.optimization_barrier((theirs, g_far))
         if step == len(order) - 3:
             d_x, output = call(
                 functools.partial(back_kernel, devices - 1),
@@ -676,21 +670,16 @@
         total = kept + got.astype(F32)
     mine = sums.astype(BF16)
     other = swap(mine, 1)
-    d_w_in, d_b_in, d_w_out = call(
-        functools.partial(finish_kernel, scale),
-        "finish",
-        0.7,
+    total = lax.optimization_barrier(kept + got.astype(F32))
+    d_kernel, *vectors, d_w_in, d_b_in, d_w_out = call(
+        functools.partial(final_kernel, scale),
+        "final",
+        1.0,
         4,
-        (struct((units, chans), F32), struct((1, units), F32), struct((units, chans), F32)),
-        (kept, got),
-    )
-    d_kernel, *vectors = call(
-        functools.partial(unpack_kernel, scale),
-        "unpack",
-        0.9,
-        4,
-        (struct(kernel.shape, F32),) + (struct((1, chans), F32),) * 5,
-        (me, mine, other),
+        (struct(kernel.shape, F32),)
+        + (struct((1, chans), F32),) * 5
+        + (struct((units, chans), F32), struct((1, units), F32), struct((units, chans), F32)),
+        (me, mine, other, total),
         [pltpu.VMEM((2, HALF, LANE), F32)],
     )
     d_b_dw, d_ln_gain, d_ln_bias, d_b_out, d_gamma = [v.reshape(chans) for v in vectors]

time: 50.8 us -> 49 us (0.965)
  Pallas kernels: 14.2 us -> 11.6 us
  waiting for transfers between devices: 13.5 us -> 14.7 us
    pallas_call x8 -> x7, Pallas kernels: 14.2 us -> 11.6 us  [call(): pl.pallas_call(body, out_shape=out_shape, in_specs=specs, out_specs=jax.t...]
    ppermute x17 -> x16, waiting for transfers between devices: 11.6 us -> 12.5 us  [swap(): return lax.ppermute(x, 'space', [(i, i ^ bit) for i in range(size)])]
    ppermute x17 -> x16, starting transfers between devices: 15.1 us -> 15.1 us  [swap(): return lax.ppermute(x, 'space', [(i, i ^ bit) for i in range(size)])]
  transfers between devices with their start and end apart: 19 -> 18, of which waited for: 11 -> 11; matrix products, arithmetic and copies ran while one was open for 1% -> 0% of each run, Pallas kernels for 18% -> 16%
where the time goes in v4:
time: 49 us; the launch traced here: 48.8 us
  starting transfers between devices  20.4 us (42%)
  waiting for transfers between devices  14.7 us (30%)
  Pallas kernels  11.6 us (24%)
  between operations  0.94 us (2%)
  local copies, waits for them, and re-layouts  0.92 us (2%)
    ppermute x16, starting transfers between devices, swap(): return lax.ppermute(x, 'space', [(i, i ^ bit) for i in range(size)])  15.1 us
    ppermute x16, waiting for transfers between devices, swap(): return lax.ppermute(x, 'space', [(i, i ^ bit) for i in range(size)])  12.5 us
    pallas_call x7, Pallas kernels, call(): pl.pallas_call(body, out_shape=out_shape, in_specs=specs, out_specs=jax.t...  11.6 us
    ppermute x2, starting transfers between devices, swap_odd(): lax.ppermute(x, 'space', [(i, (i + 1 if i % 2 else i - 1) % size) for i i...  5.34 us
    ppermute x2, waiting for transfers between devices, swap_odd(): lax.ppermute(x, 'space', [(i, (i + 1 if i % 2 else i - 1) % size) for i i...  2.17 us
  transfers between devices with their start and end apart: 18, of which 11 were waited for; matrix products, arithmetic and copies ran while one was open for 0% of the time, Pallas kernels for 16%

profile of v4, /device:TPU:0, one launch (start us, length us, event | category | flops | bytes accessed | tf_op | source)
XLA Modules:
  0.0 48.8 jit_solution(13032226512752040390)
XLA Ops:
  0.6 0.0 copy-start.1
  0.7 0.0 copy-start.8
  0.7 0.0 copy-start.7
  0.7 0.0 copy-start.6
  0.7 0.0 copy-start.5
  0.7 0.0 copy-start.4
  0.7 0.0 copy-start
  0.7 0.0 copy-start.2
  0.7 1.8 %pack.1 = (bf16[160,128]{1,0:T(8,128)(2,1)}, bf16[288,128]{1,0:T(8,128)(2,1)}, bf16[288,128]{1,0:T(8,128)(2,1)}) custom-call(s32[1]{0:T(128)} %bitcast.me_ref, bf16[48,192]{1,0:T(8,128)(2,1)} %wi_hbm.1, bf16[48]{0:T(256)(128)(2,1)} %b_hbm.1, bf16[48,192]{1,0:T(8,128)(2,1)} %wo_hbm.1, bf16[4,8,8,192]{3,2,1,0:T(8,128)(2,1)} %refs_0_.1), custom_call_target="tpu_custom_call" | custom-call | flops 1000000000 | tf_op jit(solution)/shard_map/pack/pallas_call | solution.py:530
  2.5 4.1 %collective-permute-start = (bf16[160,128]{1,0:T(8,128)(2,1)}, bf16[160,128]{1,0:T(8,128)(2,1)S(1)}, u32[]{:S(2)}, u32[]{:S(2)}) collective-permute-start(bf16[160,128]{1,0:T(8,128)(2,1)} %get-tuple-element.70.refs_8_), channel_id=1, source_target_pairs={{0,8},{1,9},{2,10},{3,11},{4,12},{5,13},{6,14},{7,15},{8,0},{9,1},... | collective-permute-start | bytes 122888 | tf_op jit(solution)/shard_map/ppermute | solution.py:92
  6.6 0.0 collective-permute-start.1
  6.6 2.4 %collective-permute-start.4 = (bf16[288,128]{1,0:T(8,128)(2,1)}, bf16[288,128]{1,0:T(8,128)(2,1)S(1)}, u32[]{:S(2)}, u32[]{:S(2)}) collective-permute-start(bf16[288,128]{1,0:T(8,128)(2,1)} %get-tuple-element.81), channel_id=1, source_target_pairs={{0,15},{1,2},{2,1},{3,4},{4,3},{5,6},{6,5},{7,8},{8,7},{9,10},{10,... | collective-permute-start | bytes 221192 | tf_op jit(solution)/shard_map/ppermute | solution.py:97
  9.0 0.0 copy-done.1
  9.0 0.0 copy-done.8
  9.0 0.0 copy-done.7
  9.0 0.0 copy-done.6
  9.0 0.0 copy-done.5
  9.0 0.0 copy-done.4
  9.1 0.0 copy-done
  9.1 0.0 copy-done.2
  9.1 0.0 copy-start.3
  9.1 0.8 %copy-done.3 = bf16[160,128]{1,0:T(8,128)(2,1)S(1)} copy-done((bf16[160,128]{1,0:T(8,128)(2,1)S(1)}, bf16[160,128]{1,0:T(8,128)(2,1)}, u32[]{:S(2)}) %copy-start.3) | copy-done | bytes 40984
  9.9 1.0 %prepare.1 = (bf16[160,128]{1,0:T(8,128)(2,1)S(1)}, f32[2,4,8,8,128]{4,3,2,1,0:T(8,128)S(1)}, f32[16,7,8,128]{3,2,1,0:T(8,128)S(1)}, f32[8,192]{1,0:T(8,128)S(1)...) custom-call(bf16[4,8,8,192]{3,2,1,0:T(8,128)(2,1)S(1)} %copy-done.1, ...), custom_call_target="tpu_custom_call" | custom-call | flops 1000000000 | tf_op jit(solution)/shard_map/prepare/pallas_call | solution.py:530
  10.9 0.0 collective-permute-done
  10.9 0.0 collective-permute-done.1.p_ref
  10.9 0.1 collective-permute-start.3
  11.0 1.4 %collective-permute-start.2 = (bf16[2,160,128]{2,1,0:T(8,128)(2,1)S(1)}, bf16[2,160,128]{2,1,0:T(8,128)(2,1)S(1)}, u32[]{:S(2)}, u32[]{:S(2)}) collective-permute-start(bf16[2,160,128]{2,1,0:T(8,128)(2,1)S(1)} %pad_maximum_fusion), channel_id=1, source_target_pairs={{0,4},{1,5},{2,6},{3,7},{4,0},{5,1},{6,2},{7,3},{8,12},{9,13},{10,... | collective-permute-start | bytes 245768 | tf_op jit(solution)/shard_map/ppermute | solution.py:92
  12.5 0.9 %collective-permute-done.4.q_ref = bf16[288,128]{1,0:T(8,128)(2,1)S(1)} collective-permute-done((bf16[288,128]{1,0:T(8,128)(2,1)}, bf16[288,128]{1,0:T(8,128)(2,1)S(1)}, u32[]{:S(2)}, u32[]{:S(2)}) %collective-permute-start.4) | collective-permute-done | bytes 73760 | tf_op jit(solution)/shard_map/ppermute | solution.py:97
  13.4 2.0 %collective-permute-done.3 = bf16[2,160,128]{2,1,0:T(8,128)(2,1)S(1)} collective-permute-done((bf16[2,160,128]{2,1,0:T(8,128)(2,1)S(1)}, bf16[2,160,128]{2,1,0:T(8,128)(2,1)S(1)}, u32[]{:S(2)}, u32[]{:S(2)}) %collective-permute-start.3) | collective-permute-done | bytes 81952 | tf_op jit(solution)/shard_map/ppermute | solution.py:92
  15.4 0.4 collective-permute-done.2
  15.8 1.2 %collective-permute-start.6 = (bf16[1,160,128]{2,1,0:T(8,128)(2,1)S(1)}, bf16[1,160,128]{2,1,0:T(8,128)(2,1)S(1)}, u32[]{:S(2)}, u32[]{:S(2)}) collective-permute-start(bf16[1,160,128]{2,1,0:T(8,128)(2,1)S(1)} %slice.34), channel_id=1, source_target_pairs={{0,4},{1,5},{2,6},{3,7},{4,0},{5,1},{6,2},{7,3},{8,12},{9,13},{10,... | collective-permute-start | bytes 122888 | tf_op jit(solution)/shard_map/ppermute | solution.py:92
  17.0 1.2 %collective-permute-start.5 = (bf16[1,160,128]{2,1,0:T(8,128)(2,1)S(1)}, bf16[1,160,128]{2,1,0:T(8,128)(2,1)S(1)}, u32[]{:S(2)}, u32[]{:S(2)}) collective-permute-start(bf16[1,160,128]{2,1,0:T(8,128)(2,1)S(1)} %slice.33), channel_id=1, source_target_pairs={{0,2},{1,3},{2,0},{3,1},{4,6},{5,7},{6,4},{7,5},{8,10},{9,11},{10,... | collective-permute-start | bytes 122888 | tf_op jit(solution)/shard_map/ppermute | solution.py:92
  18.2 2.0 %forward_stencil.1 = (bf16[256,256]{1,0:T(8,128)(2,1)S(1)}, f32[256,256]{1,0:T(8,128)S(1)}, f32[7,15,8,8,128]{4,3,2,1,0:T(8,128)S(1)}) custom-call(s32[1]{0:T(128)} %bitcast.me_ref, f32[2,4,8,8,128]{4,3,2,1,0:T(8,128)S(1)} %get-tuple-element.84.own_ref, bf16[288,128]{1,0:T(8,128)(2,1)S(1)} %collective-permute-done.1.p_ref, ...), custom_call_target="tpu_custom_call" | custom-call | flops 2500000000 | tf_op jit(solution)/shard_map/forward_stencil/pallas_call | solution.py:530
  20.3 0.7 %collective-permute-done.5 = bf16[1,160,128]{2,1,0:T(8,128)(2,1)S(1)} collective-permute-done((bf16[1,160,128]{2,1,0:T(8,128)(2,1)S(1)}, bf16[1,160,128]{2,1,0:T(8,128)(2,1)S(1)}, u32[]{:S(2)}, u32[]{:S(2)}) %collective-permute-start.5) | collective-permute-done | bytes 40992 | tf_op jit(solution)/shard_map/ppermute | solution.py:92
  21.0 0.0 collective-permute-done.6
  21.0 0.1 collective-permute-start.7
  21.1 1.6 %collective-permute-done.7.g1_ref = bf16[8,160,128]{2,1,0:T(8,128)(2,1)S(1)} collective-permute-done((bf16[8,160,128]{2,1,0:T(8,128)(2,1)S(1)}, bf16[8,160,128]{2,1,0:T(8,128)(2,1)S(1)}, u32[]{:S(2)}, u32[]{:S(2)}) %collective-permute-start.7) | collective-permute-done | bytes 327712 | tf_op jit(solution)/shard_map/ppermute | solution.py:92
  22.7 1.2 %pointwise.1 = (f32[256,192]{1,0:T(8,128)S(1)}, bf16[4,8,8,192]{3,2,1,0:T(8,128)(2,1)S(1)}, bf16[288,128]{1,0:T(8,128)(2,1)S(1)}, f32[1280,128]{1,0:T(8,128)S(1)...) custom-call(s32[1]{0:T(128)} %bitcast.me_ref, bf16[8,160,128]{2,1,0:T(8,128)(2,1)S(1)} %constant_dynamic-update-slice_fusion.g0_ref, ...), custom_call_target="tpu_custom_call" | custom-call | flops 2500000000 | tf_op jit(solution)/shard_map/pointwise/pallas_call | solution.py:530
  24.0 0.2 collective-permute-start.11
  24.2 2.0 %kernel_gradient.1 = (f32[272,128]{1,0:T(8,128)S(1)}, bf16[272,128]{1,0:T(8,128)(2,1)S(1)}) custom-call(s32[1]{0:T(128)} %bitcast.me_ref, f32[7,15,8,8,128]{4,3,2,1,0:T(8,128)S(1)} %get-tuple-element.92.s_ref, bf16[4,8,8,192]{3,2,1,0:T(8,128)(2,1)S(1)} %get-tuple-element.99.g_ref, f32[8,256]{1,0:T(8,128)S(1)} %get-tuple-element.100.small_ref), custom_call_target="tpu_custom_call" | custom-call | flops 2000000000 | tf_op jit(solution)/shard_map/kernel_gradient/pallas_call | solution.py:530
  26.2 0.4 collective-permute-start.8
  26.7 3.0 %collective-permute-start.10 = (bf16[288,128]{1,0:T(8,128)(2,1)S(1)}, bf16[288,128]{1,0:T(8,128)(2,1)S(1)}, u32[]{:S(2)}, u32[]{:S(2)}) collective-permute-start(bf16[288,128]{1,0:T(8,128)(2,1)S(1)} %get-tuple-element.105), channel_id=1, source_target_pairs={{0,15},{1,2},{2,1},{3,4},{4,3},{5,6},{6,5},{7,8},{8,7},{9,10},{10,... | collective-permute-start | bytes 221192 | tf_op jit(solution)/shard_map/ppermute | solution.py:97
  29.6 0.0 collective-permute-done.11
  29.6 0.1 convert_add_fusion
  29.7 0.1 collective-permute-start.12
  29.8 0.0 collective-permute-done.8
  29.8 2.1 %collective-permute-start.9 = (bf16[272,128]{1,0:T(8,128)(2,1)S(1)}, bf16[272,128]{1,0:T(8,128)(2,1)S(1)}, u32[]{:S(2)}, u32[]{:S(2)}) collective-permute-start(bf16[272,128]{1,0:T(8,128)(2,1)S(1)} %add_convert_fusion.3), channel_id=1, source_target_pairs={{0,8},{1,9},{2,10},{3,11},{4,12},{5,13},{6,14},{7,15},{8,0},{9,1},... | collective-permute-start | bytes 208904 | tf_op jit(solution)/shard_map/ppermute | solution.py:92
  31.9 1.3 %collective-permute-done.10.q_ref = bf16[288,128]{1,0:T(8,128)(2,1)S(1)} collective-permute-done((bf16[288,128]{1,0:T(8,128)(2,1)S(1)}, bf16[288,128]{1,0:T(8,128)(2,1)S(1)}, u32[]{:S(2)}, u32[]{:S(2)}) %collective-permute-start.10) | collective-permute-done | bytes 73760 | tf_op jit(solution)/shard_map/ppermute | solution.py:97
  33.2 2.6 %collective-permute-done.9 = bf16[272,128]{1,0:T(8,128)(2,1)S(1)} collective-permute-done((bf16[272,128]{1,0:T(8,128)(2,1)S(1)}, bf16[272,128]{1,0:T(8,128)(2,1)S(1)}, u32[]{:S(2)}, u32[]{:S(2)}) %collective-permute-start.9) | collective-permute-done | bytes 69664 | tf_op jit(solution)/shard_map/ppermute | solution.py:92
  35.8 0.0 collective-permute-done.12
  35.9 1.7 %collective-permute-start.13 = (bf16[272,128]{1,0:T(8,128)(2,1)S(1)}, bf16[272,128]{1,0:T(8,128)(2,1)S(1)}, u32[]{:S(2)}, u32[]{:S(2)}) collective-permute-start(bf16[272,128]{1,0:T(8,128)(2,1)S(1)} %add_convert_fusion.2), channel_id=1, source_target_pairs={{0,2},{1,3},{2,0},{3,1},{4,6},{5,7},{6,4},{7,5},{8,10},{9,11},{10,... | collective-permute-start | bytes 208904 | tf_op jit(solution)/shard_map/ppermute | solution.py:92
  37.6 0.1 collective-permute-start.14
  37.7 2.6 %backward_stencil.1 = (bf16[4,8,8,192]{3,2,1,0:T(8,128)(2,1)}, bf16[4,8,8,192]{3,2,1,0:T(8,128)(2,1)}) custom-call(s32[1]{0:T(128)} %bitcast.me_ref, bf16[4,8,8,192]{3,2,1,0:T(8,128)(2,1)S(1)} %get-tuple-element.99.g_ref, bf16[288,128]{1,0:T(8,128)(2,1)S(1)} %slice.45.p_ref, bf16[288,128]{1,0:T(8,128)(2,1)S(1)} %collective-permute-done.10.q_ref, ...), custom_call_target="tpu_custom_call" | custom-call | flops 2500000000 | tf_op jit(solution)/shard_map/backward_stencil/pallas_call | solution.py:530
  40.3 0.0 collective-permute-done.13
  40.3 1.8 %collective-permute-done.14 = bf16[320,128]{1,0:T(8,128)(2,1)S(1)} collective-permute-done((bf16[320,128]{1,0:T(8,128)(2,1)S(1)}, bf16[320,128]{1,0:T(8,128)(2,1)S(1)}, u32[]{:S(2)}, u32[]{:S(2)}) %collective-permute-start.14) | collective-permute-done | bytes 81952 | tf_op jit(solution)/shard_map/ppermute | solution.py:92
  42.2 0.2 collective-permute-start.15
  42.4 2.1 %collective-permute-start.17 = (bf16[160,128]{1,0:T(8,128)(2,1)S(1)}, bf16[160,128]{1,0:T(8,128)(2,1)S(1)}, u32[]{:S(2)}, u32[]{:S(2)}) collective-permute-start(bf16[160,128]{1,0:T(8,128)(2,1)S(1)} %slice.60), channel_id=1, source_target_pairs={{0,8},{1,9},{2,10},{3,11},{4,12},{5,13},{6,14},{7,15},{8,0},{9,1},... | collective-permute-start | bytes 122888 | tf_op jit(solution)/shard_map/ppermute | solution.py:92
  44.5 2.0 %collective-permute-done.15 = bf16[272,128]{1,0:T(8,128)(2,1)S(1)} collective-permute-done((bf16[272,128]{1,0:T(8,128)(2,1)S(1)}, bf16[272,128]{1,0:T(8,128)(2,1)S(1)}, u32[]{:S(2)}, u32[]{:S(2)}) %collective-permute-start.15) | collective-permute-done | bytes 69664 | tf_op jit(solution)/shard_map/ppermute | solution.py:92
  46.6 0.1 collective-permute-start.16
  46.6 0.7 %collective-permute-done.17 = bf16[160,128]{1,0:T(8,128)(2,1)S(1)} collective-permute-done((bf16[160,128]{1,0:T(8,128)(2,1)S(1)}, bf16[160,128]{1,0:T(8,128)(2,1)S(1)}, u32[]{:S(2)}, u32[]{:S(2)}) %collective-permute-start.17) | collective-permute-done | bytes 40992 | tf_op jit(solution)/shard_map/ppermute | solution.py:92
  47.4 0.5 %collective-permute-done.16.other_ref = bf16[272,128]{1,0:T(8,128)(2,1)S(1)} collective-permute-done((bf16[272,128]{1,0:T(8,128)(2,1)S(1)}, bf16[272,128]{1,0:T(8,128)(2,1)S(1)}, u32[]{:S(2)}, u32[]{:S(2)}) %collective-permute-start.16) | collective-permute-done | bytes 69664 | tf_op jit(solution)/shard_map/ppermute | solution.py:92
  47.9 0.9 %final.1 = (f32[7,7,7,192]{3,2,1,0:T(8,128)}, f32[1,192]{1,0:T(1,128)}, f32[1,192]{1,0:T(1,128)}, f32[1,192]{1,0:T(1,128)}, f32[1,192]{1,0:T(1,128)}, /*index=5*...) custom-call(s32[1]{0:T(128)} %bitcast.me_ref, ...), custom_call_target="tpu_custom_call" | custom-call | flops 1000000000 | tf_op jit(solution)/shard_map/final/pallas_call | solution.py:530
  (20 shorter events, 0.3 us)
Async XLA Ops:
  0.6 8.4 %copy-start.1 = (bf16[4,8,8,192]{3,2,1,0:T(8,128)(2,1)S(1)}, bf16[4,8,8,192]{3,2,1,0:T(8,128)(2,1)}, u32[]{:S(2)}) copy-start(bf16[4,8,8,192]{3,2,1,0:T(8,128)(2,1)} %refs_0_.1) | copy-start | bytes 294916
  0.7 8.4 %copy-start.8 = (f32[192]{0:T(256)S(1)}, f32[192]{0:T(256)}, u32[]{:S(2)}) copy-start(f32[192]{0:T(256)} %refs_7_.1) | copy-start | bytes 2308
  0.7 8.4 %copy-start.7 = (f32[192]{0:T(256)S(1)}, f32[192]{0:T(256)}, u32[]{:S(2)}) copy-start(f32[192]{0:T(256)} %refs_6_.1) | copy-start | bytes 2308
  0.7 8.4 %copy-start.6 = (f32[192]{0:T(256)S(1)}, f32[192]{0:T(256)}, u32[]{:S(2)}) copy-start(f32[192]{0:T(256)} %refs_5_.1) | copy-start | bytes 2308
  0.7 8.4 %copy-start.5 = (f32[192]{0:T(256)S(1)}, f32[192]{0:T(256)}, u32[]{:S(2)}) copy-start(f32[192]{0:T(256)} %refs_4_.1) | copy-start | bytes 2308
  0.7 8.4 %copy-start.4 = (f32[192]{0:T(256)S(1)}, f32[192]{0:T(256)}, u32[]{:S(2)}) copy-start(f32[192]{0:T(256)} %refs_3_.1) | copy-start | bytes 2308
  0.7 8.4 %copy-start = (f32[7,7,7,192]{3,2,1,0:T(8,128)S(1)}, f32[7,7,7,192]{3,2,1,0:T(8,128)}, u32[]{:S(2)}) copy-start(f32[7,7,7,192]{3,2,1,0:T(8,128)} %refs_2_.1) | copy-start | bytes 790276
  0.7 8.4 %copy-start.2 = (bf16[4,8,8,192]{3,2,1,0:T(8,128)(2,1)S(1)}, bf16[4,8,8,192]{3,2,1,0:T(8,128)(2,1)}, u32[]{:S(2)}) copy-start(bf16[4,8,8,192]{3,2,1,0:T(8,128)(2,1)} %refs_1_.1) | copy-start | bytes 294916
  2.5 8.3 %collective-permute-start = (bf16[160,128]{1,0:T(8,128)(2,1)}, bf16[160,128]{1,0:T(8,128)(2,1)S(1)}, u32[]{:S(2)}, u32[]{:S(2)}) collective-permute-start(bf16[160,128]{1,0:T(8,128)(2,1)} %get-tuple-element.70.refs_8_), channel_id=1, source_target_pairs={{0,8},{1,9},{2,10},{3,11},{4,12},{5,13},{6,14},{7,15},{8,0},{9,1},... | collective-permute-start | bytes 122888 | tf_op jit(solution)/shard_map/ppermute | solution.py:92
  6.6 4.2 %collective-permute-start.1 = (bf16[288,128]{1,0:T(8,128)(2,1)}, bf16[288,128]{1,0:T(8,128)(2,1)S(1)}, u32[]{:S(2)}, u32[]{:S(2)}) collective-permute-start(bf16[288,128]{1,0:T(8,128)(2,1)} %get-tuple-element.71), channel_id=1, source_target_pairs={{0,1},{1,0},{2,3},{3,2},{4,5},{5,4},{6,7},{7,6},{8,9},{9,8},{10,11... | collective-permute-start | bytes 221192 | tf_op jit(solution)/shard_map/ppermute | solution.py:92
  6.6 6.7 %collective-permute-start.4 = (bf16[288,128]{1,0:T(8,128)(2,1)}, bf16[288,128]{1,0:T(8,128)(2,1)S(1)}, u32[]{:S(2)}, u32[]{:S(2)}) collective-permute-start(bf16[288,128]{1,0:T(8,128)(2,1)} %get-tuple-element.81), channel_id=1, source_target_pairs={{0,15},{1,2},{2,1},{3,4},{4,3},{5,6},{6,5},{7,8},{8,7},{9,10},{10,... | collective-permute-start | bytes 221192 | tf_op jit(solution)/shard_map/ppermute | solution.py:97
  9.1 0.8 %copy-start.3 = (bf16[160,128]{1,0:T(8,128)(2,1)S(1)}, bf16[160,128]{1,0:T(8,128)(2,1)}, u32[]{:S(2)}) copy-start(bf16[160,128]{1,0:T(8,128)(2,1)} %get-tuple-element.70.refs_8_) | copy-start | bytes 122884
  10.9 4.5 %collective-permute-start.3 = (bf16[2,160,128]{2,1,0:T(8,128)(2,1)S(1)}, bf16[2,160,128]{2,1,0:T(8,128)(2,1)S(1)}, u32[]{:S(2)}, u32[]{:S(2)}) collective-permute-start(bf16[2,160,128]{2,1,0:T(8,128)(2,1)S(1)} %pad_maximum_fusion), channel_id=1, source_target_pairs={{0,2},{1,3},{2,0},{3,1},{4,6},{5,7},{6,4},{7,5},{8,10},{9,11},{10,... | collective-permute-start | bytes 245768 | tf_op jit(solution)/shard_map/ppermute | solution.py:92
  11.0 4.8 %collective-permute-start.2 = (bf16[2,160,128]{2,1,0:T(8,128)(2,1)S(1)}, bf16[2,160,128]{2,1,0:T(8,128)(2,1)S(1)}, u32[]{:S(2)}, u32[]{:S(2)}) collective-permute-start(bf16[2,160,128]{2,1,0:T(8,128)(2,1)S(1)} %pad_maximum_fusion), channel_id=1, source_target_pairs={{0,4},{1,5},{2,6},{3,7},{4,0},{5,1},{6,2},{7,3},{8,12},{9,13},{10,... | collective-permute-start | bytes 245768 | tf_op jit(solution)/shard_map/ppermute | solution.py:92
  15.8 5.2 %collective-permute-start.6 = (bf16[1,160,128]{2,1,0:T(8,128)(2,1)S(1)}, bf16[1,160,128]{2,1,0:T(8,128)(2,1)S(1)}, u32[]{:S(2)}, u32[]{:S(2)}) collective-permute-start(bf16[1,160,128]{2,1,0:T(8,128)(2,1)S(1)} %slice.34), channel_id=1, source_target_pairs={{0,4},{1,5},{2,6},{3,7},{4,0},{5,1},{6,2},{7,3},{8,12},{9,13},{10,... | collective-permute-start | bytes 122888 | tf_op jit(solution)/shard_map/ppermute | solution.py:92
  17.0 4.0 %collective-permute-start.5 = (bf16[1,160,128]{2,1,0:T(8,128)(2,1)S(1)}, bf16[1,160,128]{2,1,0:T(8,128)(2,1)S(1)}, u32[]{:S(2)}, u32[]{:S(2)}) collective-permute-start(bf16[1,160,128]{2,1,0:T(8,128)(2,1)S(1)} %slice.33), channel_id=1, source_target_pairs={{0,2},{1,3},{2,0},{3,1},{4,6},{5,7},{6,4},{7,5},{8,10},{9,11},{10,... | collective-permute-start | bytes 122888 | tf_op jit(solution)/shard_map/ppermute | solution.py:92
  21.0 1.7 %collective-permute-start.7 = (bf16[8,160,128]{2,1,0:T(8,128)(2,1)S(1)}, bf16[8,160,128]{2,1,0:T(8,128)(2,1)S(1)}, u32[]{:S(2)}, u32[]{:S(2)}) collective-permute-start(bf16[8,160,128]{2,1,0:T(8,128)(2,1)S(1)} %constant_dynamic-update-slice_fusion.g0_ref), channel_id=1, source_target_pairs={{0,1},{1,0},{2,3},{3,2},{4,5},{5,4},{6,7},{7,6},{8,9},{9,8},{10,11... | collective-permute-start | bytes 983048 | tf_op jit(solution)/shard_map/ppermute | solution.py:92
  24.0 5.7 %collective-permute-start.11 = (bf16[1568,128]{1,0:T(8,128)(2,1)S(1)}, bf16[1568,128]{1,0:T(8,128)(2,1)S(1)}, u32[]{:S(2)}, u32[]{:S(2)}) collective-permute-start(bf16[1568,128]{1,0:T(8,128)(2,1)S(1)} %get-tuple-element.108), channel_id=1, source_target_pairs={{0,1},{1,0},{2,3},{3,2},{4,5},{5,4},{6,7},{7,6},{8,9},{9,8},{10,11... | collective-permute-start | bytes 1204232 | tf_op jit(solution)/shard_map/ppermute | solution.py:92
  26.2 3.6 %collective-permute-start.8 = (bf16[272,128]{1,0:T(8,128)(2,1)S(1)}, bf16[272,128]{1,0:T(8,128)(2,1)S(1)}, u32[]{:S(2)}, u32[]{:S(2)}) collective-permute-start(bf16[272,128]{1,0:T(8,128)(2,1)S(1)} %get-tuple-element.104), channel_id=1, source_target_pairs={{0,1},{1,0},{2,3},{3,2},{4,5},{5,4},{6,7},{7,6},{8,9},{9,8},{10,11... | collective-permute-start | bytes 208904 | tf_op jit(solution)/shard_map/ppermute | solution.py:92
  26.7 6.6 %collective-permute-start.10 = (bf16[288,128]{1,0:T(8,128)(2,1)S(1)}, bf16[288,128]{1,0:T(8,128)(2,1)S(1)}, u32[]{:S(2)}, u32[]{:S(2)}) collective-permute-start(bf16[288,128]{1,0:T(8,128)(2,1)S(1)} %get-tuple-element.105), channel_id=1, source_target_pairs={{0,15},{1,2},{2,1},{3,4},{4,3},{5,6},{6,5},{7,8},{8,7},{9,10},{10,... | collective-permute-start | bytes 221192 | tf_op jit(solution)/shard_map/ppermute | solution.py:97
  29.7 6.1 %collective-permute-start.12 = (bf16[640,128]{1,0:T(8,128)(2,1)S(1)}, bf16[640,128]{1,0:T(8,128)(2,1)S(1)}, u32[]{:S(2)}, u32[]{:S(2)}) collective-permute-start(bf16[640,128]{1,0:T(8,128)(2,1)S(1)} %slice.58), channel_id=1, source_target_pairs={{0,2},{1,3},{2,0},{3,1},{4,6},{5,7},{6,4},{7,5},{8,10},{9,11},{10,... | collective-permute-start | bytes 491528 | tf_op jit(solution)/shard_map/ppermute | solution.py:92
  29.8 6.0 %collective-permute-start.9 = (bf16[272,128]{1,0:T(8,128)(2,1)S(1)}, bf16[272,128]{1,0:T(8,128)(2,1)S(1)}, u32[]{:S(2)}, u32[]{:S(2)}) collective-permute-start(bf16[272,128]{1,0:T(8,128)(2,1)S(1)} %add_convert_fusion.3), channel_id=1, source_target_pairs={{0,8},{1,9},{2,10},{3,11},{4,12},{5,13},{6,14},{7,15},{8,0},{9,1},... | collective-permute-start | bytes 208904 | tf_op jit(solution)/shard_map/ppermute | solution.py:92
  35.9 4.4 %collective-permute-start.13 = (bf16[272,128]{1,0:T(8,128)(2,1)S(1)}, bf16[272,128]{1,0:T(8,128)(2,1)S(1)}, u32[]{:S(2)}, u32[]{:S(2)}) collective-permute-start(bf16[272,128]{1,0:T(8,128)(2,1)S(1)} %add_convert_fusion.2), channel_id=1, source_target_pairs={{0,2},{1,3},{2,0},{3,1},{4,6},{5,7},{6,4},{7,5},{8,10},{9,11},{10,... | collective-permute-start | bytes 208904 | tf_op jit(solution)/shard_map/ppermute | solution.py:92
  37.6 4.5 %collective-permute-start.14 = (bf16[320,128]{1,0:T(8,128)(2,1)S(1)}, bf16[320,128]{1,0:T(8,128)(2,1)S(1)}, u32[]{:S(2)}, u32[]{:S(2)}) collective-permute-start(bf16[320,128]{1,0:T(8,128)(2,1)S(1)} %slice.59), channel_id=1, source_target_pairs={{0,4},{1,5},{2,6},{3,7},{4,0},{5,1},{6,2},{7,3},{8,12},{9,13},{10,... | collective-permute-start | bytes 245768 | tf_op jit(solution)/shard_map/ppermute | solution.py:92
  42.2 4.4 %collective-permute-start.15 = (bf16[272,128]{1,0:T(8,128)(2,1)S(1)}, bf16[272,128]{1,0:T(8,128)(2,1)S(1)}, u32[]{:S(2)}, u32[]{:S(2)}) collective-permute-start(bf16[272,128]{1,0:T(8,128)(2,1)S(1)} %add_convert_fusion.1), channel_id=1, source_target_pairs={{0,4},{1,5},{2,6},{3,7},{4,0},{5,1},{6,2},{7,3},{8,12},{9,13},{10,... | collective-permute-start | bytes 208904 | tf_op jit(solution)/shard_map/ppermute | solution.py:92
  42.4 5.0 %collective-permute-start.17 = (bf16[160,128]{1,0:T(8,128)(2,1)S(1)}, bf16[160,128]{1,0:T(8,128)(2,1)S(1)}, u32[]{:S(2)}, u32[]{:S(2)}) collective-permute-start(bf16[160,128]{1,0:T(8,128)(2,1)S(1)} %slice.60), channel_id=1, source_target_pairs={{0,8},{1,9},{2,10},{3,11},{4,12},{5,13},{6,14},{7,15},{8,0},{9,1},... | collective-permute-start | bytes 122888 | tf_op jit(solution)/shard_map/ppermute | solution.py:92
  46.6 1.3 %collective-permute-start.16 = (bf16[272,128]{1,0:T(8,128)(2,1)S(1)}, bf16[272,128]{1,0:T(8,128)(2,1)S(1)}, u32[]{:S(2)}, u32[]{:S(2)}) collective-permute-start(bf16[272,128]{1,0:T(8,128)(2,1)S(1)} %add_convert_fusion.mine_ref), channel_id=1, source_target_pairs={{0,1},{1,0},{2,3},{3,2},{4,5},{5,4},{6,7},{7,6},{8,9},{9,8},{10,11... | collective-permute-start | bytes 208904 | tf_op jit(solution)/shard_map/ppermute | solution.py:92

commit v5 on v4

--- a/solution.py
+++ b/solution.py
@@ -580,16 +580,14 @@
         + [pltpu.SemaphoreType.DMA((len(given),))],
         HBM,
     )
-    weights, x_core, prepared = lax.optimization_barrier((weights, x_core, prepared))
+    weights, prepared = lax.optimization_barrier((weights, prepared))
     piece, own, taps, vecs, x_f32, cot_f32, d_branch = prepared
     weights = jnp.stack([piece, weights])
     for bit in order[-2:2:-1]:
         weights = jnp.concatenate([weights, swap(weights, bit)], axis=0)
     over_z, over_x = swap(weights, order[2]), swap(weights, order[1])
-    over_z, over_x, x_far = lax.optimization_barrier((over_z, over_x, x_far))
-    n = over_z.shape[0] // 2
-    corner = swap(over_z[:n], order[1]), swap(over_x[n:], order[2])
-    weights = jnp.concatenate([weights, over_z, over_x, *corner], axis=0)
+    over_z, over_x, x_far, x_core = lax.optimization_barrier((over_z, over_x, x_far, x_core))
+    weights = jnp.concatenate([weights, over_z, over_x, swap(over_z, order[1])], axis=0)
     forward = call(
         functools.partial(forward_kernel, devices - 1),
         "forward_stencil",
@@ -643,16 +641,14 @@
     from_core = swap(to_core, 1)
     total = grad_keep + from_core[: pieces * lines].astype(F32)
     g_core = from_core[pieces * lines :]
-    send, to_far = lax.optimization_barrier((send, to_far))
     sums = keep + swap(send, 1).astype(F32)
+    sums, to_far = lax.optimization_barrier((sums, to_far))
     g_far = swap_odd(to_far)
     for step, (bit, sums_bit) in enumerate(zip(order[1:], sums_order[1:])):
         n = total.shape[0] // 2
         mine, kept = sums.astype(BF16), total[:n]
         theirs = swap(mine, sums_bit)
         got = swap(total[n:].astype(BF16), bit)
-        if step == 0:
-            theirs, g_far = lax.optimization_barrier((theirs, g_far))
         if step == len(order) - 3:
             d_x, output = call(
                 functools.partial(back_kernel, devices - 1),

time: 49 us -> 46.6 us (0.951)
  starting transfers between devices: 20.4 us -> 18.9 us
  waiting for transfers between devices: 14.7 us -> 14 us
    ppermute x2, starting transfers between devices: 5.34 us -> 3.18 us  [swap_odd(): lax.ppermute(x, 'space', [(i, (i + 1 if i % 2 else i - 1) % size) for i i...]
    ppermute x2, waiting for transfers between devices: 2.17 us -> 1.03 us  [swap_odd(): lax.ppermute(x, 'space', [(i, (i + 1 if i % 2 else i - 1) % size) for i i...]
    ppermute x16 -> x15, starting transfers between devices: 15.1 us -> 15.7 us  [swap(): return lax.ppermute(x, 'space', [(i, i ^ bit) for i in range(size)])]
    ppermute x16 -> x15, waiting for transfers between devices: 12.5 us -> 13 us  [swap(): return lax.ppermute(x, 'space', [(i, i ^ bit) for i in range(size)])]
  transfers between devices with their start and end apart: 18 -> 17, of which waited for: 11 -> 12; matrix products, arithmetic and copies ran while one was open for 0% -> 1% of each run, Pallas kernels for 16% -> 16%
where the time goes in v5:
time: 46.6 us; the launch traced here: 46.4 us
  starting transfers between devices  18.9 us (41%)
  waiting for transfers between devices  14 us (30%)
  Pallas kernels  11.6 us (25%)
  local copies, waits for them, and re-layouts  0.91 us (2%)
  between operations  0.89 us (2%)
    ppermute x15, starting transfers between devices, swap(): return lax.ppermute(x, 'space', [(i, i ^ bit) for i in range(size)])  15.7 us
    ppermute x15, waiting for transfers between devices, swap(): return lax.ppermute(x, 'space', [(i, i ^ bit) for i in range(size)])  13 us
    pallas_call x7, Pallas kernels, call(): pl.pallas_call(body, out_shape=out_shape, in_specs=specs, out_specs=jax.t...  11.6 us
    ppermute x2, starting transfers between devices, swap_odd(): lax.ppermute(x, 'space', [(i, (i + 1 if i % 2 else i - 1) % size) for i i...  3.18 us
    ppermute x2, waiting for transfers between devices, swap_odd(): lax.ppermute(x, 'space', [(i, (i + 1 if i % 2 else i - 1) % size) for i i...  1.03 us
  transfers between devices with their start and end apart: 17, of which 12 were waited for; matrix products, arithmetic and copies ran while one was open for 1% of the time, Pallas kernels for 16%

profile of v5, /device:TPU:0, one launch (start us, length us, event | category | flops | bytes accessed | tf_op | source)
XLA Modules:
  0.0 46.4 jit_solution(2637186201943797638)
XLA Ops:
  0.6 0.0 copy-start.1
  0.7 0.0 copy-start.8
  0.7 0.0 copy-start.7
  0.7 0.0 copy-start.6
  0.7 0.0 copy-start.5
  0.7 0.0 copy-start.4
  0.7 0.0 copy-start
  0.7 0.0 copy-start.2
  0.7 1.8 %pack.1 = (bf16[160,128]{1,0:T(8,128)(2,1)}, bf16[288,128]{1,0:T(8,128)(2,1)}, bf16[288,128]{1,0:T(8,128)(2,1)}) custom-call(s32[1]{0:T(128)} %bitcast.me_ref, bf16[48,192]{1,0:T(8,128)(2,1)} %wi_hbm.1, bf16[48]{0:T(256)(128)(2,1)} %b_hbm.1, bf16[48,192]{1,0:T(8,128)(2,1)} %wo_hbm.1, bf16[4,8,8,192]{3,2,1,0:T(8,128)(2,1)} %refs_0_.1), custom_call_target="tpu_custom_call" | custom-call | flops 1000000000 | tf_op jit(solution)/shard_map/pack/pallas_call | solution.py:530
  2.5 4.1 %collective-permute-start = (bf16[160,128]{1,0:T(8,128)(2,1)}, bf16[160,128]{1,0:T(8,128)(2,1)S(1)}, u32[]{:S(2)}, u32[]{:S(2)}) collective-permute-start(bf16[160,128]{1,0:T(8,128)(2,1)} %get-tuple-element.68.refs_8_), channel_id=1, source_target_pairs={{0,8},{1,9},{2,10},{3,11},{4,12},{5,13},{6,14},{7,15},{8,0},{9,1},... | collective-permute-start | bytes 122888 | tf_op jit(solution)/shard_map/ppermute | solution.py:92
  6.6 1.5 %collective-permute-start.3 = (bf16[288,128]{1,0:T(8,128)(2,1)}, bf16[288,128]{1,0:T(8,128)(2,1)S(1)}, u32[]{:S(2)}, u32[]{:S(2)}) collective-permute-start(bf16[288,128]{1,0:T(8,128)(2,1)} %get-tuple-element.78), channel_id=1, source_target_pairs={{0,15},{1,2},{2,1},{3,4},{4,3},{5,6},{6,5},{7,8},{8,7},{9,10},{10,... | collective-permute-start | bytes 221192 | tf_op jit(solution)/shard_map/ppermute | solution.py:97
  8.1 0.1 collective-permute-start.4
  8.2 0.0 copy-done.1
  8.2 0.0 copy-done.8
  8.2 0.0 copy-done.7
  8.2 0.0 copy-done.6
  8.3 0.0 copy-done.5
  8.3 0.0 copy-done.4
  8.3 0.0 copy-done
  8.3 0.0 copy-done.2
  8.3 0.0 copy-start.3
  8.3 0.8 %copy-done.3 = bf16[160,128]{1,0:T(8,128)(2,1)S(1)} copy-done((bf16[160,128]{1,0:T(8,128)(2,1)S(1)}, bf16[160,128]{1,0:T(8,128)(2,1)}, u32[]{:S(2)}) %copy-start.3) | copy-done | bytes 40984
  9.1 1.0 %prepare.1 = (bf16[160,128]{1,0:T(8,128)(2,1)S(1)}, f32[2,4,8,8,128]{4,3,2,1,0:T(8,128)S(1)}, f32[16,7,8,128]{3,2,1,0:T(8,128)S(1)}, f32[8,192]{1,0:T(8,128)S(1)...) custom-call(bf16[4,8,8,192]{3,2,1,0:T(8,128)(2,1)S(1)} %copy-done.1, ...), custom_call_target="tpu_custom_call" | custom-call | flops 1000000000 | tf_op jit(solution)/shard_map/prepare/pallas_call | solution.py:530
  10.1 0.0 collective-permute-done
  10.1 1.6 %collective-permute-start.2 = (bf16[2,160,128]{2,1,0:T(8,128)(2,1)S(1)}, bf16[2,160,128]{2,1,0:T(8,128)(2,1)S(1)}, u32[]{:S(2)}, u32[]{:S(2)}) collective-permute-start(bf16[2,160,128]{2,1,0:T(8,128)(2,1)S(1)} %pad_maximum_fusion), channel_id=1, source_target_pairs={{0,2},{1,3},{2,0},{3,1},{4,6},{5,7},{6,4},{7,5},{8,10},{9,11},{10,... | collective-permute-start | bytes 245768 | tf_op jit(solution)/shard_map/ppermute | solution.py:92
  11.7 0.8 %collective-permute-start.1 = (bf16[2,160,128]{2,1,0:T(8,128)(2,1)S(1)}, bf16[2,160,128]{2,1,0:T(8,128)(2,1)S(1)}, u32[]{:S(2)}, u32[]{:S(2)}) collective-permute-start(bf16[2,160,128]{2,1,0:T(8,128)(2,1)S(1)} %pad_maximum_fusion), channel_id=1, source_target_pairs={{0,4},{1,5},{2,6},{3,7},{4,0},{5,1},{6,2},{7,3},{8,12},{9,13},{10,... | collective-permute-start | bytes 245768 | tf_op jit(solution)/shard_map/ppermute | solution.py:92
  12.5 0.8 %collective-permute-done.3.q_ref = bf16[288,128]{1,0:T(8,128)(2,1)S(1)} collective-permute-done((bf16[288,128]{1,0:T(8,128)(2,1)}, bf16[288,128]{1,0:T(8,128)(2,1)S(1)}, u32[]{:S(2)}, u32[]{:S(2)}) %collective-permute-start.3) | collective-permute-done | bytes 73760 | tf_op jit(solution)/shard_map/ppermute | solution.py:97
  13.3 0.0 collective-permute-done.4.p_ref
  13.3 1.7 %collective-permute-done.2 = bf16[2,160,128]{2,1,0:T(8,128)(2,1)S(1)} collective-permute-done((bf16[2,160,128]{2,1,0:T(8,128)(2,1)S(1)}, bf16[2,160,128]{2,1,0:T(8,128)(2,1)S(1)}, u32[]{:S(2)}, u32[]{:S(2)}) %collective-permute-start.2) | collective-permute-done | bytes 81952 | tf_op jit(solution)/shard_map/ppermute | solution.py:92
  15.1 1.1 %collective-permute-done.1 = bf16[2,160,128]{2,1,0:T(8,128)(2,1)S(1)} collective-permute-done((bf16[2,160,128]{2,1,0:T(8,128)(2,1)S(1)}, bf16[2,160,128]{2,1,0:T(8,128)(2,1)S(1)}, u32[]{:S(2)}, u32[]{:S(2)}) %collective-permute-start.1) | collective-permute-done | bytes 81952 | tf_op jit(solution)/shard_map/ppermute | solution.py:92
  16.2 0.5 %collective-permute-start.5 = (bf16[2,160,128]{2,1,0:T(8,128)(2,1)S(1)}, bf16[2,160,128]{2,1,0:T(8,128)(2,1)S(1)}, u32[]{:S(2)}, u32[]{:S(2)}) collective-permute-start(bf16[2,160,128]{2,1,0:T(8,128)(2,1)S(1)} %collective-permute-done.1), channel_id=1, source_target_pairs={{0,2},{1,3},{2,0},{3,1},{4,6},{5,7},{6,4},{7,5},{8,10},{9,11},{10,... | collective-permute-start | bytes 245768 | tf_op jit(solution)/shard_map/ppermute | solution.py:92
  16.7 2.0 %forward_stencil.1 = (bf16[256,256]{1,0:T(8,128)(2,1)S(1)}, f32[256,256]{1,0:T(8,128)S(1)}, f32[7,15,8,8,128]{4,3,2,1,0:T(8,128)S(1)}) custom-call(s32[1]{0:T(128)} %bitcast.me_ref, f32[2,4,8,8,128]{4,3,2,1,0:T(8,128)S(1)} %get-tuple-element.82.own_ref, bf16[288,128]{1,0:T(8,128)(2,1)S(1)} %collective-permute-done.4.p_ref, ...), custom_call_target="tpu_custom_call" | custom-call | flops 2500000000 | tf_op jit(solution)/shard_map/forward_stencil/pallas_call | solution.py:530
  18.7 1.9 %collective-permute-done.5 = bf16[2,160,128]{2,1,0:T(8,128)(2,1)S(1)} collective-permute-done((bf16[2,160,128]{2,1,0:T(8,128)(2,1)S(1)}, bf16[2,160,128]{2,1,0:T(8,128)(2,1)S(1)}, u32[]{:S(2)}, u32[]{:S(2)}) %collective-permute-start.5) | collective-permute-done | bytes 81952 | tf_op jit(solution)/shard_map/ppermute | solution.py:92
  20.6 0.1 collective-permute-start.6
  20.7 1.6 %collective-permute-done.6.g1_ref = bf16[8,160,128]{2,1,0:T(8,128)(2,1)S(1)} collective-permute-done((bf16[8,160,128]{2,1,0:T(8,128)(2,1)S(1)}, bf16[8,160,128]{2,1,0:T(8,128)(2,1)S(1)}, u32[]{:S(2)}, u32[]{:S(2)}) %collective-permute-start.6) | collective-permute-done | bytes 327712 | tf_op jit(solution)/shard_map/ppermute | solution.py:92
  22.3 1.2 %pointwise.1 = (f32[256,192]{1,0:T(8,128)S(1)}, bf16[4,8,8,192]{3,2,1,0:T(8,128)(2,1)S(1)}, bf16[288,128]{1,0:T(8,128)(2,1)S(1)}, f32[1280,128]{1,0:T(8,128)S(1)...) custom-call(s32[1]{0:T(128)} %bitcast.me_ref, bf16[8,160,128]{2,1,0:T(8,128)(2,1)S(1)} %constant_dynamic-update-slice_fusion.g0_ref, ...), custom_call_target="tpu_custom_call" | custom-call | flops 2500000000 | tf_op jit(solution)/shard_map/pointwise/pallas_call | solution.py:530
  23.5 0.2 collective-permute-start.9
  23.7 2.0 %kernel_gradient.1 = (f32[272,128]{1,0:T(8,128)S(1)}, bf16[272,128]{1,0:T(8,128)(2,1)S(1)}) custom-call(s32[1]{0:T(128)} %bitcast.me_ref, f32[7,15,8,8,128]{4,3,2,1,0:T(8,128)S(1)} %get-tuple-element.90.s_ref, bf16[4,8,8,192]{3,2,1,0:T(8,128)(2,1)S(1)} %get-tuple-element.97.g_ref, f32[8,256]{1,0:T(8,128)S(1)} %get-tuple-element.98.small_ref), custom_call_target="tpu_custom_call" | custom-call | flops 2000000000 | tf_op jit(solution)/shard_map/kernel_gradient/pallas_call | solution.py:530
  25.8 0.4 collective-permute-start.7
  26.2 0.0 collective-permute-done.9
  26.2 0.1 convert_add_fusion
  26.3 0.6 %collective-permute-start.10 = (bf16[640,128]{1,0:T(8,128)(2,1)S(1)}, bf16[640,128]{1,0:T(8,128)(2,1)S(1)}, u32[]{:S(2)}, u32[]{:S(2)}) collective-permute-start(bf16[640,128]{1,0:T(8,128)(2,1)S(1)} %slice.50), channel_id=1, source_target_pairs={{0,2},{1,3},{2,0},{3,1},{4,6},{5,7},{6,4},{7,5},{8,10},{9,11},{10,... | collective-permute-start | bytes 491528 | tf_op jit(solution)/shard_map/ppermute | solution.py:92
  26.9 0.3 collective-permute-done.7
  27.2 2.1 %collective-permute-start.8 = (bf16[272,128]{1,0:T(8,128)(2,1)S(1)}, bf16[272,128]{1,0:T(8,128)(2,1)S(1)}, u32[]{:S(2)}, u32[]{:S(2)}) collective-permute-start(bf16[272,128]{1,0:T(8,128)(2,1)S(1)} %convert_add_fusion.1), channel_id=1, source_target_pairs={{0,8},{1,9},{2,10},{3,11},{4,12},{5,13},{6,14},{7,15},{8,0},{9,1},... | collective-permute-start | bytes 208904 | tf_op jit(solution)/shard_map/ppermute | solution.py:92
  29.2 1.7 %collective-permute-start.12 = (bf16[288,128]{1,0:T(8,128)(2,1)S(1)}, bf16[288,128]{1,0:T(8,128)(2,1)S(1)}, u32[]{:S(2)}, u32[]{:S(2)}) collective-permute-start(bf16[288,128]{1,0:T(8,128)(2,1)S(1)} %get-tuple-element.106), channel_id=1, source_target_pairs={{0,15},{1,2},{2,1},{3,4},{4,3},{5,6},{6,5},{7,8},{8,7},{9,10},{10,... | collective-permute-start | bytes 221192 | tf_op jit(solution)/shard_map/ppermute | solution.py:97
  31.0 3.2 %collective-permute-done.8 = bf16[272,128]{1,0:T(8,128)(2,1)S(1)} collective-permute-done((bf16[272,128]{1,0:T(8,128)(2,1)S(1)}, bf16[272,128]{1,0:T(8,128)(2,1)S(1)}, u32[]{:S(2)}, u32[]{:S(2)}) %collective-permute-start.8) | collective-permute-done | bytes 69664 | tf_op jit(solution)/shard_map/ppermute | solution.py:92
  34.2 0.0 collective-permute-done.10
  34.2 0.8 %collective-permute-start.11 = (bf16[272,128]{1,0:T(8,128)(2,1)S(1)}, bf16[272,128]{1,0:T(8,128)(2,1)S(1)}, u32[]{:S(2)}, u32[]{:S(2)}) collective-permute-start(bf16[272,128]{1,0:T(8,128)(2,1)S(1)} %add_convert_fusion.2), channel_id=1, source_target_pairs={{0,2},{1,3},{2,0},{3,1},{4,6},{5,7},{6,4},{7,5},{8,10},{9,11},{10,... | collective-permute-start | bytes 208904 | tf_op jit(solution)/shard_map/ppermute | solution.py:92
  35.1 0.4 collective-permute-start.13
  35.5 0.2 collective-permute-done.12.q_ref
  35.7 2.6 %backward_stencil.1 = (bf16[4,8,8,192]{3,2,1,0:T(8,128)(2,1)}, bf16[4,8,8,192]{3,2,1,0:T(8,128)(2,1)}) custom-call(s32[1]{0:T(128)} %bitcast.me_ref, bf16[4,8,8,192]{3,2,1,0:T(8,128)(2,1)S(1)} %get-tuple-element.97.g_ref, bf16[288,128]{1,0:T(8,128)(2,1)S(1)} %slice.37.p_ref, bf16[288,128]{1,0:T(8,128)(2,1)S(1)} %collective-permute-done.12.q_ref, ...), custom_call_target="tpu_custom_call" | custom-call | flops 2500000000 | tf_op jit(solution)/shard_map/backward_stencil/pallas_call | solution.py:530
  38.3 0.3 collective-permute-done.11
  38.6 1.0 %collective-permute-done.13 = bf16[320,128]{1,0:T(8,128)(2,1)S(1)} collective-permute-done((bf16[320,128]{1,0:T(8,128)(2,1)S(1)}, bf16[320,128]{1,0:T(8,128)(2,1)S(1)}, u32[]{:S(2)}, u32[]{:S(2)}) %collective-permute-start.13) | collective-permute-done | bytes 81952 | tf_op jit(solution)/shard_map/ppermute | solution.py:92
  39.6 0.4 collective-permute-start.14
  40.1 3.4 %collective-permute-start.16 = (bf16[160,128]{1,0:T(8,128)(2,1)S(1)}, bf16[160,128]{1,0:T(8,128)(2,1)S(1)}, u32[]{:S(2)}, u32[]{:S(2)}) collective-permute-start(bf16[160,128]{1,0:T(8,128)(2,1)S(1)} %slice.52), channel_id=1, source_target_pairs={{0,8},{1,9},{2,10},{3,11},{4,12},{5,13},{6,14},{7,15},{8,0},{9,1},... | collective-permute-start | bytes 122888 | tf_op jit(solution)/shard_map/ppermute | solution.py:92
  43.6 0.6 %collective-permute-done.14 = bf16[272,128]{1,0:T(8,128)(2,1)S(1)} collective-permute-done((bf16[272,128]{1,0:T(8,128)(2,1)S(1)}, bf16[272,128]{1,0:T(8,128)(2,1)S(1)}, u32[]{:S(2)}, u32[]{:S(2)}) %collective-permute-start.14) | collective-permute-done | bytes 69664 | tf_op jit(solution)/shard_map/ppermute | solution.py:92
  44.2 0.1 collective-permute-start.15
  44.3 1.3 %collective-permute-done.16 = bf16[160,128]{1,0:T(8,128)(2,1)S(1)} collective-permute-done((bf16[160,128]{1,0:T(8,128)(2,1)S(1)}, bf16[160,128]{1,0:T(8,128)(2,1)S(1)}, u32[]{:S(2)}, u32[]{:S(2)}) %collective-permute-start.16) | collective-permute-done | bytes 40992 | tf_op jit(solution)/shard_map/ppermute | solution.py:92
  45.5 0.0 collective-permute-done.15.other_ref
  45.6 0.9 %final.1 = (f32[7,7,7,192]{3,2,1,0:T(8,128)}, f32[1,192]{1,0:T(1,128)}, f32[1,192]{1,0:T(1,128)}, f32[1,192]{1,0:T(1,128)}, f32[1,192]{1,0:T(1,128)}, /*index=5*...) custom-call(s32[1]{0:T(128)} %bitcast.me_ref, ...), custom_call_target="tpu_custom_call" | custom-call | flops 1000000000 | tf_op jit(solution)/shard_map/final/pallas_call | solution.py:530
  (17 shorter events, 0.3 us)
Async XLA Ops:
  0.6 7.6 %copy-start.1 = (bf16[4,8,8,192]{3,2,1,0:T(8,128)(2,1)S(1)}, bf16[4,8,8,192]{3,2,1,0:T(8,128)(2,1)}, u32[]{:S(2)}) copy-start(bf16[4,8,8,192]{3,2,1,0:T(8,128)(2,1)} %refs_0_.1) | copy-start | bytes 294916
  0.7 7.6 %copy-start.8 = (f32[192]{0:T(256)S(1)}, f32[192]{0:T(256)}, u32[]{:S(2)}) copy-start(f32[192]{0:T(256)} %refs_7_.1) | copy-start | bytes 2308
  0.7 7.6 %copy-start.7 = (f32[192]{0:T(256)S(1)}, f32[192]{0:T(256)}, u32[]{:S(2)}) copy-start(f32[192]{0:T(256)} %refs_6_.1) | copy-start | bytes 2308
  0.7 7.6 %copy-start.6 = (f32[192]{0:T(256)S(1)}, f32[192]{0:T(256)}, u32[]{:S(2)}) copy-start(f32[192]{0:T(256)} %refs_5_.1) | copy-start | bytes 2308
  0.7 7.6 %copy-start.5 = (f32[192]{0:T(256)S(1)}, f32[192]{0:T(256)}, u32[]{:S(2)}) copy-start(f32[192]{0:T(256)} %refs_4_.1) | copy-start | bytes 2308
  0.7 7.6 %copy-start.4 = (f32[192]{0:T(256)S(1)}, f32[192]{0:T(256)}, u32[]{:S(2)}) copy-start(f32[192]{0:T(256)} %refs_3_.1) | copy-start | bytes 2308
  0.7 7.6 %copy-start = (f32[7,7,7,192]{3,2,1,0:T(8,128)S(1)}, f32[7,7,7,192]{3,2,1,0:T(8,128)}, u32[]{:S(2)}) copy-start(f32[7,7,7,192]{3,2,1,0:T(8,128)} %refs_2_.1) | copy-start | bytes 790276
  0.7 7.6 %copy-start.2 = (bf16[4,8,8,192]{3,2,1,0:T(8,128)(2,1)S(1)}, bf16[4,8,8,192]{3,2,1,0:T(8,128)(2,1)}, u32[]{:S(2)}) copy-start(bf16[4,8,8,192]{3,2,1,0:T(8,128)(2,1)} %refs_1_.1) | copy-start | bytes 294916
  2.5 7.5 %collective-permute-start = (bf16[160,128]{1,0:T(8,128)(2,1)}, bf16[160,128]{1,0:T(8,128)(2,1)S(1)}, u32[]{:S(2)}, u32[]{:S(2)}) collective-permute-start(bf16[160,128]{1,0:T(8,128)(2,1)} %get-tuple-element.68.refs_8_), channel_id=1, source_target_pairs={{0,8},{1,9},{2,10},{3,11},{4,12},{5,13},{6,14},{7,15},{8,0},{9,1},... | collective-permute-start | bytes 122888 | tf_op jit(solution)/shard_map/ppermute | solution.py:92
  6.6 6.7 %collective-permute-start.3 = (bf16[288,128]{1,0:T(8,128)(2,1)}, bf16[288,128]{1,0:T(8,128)(2,1)S(1)}, u32[]{:S(2)}, u32[]{:S(2)}) collective-permute-start(bf16[288,128]{1,0:T(8,128)(2,1)} %get-tuple-element.78), channel_id=1, source_target_pairs={{0,15},{1,2},{2,1},{3,4},{4,3},{5,6},{6,5},{7,8},{8,7},{9,10},{10,... | collective-permute-start | bytes 221192 | tf_op jit(solution)/shard_map/ppermute | solution.py:97
  8.1 5.2 %collective-permute-start.4 = (bf16[288,128]{1,0:T(8,128)(2,1)}, bf16[288,128]{1,0:T(8,128)(2,1)S(1)}, u32[]{:S(2)}, u32[]{:S(2)}) collective-permute-start(bf16[288,128]{1,0:T(8,128)(2,1)} %get-tuple-element.79), channel_id=1, source_target_pairs={{0,1},{1,0},{2,3},{3,2},{4,5},{5,4},{6,7},{7,6},{8,9},{9,8},{10,11... | collective-permute-start | bytes 221192 | tf_op jit(solution)/shard_map/ppermute | solution.py:92
  8.3 0.8 %copy-start.3 = (bf16[160,128]{1,0:T(8,128)(2,1)S(1)}, bf16[160,128]{1,0:T(8,128)(2,1)}, u32[]{:S(2)}) copy-start(bf16[160,128]{1,0:T(8,128)(2,1)} %get-tuple-element.68.refs_8_) | copy-start | bytes 122884
  10.1 5.0 %collective-permute-start.2 = (bf16[2,160,128]{2,1,0:T(8,128)(2,1)S(1)}, bf16[2,160,128]{2,1,0:T(8,128)(2,1)S(1)}, u32[]{:S(2)}, u32[]{:S(2)}) collective-permute-start(bf16[2,160,128]{2,1,0:T(8,128)(2,1)S(1)} %pad_maximum_fusion), channel_id=1, source_target_pairs={{0,2},{1,3},{2,0},{3,1},{4,6},{5,7},{6,4},{7,5},{8,10},{9,11},{10,... | collective-permute-start | bytes 245768 | tf_op jit(solution)/shard_map/ppermute | solution.py:92
  11.7 4.4 %collective-permute-start.1 = (bf16[2,160,128]{2,1,0:T(8,128)(2,1)S(1)}, bf16[2,160,128]{2,1,0:T(8,128)(2,1)S(1)}, u32[]{:S(2)}, u32[]{:S(2)}) collective-permute-start(bf16[2,160,128]{2,1,0:T(8,128)(2,1)S(1)} %pad_maximum_fusion), channel_id=1, source_target_pairs={{0,4},{1,5},{2,6},{3,7},{4,0},{5,1},{6,2},{7,3},{8,12},{9,13},{10,... | collective-permute-start | bytes 245768 | tf_op jit(solution)/shard_map/ppermute | solution.py:92
  16.2 4.4 %collective-permute-start.5 = (bf16[2,160,128]{2,1,0:T(8,128)(2,1)S(1)}, bf16[2,160,128]{2,1,0:T(8,128)(2,1)S(1)}, u32[]{:S(2)}, u32[]{:S(2)}) collective-permute-start(bf16[2,160,128]{2,1,0:T(8,128)(2,1)S(1)} %collective-permute-done.1), channel_id=1, source_target_pairs={{0,2},{1,3},{2,0},{3,1},{4,6},{5,7},{6,4},{7,5},{8,10},{9,11},{10,... | collective-permute-start | bytes 245768 | tf_op jit(solution)/shard_map/ppermute | solution.py:92
  20.6 1.7 %collective-permute-start.6 = (bf16[8,160,128]{2,1,0:T(8,128)(2,1)S(1)}, bf16[8,160,128]{2,1,0:T(8,128)(2,1)S(1)}, u32[]{:S(2)}, u32[]{:S(2)}) collective-permute-start(bf16[8,160,128]{2,1,0:T(8,128)(2,1)S(1)} %constant_dynamic-update-slice_fusion.g0_ref), channel_id=1, source_target_pairs={{0,1},{1,0},{2,3},{3,2},{4,5},{5,4},{6,7},{7,6},{8,9},{9,8},{10,11... | collective-permute-start | bytes 983048 | tf_op jit(solution)/shard_map/ppermute | solution.py:92
  23.5 2.7 %collective-permute-start.9 = (bf16[1568,128]{1,0:T(8,128)(2,1)S(1)}, bf16[1568,128]{1,0:T(8,128)(2,1)S(1)}, u32[]{:S(2)}, u32[]{:S(2)}) collective-permute-start(bf16[1568,128]{1,0:T(8,128)(2,1)S(1)} %get-tuple-element.104), channel_id=1, source_target_pairs={{0,1},{1,0},{2,3},{3,2},{4,5},{5,4},{6,7},{7,6},{8,9},{9,8},{10,11... | collective-permute-start | bytes 1204232 | tf_op jit(solution)/shard_map/ppermute | solution.py:92
  25.8 1.3 %collective-permute-start.7 = (bf16[272,128]{1,0:T(8,128)(2,1)S(1)}, bf16[272,128]{1,0:T(8,128)(2,1)S(1)}, u32[]{:S(2)}, u32[]{:S(2)}) collective-permute-start(bf16[272,128]{1,0:T(8,128)(2,1)S(1)} %get-tuple-element.100), channel_id=1, source_target_pairs={{0,1},{1,0},{2,3},{3,2},{4,5},{5,4},{6,7},{7,6},{8,9},{9,8},{10,11... | collective-permute-start | bytes 208904 | tf_op jit(solution)/shard_map/ppermute | solution.py:92
  26.3 7.8 %collective-permute-start.10 = (bf16[640,128]{1,0:T(8,128)(2,1)S(1)}, bf16[640,128]{1,0:T(8,128)(2,1)S(1)}, u32[]{:S(2)}, u32[]{:S(2)}) collective-permute-start(bf16[640,128]{1,0:T(8,128)(2,1)S(1)} %slice.50), channel_id=1, source_target_pairs={{0,2},{1,3},{2,0},{3,1},{4,6},{5,7},{6,4},{7,5},{8,10},{9,11},{10,... | collective-permute-start | bytes 491528 | tf_op jit(solution)/shard_map/ppermute | solution.py:92
  27.2 7.0 %collective-permute-start.8 = (bf16[272,128]{1,0:T(8,128)(2,1)S(1)}, bf16[272,128]{1,0:T(8,128)(2,1)S(1)}, u32[]{:S(2)}, u32[]{:S(2)}) collective-permute-start(bf16[272,128]{1,0:T(8,128)(2,1)S(1)} %convert_add_fusion.1), channel_id=1, source_target_pairs={{0,8},{1,9},{2,10},{3,11},{4,12},{5,13},{6,14},{7,15},{8,0},{9,1},... | collective-permute-start | bytes 208904 | tf_op jit(solution)/shard_map/ppermute | solution.py:92
  29.2 6.5 %collective-permute-start.12 = (bf16[288,128]{1,0:T(8,128)(2,1)S(1)}, bf16[288,128]{1,0:T(8,128)(2,1)S(1)}, u32[]{:S(2)}, u32[]{:S(2)}) collective-permute-start(bf16[288,128]{1,0:T(8,128)(2,1)S(1)} %get-tuple-element.106), channel_id=1, source_target_pairs={{0,15},{1,2},{2,1},{3,4},{4,3},{5,6},{6,5},{7,8},{8,7},{9,10},{10,... | collective-permute-start | bytes 221192 | tf_op jit(solution)/shard_map/ppermute | solution.py:97
  34.2 4.4 %collective-permute-start.11 = (bf16[272,128]{1,0:T(8,128)(2,1)S(1)}, bf16[272,128]{1,0:T(8,128)(2,1)S(1)}, u32[]{:S(2)}, u32[]{:S(2)}) collective-permute-start(bf16[272,128]{1,0:T(8,128)(2,1)S(1)} %add_convert_fusion.2), channel_id=1, source_target_pairs={{0,2},{1,3},{2,0},{3,1},{4,6},{5,7},{6,4},{7,5},{8,10},{9,11},{10,... | collective-permute-start | bytes 208904 | tf_op jit(solution)/shard_map/ppermute | solution.py:92
  35.1 4.5 %collective-permute-start.13 = (bf16[320,128]{1,0:T(8,128)(2,1)S(1)}, bf16[320,128]{1,0:T(8,128)(2,1)S(1)}, u32[]{:S(2)}, u32[]{:S(2)}) collective-permute-start(bf16[320,128]{1,0:T(8,128)(2,1)S(1)} %slice.51), channel_id=1, source_target_pairs={{0,4},{1,5},{2,6},{3,7},{4,0},{5,1},{6,2},{7,3},{8,12},{9,13},{10,... | collective-permute-start | bytes 245768 | tf_op jit(solution)/shard_map/ppermute | solution.py:92
  39.6 4.5 %collective-permute-start.14 = (bf16[272,128]{1,0:T(8,128)(2,1)S(1)}, bf16[272,128]{1,0:T(8,128)(2,1)S(1)}, u32[]{:S(2)}, u32[]{:S(2)}) collective-permute-start(bf16[272,128]{1,0:T(8,128)(2,1)S(1)} %add_convert_fusion.1), channel_id=1, source_target_pairs={{0,4},{1,5},{2,6},{3,7},{4,0},{5,1},{6,2},{7,3},{8,12},{9,13},{10,... | collective-permute-start | bytes 208904 | tf_op jit(solution)/shard_map/ppermute | solution.py:92
  40.1 5.4 %collective-permute-start.16 = (bf16[160,128]{1,0:T(8,128)(2,1)S(1)}, bf16[160,128]{1,0:T(8,128)(2,1)S(1)}, u32[]{:S(2)}, u32[]{:S(2)}) collective-permute-start(bf16[160,128]{1,0:T(8,128)(2,1)S(1)} %slice.52), channel_id=1, source_target_pairs={{0,8},{1,9},{2,10},{3,11},{4,12},{5,13},{6,14},{7,15},{8,0},{9,1},... | collective-permute-start | bytes 122888 | tf_op jit(solution)/shard_map/ppermute | solution.py:92
  44.2 1.4 %collective-permute-start.15 = (bf16[272,128]{1,0:T(8,128)(2,1)S(1)}, bf16[272,128]{1,0:T(8,128)(2,1)S(1)}, u32[]{:S(2)}, u32[]{:S(2)}) collective-permute-start(bf16[272,128]{1,0:T(8,128)(2,1)S(1)} %add_convert_fusion.mine_ref), channel_id=1, source_target_pairs={{0,1},{1,0},{2,3},{3,2},{4,5},{5,4},{6,7},{7,6},{8,9},{9,8},{10,11... | collective-permute-start | bytes 208904 | tf_op jit(solution)/shard_map/ppermute | solution.py:92

commit v6 on v5

--- a/solution.py
+++ b/solution.py
@@ -659,12 +659,12 @@
                 (me, d_mixed, g_core, g_far, taps, cot_f32, x_f32, branch),
                 [z_scratch, pltpu.VMEM(shifts, F32), u_scratch],
             )
-            theirs, d_x, output = lax.optimization_barrier((theirs, d_x, output))
         if step < len(order) - 2:
             theirs, got = lax.optimization_barrier((theirs, got))
         sums = mine.astype(F32) + theirs.astype(F32)
         total = kept + got.astype(F32)
     mine = sums.astype(BF16)
+    mine, d_x, output = lax.optimization_barrier((mine, d_x, output))
     other = swap(mine, 1)
     total = lax.optimization_barrier(kept + got.astype(F32))
     d_kernel, *vectors, d_w_in, d_b_in, d_w_out = call(

time: 46.6 us -> 46.6 us (level)
  no operation moved by 1% of the time
where the time goes in v6:
time: 46.6 us; the launch traced here: 46.4 us
  starting transfers between devices  18.9 us (41%)
  waiting for transfers between devices  14 us (30%)
  Pallas kernels  11.6 us (25%)
  local copies, waits for them, and re-layouts  0.91 us (2%)
  between operations  0.89 us (2%)
    ppermute x15, starting transfers between devices, swap(): return lax.ppermute(x, 'space', [(i, i ^ bit) for i in range(size)])  15.7 us
    ppermute x15, waiting for transfers between devices, swap(): return lax.ppermute(x, 'space', [(i, i ^ bit) for i in range(size)])  13 us
    pallas_call x7, Pallas kernels, call(): pl.pallas_call(body, out_shape=out_shape, in_specs=specs, out_specs=jax.t...  11.6 us
    ppermute x2, starting transfers between devices, swap_odd(): lax.ppermute(x, 'space', [(i, (i + 1 if i % 2 else i - 1) % size) for i i...  3.18 us
    ppermute x2, waiting for transfers between devices, swap_odd(): lax.ppermute(x, 'space', [(i, (i + 1 if i % 2 else i - 1) % size) for i i...  1.03 us
  transfers between devices with their start and end apart: 17, of which 12 were waited for; matrix products, arithmetic and copies ran while one was open for 1% of the time, Pallas kernels for 16%

profile of v6, /device:TPU:0, one launch (start us, length us, event | category | flops | bytes accessed | tf_op | source)
XLA Modules:
  0.0 46.4 jit_solution(13288901080718017384)
XLA Ops:
  0.6 0.0 copy-start.1
  0.7 0.0 copy-start.8
  0.7 0.0 copy-start.7
  0.7 0.0 copy-start.6
  0.7 0.0 copy-start.5
  0.7 0.0 copy-start.4
  0.7 0.0 copy-start
  0.7 0.0 copy-start.2
  0.7 1.8 %pack.1 = (bf16[160,128]{1,0:T(8,128)(2,1)}, bf16[288,128]{1,0:T(8,128)(2,1)}, bf16[288,128]{1,0:T(8,128)(2,1)}) custom-call(s32[1]{0:T(128)} %bitcast.me_ref, bf16[48,192]{1,0:T(8,128)(2,1)} %wi_hbm.1, bf16[48]{0:T(256)(128)(2,1)} %b_hbm.1, bf16[48,192]{1,0:T(8,128)(2,1)} %wo_hbm.1, bf16[4,8,8,192]{3,2,1,0:T(8,128)(2,1)} %refs_0_.1), custom_call_target="tpu_custom_call" | custom-call | flops 1000000000 | tf_op jit(solution)/shard_map/pack/pallas_call | solution.py:530
  2.5 4.1 %collective-permute-start = (bf16[160,128]{1,0:T(8,128)(2,1)}, bf16[160,128]{1,0:T(8,128)(2,1)S(1)}, u32[]{:S(2)}, u32[]{:S(2)}) collective-permute-start(bf16[160,128]{1,0:T(8,128)(2,1)} %get-tuple-element.68.refs_8_), channel_id=1, source_target_pairs={{0,8},{1,9},{2,10},{3,11},{4,12},{5,13},{6,14},{7,15},{8,0},{9,1},... | collective-permute-start | bytes 122888 | tf_op jit(solution)/shard_map/ppermute | solution.py:92
  6.6 1.5 %collective-permute-start.3 = (bf16[288,128]{1,0:T(8,128)(2,1)}, bf16[288,128]{1,0:T(8,128)(2,1)S(1)}, u32[]{:S(2)}, u32[]{:S(2)}) collective-permute-start(bf16[288,128]{1,0:T(8,128)(2,1)} %get-tuple-element.78), channel_id=1, source_target_pairs={{0,15},{1,2},{2,1},{3,4},{4,3},{5,6},{6,5},{7,8},{8,7},{9,10},{10,... | collective-permute-start | bytes 221192 | tf_op jit(solution)/shard_map/ppermute | solution.py:97
  8.1 0.1 collective-permute-start.4
  8.2 0.0 copy-done.1
  8.2 0.0 copy-done.8
  8.2 0.0 copy-done.7
  8.2 0.0 copy-done.6
  8.3 0.0 copy-done.5
  8.3 0.0 copy-done.4
  8.3 0.0 copy-done
  8.3 0.0 copy-done.2
  8.3 0.0 copy-start.3
  8.3 0.8 %copy-done.3 = bf16[160,128]{1,0:T(8,128)(2,1)S(1)} copy-done((bf16[160,128]{1,0:T(8,128)(2,1)S(1)}, bf16[160,128]{1,0:T(8,128)(2,1)}, u32[]{:S(2)}) %copy-start.3) | copy-done | bytes 40984
  9.1 1.0 %prepare.1 = (bf16[160,128]{1,0:T(8,128)(2,1)S(1)}, f32[2,4,8,8,128]{4,3,2,1,0:T(8,128)S(1)}, f32[16,7,8,128]{3,2,1,0:T(8,128)S(1)}, f32[8,192]{1,0:T(8,128)S(1)...) custom-call(bf16[4,8,8,192]{3,2,1,0:T(8,128)(2,1)S(1)} %copy-done.1, ...), custom_call_target="tpu_custom_call" | custom-call | flops 1000000000 | tf_op jit(solution)/shard_map/prepare/pallas_call | solution.py:530
  10.1 0.0 collective-permute-done
  10.1 1.6 %collective-permute-start.2 = (bf16[2,160,128]{2,1,0:T(8,128)(2,1)S(1)}, bf16[2,160,128]{2,1,0:T(8,128)(2,1)S(1)}, u32[]{:S(2)}, u32[]{:S(2)}) collective-permute-start(bf16[2,160,128]{2,1,0:T(8,128)(2,1)S(1)} %pad_maximum_fusion), channel_id=1, source_target_pairs={{0,2},{1,3},{2,0},{3,1},{4,6},{5,7},{6,4},{7,5},{8,10},{9,11},{10,... | collective-permute-start | bytes 245768 | tf_op jit(solution)/shard_map/ppermute | solution.py:92
  11.7 0.8 %collective-permute-start.1 = (bf16[2,160,128]{2,1,0:T(8,128)(2,1)S(1)}, bf16[2,160,128]{2,1,0:T(8,128)(2,1)S(1)}, u32[]{:S(2)}, u32[]{:S(2)}) collective-permute-start(bf16[2,160,128]{2,1,0:T(8,128)(2,1)S(1)} %pad_maximum_fusion), channel_id=1, source_target_pairs={{0,4},{1,5},{2,6},{3,7},{4,0},{5,1},{6,2},{7,3},{8,12},{9,13},{10,... | collective-permute-start | bytes 245768 | tf_op jit(solution)/shard_map/ppermute | solution.py:92
  12.5 0.8 %collective-permute-done.3.q_ref = bf16[288,128]{1,0:T(8,128)(2,1)S(1)} collective-permute-done((bf16[288,128]{1,0:T(8,128)(2,1)}, bf16[288,128]{1,0:T(8,128)(2,1)S(1)}, u32[]{:S(2)}, u32[]{:S(2)}) %collective-permute-start.3) | collective-permute-done | bytes 73760 | tf_op jit(solution)/shard_map/ppermute | solution.py:97
  13.3 0.0 collective-permute-done.4.p_ref
  13.3 1.7 %collective-permute-done.2 = bf16[2,160,128]{2,1,0:T(8,128)(2,1)S(1)} collective-permute-done((bf16[2,160,128]{2,1,0:T(8,128)(2,1)S(1)}, bf16[2,160,128]{2,1,0:T(8,128)(2,1)S(1)}, u32[]{:S(2)}, u32[]{:S(2)}) %collective-permute-start.2) | collective-permute-done | bytes 81952 | tf_op jit(solution)/shard_map/ppermute | solution.py:92
  15.1 1.1 %collective-permute-done.1 = bf16[2,160,128]{2,1,0:T(8,128)(2,1)S(1)} collective-permute-done((bf16[2,160,128]{2,1,0:T(8,128)(2,1)S(1)}, bf16[2,160,128]{2,1,0:T(8,128)(2,1)S(1)}, u32[]{:S(2)}, u32[]{:S(2)}) %collective-permute-start.1) | collective-permute-done | bytes 81952 | tf_op jit(solution)/shard_map/ppermute | solution.py:92
  16.2 0.5 %collective-permute-start.5 = (bf16[2,160,128]{2,1,0:T(8,128)(2,1)S(1)}, bf16[2,160,128]{2,1,0:T(8,128)(2,1)S(1)}, u32[]{:S(2)}, u32[]{:S(2)}) collective-permute-start(bf16[2,160,128]{2,1,0:T(8,128)(2,1)S(1)} %collective-permute-done.1), channel_id=1, source_target_pairs={{0,2},{1,3},{2,0},{3,1},{4,6},{5,7},{6,4},{7,5},{8,10},{9,11},{10,... | collective-permute-start | bytes 245768 | tf_op jit(solution)/shard_map/ppermute | solution.py:92
  16.7 2.0 %forward_stencil.1 = (bf16[256,256]{1,0:T(8,128)(2,1)S(1)}, f32[256,256]{1,0:T(8,128)S(1)}, f32[7,15,8,8,128]{4,3,2,1,0:T(8,128)S(1)}) custom-call(s32[1]{0:T(128)} %bitcast.me_ref, f32[2,4,8,8,128]{4,3,2,1,0:T(8,128)S(1)} %get-tuple-element.82.own_ref, bf16[288,128]{1,0:T(8,128)(2,1)S(1)} %collective-permute-done.4.p_ref, ...), custom_call_target="tpu_custom_call" | custom-call | flops 2500000000 | tf_op jit(solution)/shard_map/forward_stencil/pallas_call | solution.py:530
  18.7 1.9 %collective-permute-done.5 = bf16[2,160,128]{2,1,0:T(8,128)(2,1)S(1)} collective-permute-done((bf16[2,160,128]{2,1,0:T(8,128)(2,1)S(1)}, bf16[2,160,128]{2,1,0:T(8,128)(2,1)S(1)}, u32[]{:S(2)}, u32[]{:S(2)}) %collective-permute-start.5) | collective-permute-done | bytes 81952 | tf_op jit(solution)/shard_map/ppermute | solution.py:92
  20.6 0.1 collective-permute-start.6
  20.7 1.6 %collective-permute-done.6.g1_ref = bf16[8,160,128]{2,1,0:T(8,128)(2,1)S(1)} collective-permute-done((bf16[8,160,128]{2,1,0:T(8,128)(2,1)S(1)}, bf16[8,160,128]{2,1,0:T(8,128)(2,1)S(1)}, u32[]{:S(2)}, u32[]{:S(2)}) %collective-permute-start.6) | collective-permute-done | bytes 327712 | tf_op jit(solution)/shard_map/ppermute | solution.py:92
  22.3 1.2 %pointwise.1 = (f32[256,192]{1,0:T(8,128)S(1)}, bf16[4,8,8,192]{3,2,1,0:T(8,128)(2,1)S(1)}, bf16[288,128]{1,0:T(8,128)(2,1)S(1)}, f32[1280,128]{1,0:T(8,128)S(1)...) custom-call(s32[1]{0:T(128)} %bitcast.me_ref, bf16[8,160,128]{2,1,0:T(8,128)(2,1)S(1)} %constant_dynamic-update-slice_fusion.g0_ref, ...), custom_call_target="tpu_custom_call" | custom-call | flops 2500000000 | tf_op jit(solution)/shard_map/pointwise/pallas_call | solution.py:530
  23.5 0.2 collective-permute-start.9
  23.7 2.0 %kernel_gradient.1 = (f32[272,128]{1,0:T(8,128)S(1)}, bf16[272,128]{1,0:T(8,128)(2,1)S(1)}) custom-call(s32[1]{0:T(128)} %bitcast.me_ref, f32[7,15,8,8,128]{4,3,2,1,0:T(8,128)S(1)} %get-tuple-element.90.s_ref, bf16[4,8,8,192]{3,2,1,0:T(8,128)(2,1)S(1)} %get-tuple-element.97.g_ref, f32[8,256]{1,0:T(8,128)S(1)} %get-tuple-element.98.small_ref), custom_call_target="tpu_custom_call" | custom-call | flops 2000000000 | tf_op jit(solution)/shard_map/kernel_gradient/pallas_call | solution.py:530
  25.8 0.4 collective-permute-start.7
  26.2 0.0 collective-permute-done.9
  26.2 0.1 convert_add_fusion
  26.3 0.6 %collective-permute-start.10 = (bf16[640,128]{1,0:T(8,128)(2,1)S(1)}, bf16[640,128]{1,0:T(8,128)(2,1)S(1)}, u32[]{:S(2)}, u32[]{:S(2)}) collective-permute-start(bf16[640,128]{1,0:T(8,128)(2,1)S(1)} %slice.50), channel_id=1, source_target_pairs={{0,2},{1,3},{2,0},{3,1},{4,6},{5,7},{6,4},{7,5},{8,10},{9,11},{10,... | collective-permute-start | bytes 491528 | tf_op jit(solution)/shard_map/ppermute | solution.py:92
  26.9 0.3 collective-permute-done.7
  27.2 2.1 %collective-permute-start.8 = (bf16[272,128]{1,0:T(8,128)(2,1)S(1)}, bf16[272,128]{1,0:T(8,128)(2,1)S(1)}, u32[]{:S(2)}, u32[]{:S(2)}) collective-permute-start(bf16[272,128]{1,0:T(8,128)(2,1)S(1)} %convert_add_fusion.1), channel_id=1, source_target_pairs={{0,8},{1,9},{2,10},{3,11},{4,12},{5,13},{6,14},{7,15},{8,0},{9,1},... | collective-permute-start | bytes 208904 | tf_op jit(solution)/shard_map/ppermute | solution.py:92
  29.2 1.7 %collective-permute-start.14 = (bf16[288,128]{1,0:T(8,128)(2,1)S(1)}, bf16[288,128]{1,0:T(8,128)(2,1)S(1)}, u32[]{:S(2)}, u32[]{:S(2)}) collective-permute-start(bf16[288,128]{1,0:T(8,128)(2,1)S(1)} %get-tuple-element.108), channel_id=1, source_target_pairs={{0,15},{1,2},{2,1},{3,4},{4,3},{5,6},{6,5},{7,8},{8,7},{9,10},{10,... | collective-permute-start | bytes 221192 | tf_op jit(solution)/shard_map/ppermute | solution.py:97
  31.0 3.2 %collective-permute-done.8 = bf16[272,128]{1,0:T(8,128)(2,1)S(1)} collective-permute-done((bf16[272,128]{1,0:T(8,128)(2,1)S(1)}, bf16[272,128]{1,0:T(8,128)(2,1)S(1)}, u32[]{:S(2)}, u32[]{:S(2)}) %collective-permute-start.8) | collective-permute-done | bytes 69664 | tf_op jit(solution)/shard_map/ppermute | solution.py:92
  34.2 0.0 collective-permute-done.10
  34.2 0.8 %collective-permute-start.11 = (bf16[272,128]{1,0:T(8,128)(2,1)S(1)}, bf16[272,128]{1,0:T(8,128)(2,1)S(1)}, u32[]{:S(2)}, u32[]{:S(2)}) collective-permute-start(bf16[272,128]{1,0:T(8,128)(2,1)S(1)} %add_convert_fusion.2), channel_id=1, source_target_pairs={{0,2},{1,3},{2,0},{3,1},{4,6},{5,7},{6,4},{7,5},{8,10},{9,11},{10,... | collective-permute-start | bytes 208904 | tf_op jit(solution)/shard_map/ppermute | solution.py:92
  35.1 0.4 collective-permute-start.12
  35.5 0.2 collective-permute-done.14.q_ref
  35.7 2.6 %backward_stencil.1 = (bf16[4,8,8,192]{3,2,1,0:T(8,128)(2,1)}, bf16[4,8,8,192]{3,2,1,0:T(8,128)(2,1)}) custom-call(s32[1]{0:T(128)} %bitcast.me_ref, bf16[4,8,8,192]{3,2,1,0:T(8,128)(2,1)S(1)} %get-tuple-element.97.g_ref, bf16[288,128]{1,0:T(8,128)(2,1)S(1)} %slice.39.p_ref, bf16[288,128]{1,0:T(8,128)(2,1)S(1)} %collective-permute-done.14.q_ref, ...), custom_call_target="tpu_custom_call" | custom-call | flops 2500000000 | tf_op jit(solution)/shard_map/backward_stencil/pallas_call | solution.py:530
  38.3 0.3 collective-permute-done.11
  38.6 1.0 %collective-permute-done.12 = bf16[320,128]{1,0:T(8,128)(2,1)S(1)} collective-permute-done((bf16[320,128]{1,0:T(8,128)(2,1)S(1)}, bf16[320,128]{1,0:T(8,128)(2,1)S(1)}, u32[]{:S(2)}, u32[]{:S(2)}) %collective-permute-start.12) | collective-permute-done | bytes 81952 | tf_op jit(solution)/shard_map/ppermute | solution.py:92
  39.6 0.4 collective-permute-start.13
  40.1 3.4 %collective-permute-start.16 = (bf16[160,128]{1,0:T(8,128)(2,1)S(1)}, bf16[160,128]{1,0:T(8,128)(2,1)S(1)}, u32[]{:S(2)}, u32[]{:S(2)}) collective-permute-start(bf16[160,128]{1,0:T(8,128)(2,1)S(1)} %slice.52), channel_id=1, source_target_pairs={{0,8},{1,9},{2,10},{3,11},{4,12},{5,13},{6,14},{7,15},{8,0},{9,1},... | collective-permute-start | bytes 122888 | tf_op jit(solution)/shard_map/ppermute | solution.py:92
  43.6 0.6 %collective-permute-done.13 = bf16[272,128]{1,0:T(8,128)(2,1)S(1)} collective-permute-done((bf16[272,128]{1,0:T(8,128)(2,1)S(1)}, bf16[272,128]{1,0:T(8,128)(2,1)S(1)}, u32[]{:S(2)}, u32[]{:S(2)}) %collective-permute-start.13) | collective-permute-done | bytes 69664 | tf_op jit(solution)/shard_map/ppermute | solution.py:92
  44.2 0.1 collective-permute-start.15
  44.3 1.3 %collective-permute-done.16 = bf16[160,128]{1,0:T(8,128)(2,1)S(1)} collective-permute-done((bf16[160,128]{1,0:T(8,128)(2,1)S(1)}, bf16[160,128]{1,0:T(8,128)(2,1)S(1)}, u32[]{:S(2)}, u32[]{:S(2)}) %collective-permute-start.16) | collective-permute-done | bytes 40992 | tf_op jit(solution)/shard_map/ppermute | solution.py:92
  45.5 0.0 collective-permute-done.15.other_ref
  45.6 0.9 %final.1 = (f32[7,7,7,192]{3,2,1,0:T(8,128)}, f32[1,192]{1,0:T(1,128)}, f32[1,192]{1,0:T(1,128)}, f32[1,192]{1,0:T(1,128)}, f32[1,192]{1,0:T(1,128)}, /*index=5*...) custom-call(s32[1]{0:T(128)} %bitcast.me_ref, ...), custom_call_target="tpu_custom_call" | custom-call | flops 1000000000 | tf_op jit(solution)/shard_map/final/pallas_call | solution.py:530
  (17 shorter events, 0.3 us)
Async XLA Ops:
  0.6 7.6 %copy-start.1 = (bf16[4,8,8,192]{3,2,1,0:T(8,128)(2,1)S(1)}, bf16[4,8,8,192]{3,2,1,0:T(8,128)(2,1)}, u32[]{:S(2)}) copy-start(bf16[4,8,8,192]{3,2,1,0:T(8,128)(2,1)} %refs_0_.1) | copy-start | bytes 294916
  0.7 7.6 %copy-start.8 = (f32[192]{0:T(256)S(1)}, f32[192]{0:T(256)}, u32[]{:S(2)}) copy-start(f32[192]{0:T(256)} %refs_7_.1) | copy-start | bytes 2308
  0.7 7.6 %copy-start.7 = (f32[192]{0:T(256)S(1)}, f32[192]{0:T(256)}, u32[]{:S(2)}) copy-start(f32[192]{0:T(256)} %refs_6_.1) | copy-start | bytes 2308
  0.7 7.6 %copy-start.6 = (f32[192]{0:T(256)S(1)}, f32[192]{0:T(256)}, u32[]{:S(2)}) copy-start(f32[192]{0:T(256)} %refs_5_.1) | copy-start | bytes 2308
  0.7 7.6 %copy-start.5 = (f32[192]{0:T(256)S(1)}, f32[192]{0:T(256)}, u32[]{:S(2)}) copy-start(f32[192]{0:T(256)} %refs_4_.1) | copy-start | bytes 2308
  0.7 7.6 %copy-start.4 = (f32[192]{0:T(256)S(1)}, f32[192]{0:T(256)}, u32[]{:S(2)}) copy-start(f32[192]{0:T(256)} %refs_3_.1) | copy-start | bytes 2308
  0.7 7.6 %copy-start = (f32[7,7,7,192]{3,2,1,0:T(8,128)S(1)}, f32[7,7,7,192]{3,2,1,0:T(8,128)}, u32[]{:S(2)}) copy-start(f32[7,7,7,192]{3,2,1,0:T(8,128)} %refs_2_.1) | copy-start | bytes 790276
  0.7 7.6 %copy-start.2 = (bf16[4,8,8,192]{3,2,1,0:T(8,128)(2,1)S(1)}, bf16[4,8,8,192]{3,2,1,0:T(8,128)(2,1)}, u32[]{:S(2)}) copy-start(bf16[4,8,8,192]{3,2,1,0:T(8,128)(2,1)} %refs_1_.1) | copy-start | bytes 294916
  2.5 7.5 %collective-permute-start = (bf16[160,128]{1,0:T(8,128)(2,1)}, bf16[160,128]{1,0:T(8,128)(2,1)S(1)}, u32[]{:S(2)}, u32[]{:S(2)}) collective-permute-start(bf16[160,128]{1,0:T(8,128)(2,1)} %get-tuple-element.68.refs_8_), channel_id=1, source_target_pairs={{0,8},{1,9},{2,10},{3,11},{4,12},{5,13},{6,14},{7,15},{8,0},{9,1},... | collective-permute-start | bytes 122888 | tf_op jit(solution)/shard_map/ppermute | solution.py:92
  6.6 6.7 %collective-permute-start.3 = (bf16[288,128]{1,0:T(8,128)(2,1)}, bf16[288,128]{1,0:T(8,128)(2,1)S(1)}, u32[]{:S(2)}, u32[]{:S(2)}) collective-permute-start(bf16[288,128]{1,0:T(8,128)(2,1)} %get-tuple-element.78), channel_id=1, source_target_pairs={{0,15},{1,2},{2,1},{3,4},{4,3},{5,6},{6,5},{7,8},{8,7},{9,10},{10,... | collective-permute-start | bytes 221192 | tf_op jit(solution)/shard_map/ppermute | solution.py:97
  8.1 5.2 %collective-permute-start.4 = (bf16[288,128]{1,0:T(8,128)(2,1)}, bf16[288,128]{1,0:T(8,128)(2,1)S(1)}, u32[]{:S(2)}, u32[]{:S(2)}) collective-permute-start(bf16[288,128]{1,0:T(8,128)(2,1)} %get-tuple-element.79), channel_id=1, source_target_pairs={{0,1},{1,0},{2,3},{3,2},{4,5},{5,4},{6,7},{7,6},{8,9},{9,8},{10,11... | collective-permute-start | bytes 221192 | tf_op jit(solution)/shard_map/ppermute | solution.py:92
  8.3 0.8 %copy-start.3 = (bf16[160,128]{1,0:T(8,128)(2,1)S(1)}, bf16[160,128]{1,0:T(8,128)(2,1)}, u32[]{:S(2)}) copy-start(bf16[160,128]{1,0:T(8,128)(2,1)} %get-tuple-element.68.refs_8_) | copy-start | bytes 122884
  10.1 5.0 %collective-permute-start.2 = (bf16[2,160,128]{2,1,0:T(8,128)(2,1)S(1)}, bf16[2,160,128]{2,1,0:T(8,128)(2,1)S(1)}, u32[]{:S(2)}, u32[]{:S(2)}) collective-permute-start(bf16[2,160,128]{2,1,0:T(8,128)(2,1)S(1)} %pad_maximum_fusion), channel_id=1, source_target_pairs={{0,2},{1,3},{2,0},{3,1},{4,6},{5,7},{6,4},{7,5},{8,10},{9,11},{10,... | collective-permute-start | bytes 245768 | tf_op jit(solution)/shard_map/ppermute | solution.py:92
  11.7 4.4 %collective-permute-start.1 = (bf16[2,160,128]{2,1,0:T(8,128)(2,1)S(1)}, bf16[2,160,128]{2,1,0:T(8,128)(2,1)S(1)}, u32[]{:S(2)}, u32[]{:S(2)}) collective-permute-start(bf16[2,160,128]{2,1,0:T(8,128)(2,1)S(1)} %pad_maximum_fusion), channel_id=1, source_target_pairs={{0,4},{1,5},{2,6},{3,7},{4,0},{5,1},{6,2},{7,3},{8,12},{9,13},{10,... | collective-permute-start | bytes 245768 | tf_op jit(solution)/shard_map/ppermute | solution.py:92
  16.2 4.4 %collective-permute-start.5 = (bf16[2,160,128]{2,1,0:T(8,128)(2,1)S(1)}, bf16[2,160,128]{2,1,0:T(8,128)(2,1)S(1)}, u32[]{:S(2)}, u32[]{:S(2)}) collective-permute-start(bf16[2,160,128]{2,1,0:T(8,128)(2,1)S(1)} %collective-permute-done.1), channel_id=1, source_target_pairs={{0,2},{1,3},{2,0},{3,1},{4,6},{5,7},{6,4},{7,5},{8,10},{9,11},{10,... | collective-permute-start | bytes 245768 | tf_op jit(solution)/shard_map/ppermute | solution.py:92
  20.6 1.7 %collective-permute-start.6 = (bf16[8,160,128]{2,1,0:T(8,128)(2,1)S(1)}, bf16[8,160,128]{2,1,0:T(8,128)(2,1)S(1)}, u32[]{:S(2)}, u32[]{:S(2)}) collective-permute-start(bf16[8,160,128]{2,1,0:T(8,128)(2,1)S(1)} %constant_dynamic-update-slice_fusion.g0_ref), channel_id=1, source_target_pairs={{0,1},{1,0},{2,3},{3,2},{4,5},{5,4},{6,7},{7,6},{8,9},{9,8},{10,11... | collective-permute-start | bytes 983048 | tf_op jit(solution)/shard_map/ppermute | solution.py:92
  23.5 2.7 %collective-permute-start.9 = (bf16[1568,128]{1,0:T(8,128)(2,1)S(1)}, bf16[1568,128]{1,0:T(8,128)(2,1)S(1)}, u32[]{:S(2)}, u32[]{:S(2)}) collective-permute-start(bf16[1568,128]{1,0:T(8,128)(2,1)S(1)} %get-tuple-element.104), channel_id=1, source_target_pairs={{0,1},{1,0},{2,3},{3,2},{4,5},{5,4},{6,7},{7,6},{8,9},{9,8},{10,11... | collective-permute-start | bytes 1204232 | tf_op jit(solution)/shard_map/ppermute | solution.py:92
  25.8 1.3 %collective-permute-start.7 = (bf16[272,128]{1,0:T(8,128)(2,1)S(1)}, bf16[272,128]{1,0:T(8,128)(2,1)S(1)}, u32[]{:S(2)}, u32[]{:S(2)}) collective-permute-start(bf16[272,128]{1,0:T(8,128)(2,1)S(1)} %get-tuple-element.100), channel_id=1, source_target_pairs={{0,1},{1,0},{2,3},{3,2},{4,5},{5,4},{6,7},{7,6},{8,9},{9,8},{10,11... | collective-permute-start | bytes 208904 | tf_op jit(solution)/shard_map/ppermute | solution.py:92
  26.3 7.8 %collective-permute-start.10 = (bf16[640,128]{1,0:T(8,128)(2,1)S(1)}, bf16[640,128]{1,0:T(8,128)(2,1)S(1)}, u32[]{:S(2)}, u32[]{:S(2)}) collective-permute-start(bf16[640,128]{1,0:T(8,128)(2,1)S(1)} %slice.50), channel_id=1, source_target_pairs={{0,2},{1,3},{2,0},{3,1},{4,6},{5,7},{6,4},{7,5},{8,10},{9,11},{10,... | collective-permute-start | bytes 491528 | tf_op jit(solution)/shard_map/ppermute | solution.py:92
  27.2 7.0 %collective-permute-start.8 = (bf16[272,128]{1,0:T(8,128)(2,1)S(1)}, bf16[272,128]{1,0:T(8,128)(2,1)S(1)}, u32[]{:S(2)}, u32[]{:S(2)}) collective-permute-start(bf16[272,128]{1,0:T(8,128)(2,1)S(1)} %convert_add_fusion.1), channel_id=1, source_target_pairs={{0,8},{1,9},{2,10},{3,11},{4,12},{5,13},{6,14},{7,15},{8,0},{9,1},... | collective-permute-start | bytes 208904 | tf_op jit(solution)/shard_map/ppermute | solution.py:92
  29.2 6.5 %collective-permute-start.14 = (bf16[288,128]{1,0:T(8,128)(2,1)S(1)}, bf16[288,128]{1,0:T(8,128)(2,1)S(1)}, u32[]{:S(2)}, u32[]{:S(2)}) collective-permute-start(bf16[288,128]{1,0:T(8,128)(2,1)S(1)} %get-tuple-element.108), channel_id=1, source_target_pairs={{0,15},{1,2},{2,1},{3,4},{4,3},{5,6},{6,5},{7,8},{8,7},{9,10},{10,... | collective-permute-start | bytes 221192 | tf_op jit(solution)/shard_map/ppermute | solution.py:97
  34.2 4.4 %collective-permute-start.11 = (bf16[272,128]{1,0:T(8,128)(2,1)S(1)}, bf16[272,128]{1,0:T(8,128)(2,1)S(1)}, u32[]{:S(2)}, u32[]{:S(2)}) collective-permute-start(bf16[272,128]{1,0:T(8,128)(2,1)S(1)} %add_convert_fusion.2), channel_id=1, source_target_pairs={{0,2},{1,3},{2,0},{3,1},{4,6},{5,7},{6,4},{7,5},{8,10},{9,11},{10,... | collective-permute-start | bytes 208904 | tf_op jit(solution)/shard_map/ppermute | solution.py:92
  35.1 4.5 %collective-permute-start.12 = (bf16[320,128]{1,0:T(8,128)(2,1)S(1)}, bf16[320,128]{1,0:T(8,128)(2,1)S(1)}, u32[]{:S(2)}, u32[]{:S(2)}) collective-permute-start(bf16[320,128]{1,0:T(8,128)(2,1)S(1)} %slice.51), channel_id=1, source_target_pairs={{0,4},{1,5},{2,6},{3,7},{4,0},{5,1},{6,2},{7,3},{8,12},{9,13},{10,... | collective-permute-start | bytes 245768 | tf_op jit(solution)/shard_map/ppermute | solution.py:92
  39.6 4.5 %collective-permute-start.13 = (bf16[272,128]{1,0:T(8,128)(2,1)S(1)}, bf16[272,128]{1,0:T(8,128)(2,1)S(1)}, u32[]{:S(2)}, u32[]{:S(2)}) collective-permute-start(bf16[272,128]{1,0:T(8,128)(2,1)S(1)} %add_convert_fusion.1), channel_id=1, source_target_pairs={{0,4},{1,5},{2,6},{3,7},{4,0},{5,1},{6,2},{7,3},{8,12},{9,13},{10,... | collective-permute-start | bytes 208904 | tf_op jit(solution)/shard_map/ppermute | solution.py:92
  40.1 5.4 %collective-permute-start.16 = (bf16[160,128]{1,0:T(8,128)(2,1)S(1)}, bf16[160,128]{1,0:T(8,128)(2,1)S(1)}, u32[]{:S(2)}, u32[]{:S(2)}) collective-permute-start(bf16[160,128]{1,0:T(8,128)(2,1)S(1)} %slice.52), channel_id=1, source_target_pairs={{0,8},{1,9},{2,10},{3,11},{4,12},{5,13},{6,14},{7,15},{8,0},{9,1},... | collective-permute-start | bytes 122888 | tf_op jit(solution)/shard_map/ppermute | solution.py:92
  44.2 1.4 %collective-permute-start.15 = (bf16[272,128]{1,0:T(8,128)(2,1)S(1)}, bf16[272,128]{1,0:T(8,128)(2,1)S(1)}, u32[]{:S(2)}, u32[]{:S(2)}) collective-permute-start(bf16[272,128]{1,0:T(8,128)(2,1)S(1)} %add_convert_fusion.mine_ref), channel_id=1, source_target_pairs={{0,1},{1,0},{2,3},{3,2},{4,5},{5,4},{6,7},{7,6},{8,9},{9,8},{10,11... | collective-permute-start | bytes 208904 | tf_op jit(solution)/shard_map/ppermute | solution.py:92
